TPU v7x, 32 devices: a whole 2x2x4 slice. The times are simulated.
32 devices in a mesh: expert: 16 (over z, y, core), tensor: 2 (over x).
Axes of the slice: x: 2, y: 2, z: 4, core: 2. Of those that a mesh axis runs over, the one named last changes fastest.
Arguments:
- tokens: bfloat16 [512, 7168], P(('expert', 'tensor')), may hold values from -6 to 6
- expert_ids: int32 [512, 8], P(('expert', 'tensor')), may hold values from 0 to 15, all different within a row; in each aligned block of 16 rows (0 to 15, 16 to 31, ...) at most 16 rows name the same one
- gate_values: float32 [512, 8], P(('expert', 'tensor')), may hold values from 0.05 to 0.6
- w_gate: bfloat16 [16, 7168, 1024], P('expert', None, 'tensor'), may hold values from -0.0625 to 0.0625
- w_up: bfloat16 [16, 7168, 1024], P('expert', None, 'tensor'), may hold values from -0.0625 to 0.0625
- w_down: bfloat16 [16, 1024, 7168], P('expert', 'tensor'), may hold values from -0.1875 to 0.1875
Outputs:
- mixed: bfloat16 [512, 7168], P(('expert', 'tensor'))
Inputs may be any that keep to these rules, and one draw needn't show every extreme that they name: `expert_ids`: each row names 8 different experts; within each aligned block of 16 rows (the rows of one device) no expert is named by more than 16 rows.
All inputs are finite; a program needn't handle non-finite values.
Results may differ from a plain program's by a relative error of at most 0.012.
Values may be sent and summed in bfloat16 or wider, within the bound.
No kernel may reach another device: no remote copies, remote signals or barrier semaphores. Data moves between devices by JAX's collectives and lax.ppermute only.
A program may use at most 128 MiB of HBM per device.

v0:
```python
import jax
import jax.numpy as jnp
from jax import lax
from jax.sharding import PartitionSpec as P

AXES = ("expert", "tensor")


def slot_places(expert_ids, experts, capacity):
    count = expert_ids.shape[0] * expert_ids.shape[1]
    flat = expert_ids.reshape(count)
    onehot = (flat[:, None] == jnp.arange(experts, dtype=jnp.int32)[None, :]).astype(jnp.int32)
    ranks = jnp.sum(jnp.cumsum(onehot, axis=0) * onehot, axis=1) - 1
    return flat * capacity + ranks


def dispatch_rows(tokens, places, experts, capacity, top):
    count = tokens.shape[0]
    table = (places[:, None] == jnp.arange(experts * capacity, dtype=jnp.int32)[None, :]).astype(
        jnp.bfloat16
    )
    table = jnp.sum(table.reshape(count, top, experts * capacity), axis=1)
    rows = jnp.einsum("ns,nd->sd", table, tokens, preferred_element_type=jnp.float32)
    return rows.astype(jnp.bfloat16).reshape(experts, capacity, tokens.shape[1])


def swiglu(rows, wg, wu):
    gate = jnp.dot(rows, wg, preferred_element_type=jnp.float32)
    up = jnp.dot(rows, wu, preferred_element_type=jnp.float32)
    return (jax.nn.silu(gate) * up).astype(jnp.bfloat16)


def slotted(tokens, expert_ids, gate_values, w_gate, w_up, w_down, capacity):
    experts = lax.axis_size("expert")
    count, top = expert_ids.shape
    width = tokens.shape[1]
    places = slot_places(expert_ids, experts, capacity)
    sending = dispatch_rows(tokens, places, experts, capacity, top)
    arrived = lax.all_to_all(sending, "expert", split_axis=0, concat_axis=0, tiled=True)
    rows = arrived.reshape(experts * capacity, width)
    hidden = swiglu(lax.all_gather(rows, "tensor", axis=0, tiled=True), w_gate[0], w_up[0])
    summed = lax.psum_scatter(
        jnp.dot(hidden, w_down[0], preferred_element_type=jnp.float32).astype(jnp.bfloat16),
        "tensor",
        scatter_dimension=0,
        tiled=True,
    )
    out_rows = summed.reshape(experts, capacity, width)
    returned = lax.all_to_all(out_rows, "expert", split_axis=0, concat_axis=0, tiled=True)
    picked = returned.reshape(experts * capacity, width)[places].reshape(count, top, width)
    mixed = jnp.sum(gate_values[:, :, None] * picked.astype(jnp.float32), axis=1)
    return mixed.astype(jnp.bfloat16)


def expert_weights(expert_ids, gate_values, experts):
    named = expert_ids[:, :, None] == jnp.arange(experts, dtype=jnp.int32)[None, None, :]
    return jnp.sum(jnp.where(named, gate_values[:, :, None], 0.0), axis=1)


def partner(step, e, t):
    if step == "core":
        return e ^ 1, t
    if step == "far":
        return e ^ 8, t
    if step == "near":
        return e ^ 4, t
    return (e, t ^ 1) if (e & 1) == (step == "late") else (e ^ 2, t)


def exchange(block, step):
    parts = lax.axis_size("tensor")
    perm = []
    for e in range(lax.axis_size("expert")):
        for t in range(parts):
            other = partner(step, e, t)
            perm.append((e * parts + t, other[0] * parts + other[1]))
    return lax.ppermute(block, AXES, perm)


STEPS = ("far", "near", "late", "early")
GATHER = (
    (20, ("near", "far", "early", "late")),
    (20, ("far", "early", "late", "near")),
    (16, ("far", "early", "near", "late")),
)
SCATTER = (
    (16, ("late", "far", "early", "near")),
    (20, ("near", "late", "early", "far")),
    (20, ("late", "early", "far", "near")),
)
TURNS = (0, 1, 2, 0, 2, 1, 2, 0, 1, 0, 1, 2, 0, 1, 2)


def chunks_of(width, plan):
    tiles, total = width // 128, sum(share for share, _ in plan)
    edges, at = [0], 0
    for share, _ in plan:
        at += share
        edges.append(128 * (tiles * at // total))
    return [(lo, hi, order) for lo, hi, (_, order) in zip(edges[:-1], edges[1:], plan)]


def gather_rows(block, order):
    count, width = block.shape
    rows = block.reshape(1, 1, 1, 1, count, width)
    for step in order:
        rows = jnp.concatenate([rows, exchange(rows, step)], axis=STEPS.index(step))
    rows = rows.reshape(-1, width)
    return rows, exchange(rows, "core")


def scatter_rows(hidden, scale, w_down, chunks):
    def product(j, chunk):
        lo, hi, _ = chunk
        return scale[j] * jnp.dot(hidden[j], w_down[:, lo:hi], preferred_element_type=jnp.float32)

    state = [[exchange(product(1, chunk).astype(jnp.bfloat16), "core"), None, 0] for chunk in chunks]
    before = hidden[0]
    count = hidden[0].shape[0] // 16
    outs = [None] * len(chunks)
    for k in TURNS:
        arrived, mine, done = state[k]
        lo, hi, order = chunks[k]
        arrived, before = lax.optimization_barrier((arrived, before))
        if done == 0:
            total = product(0, chunks[k]) + arrived.astype(jnp.float32)
            total = total.reshape(2, 2, 2, 2, count, hi - lo).astype(jnp.bfloat16)
        else:
            total = (mine.astype(jnp.float32) + arrived.astype(jnp.float32)).astype(jnp.bfloat16)
        before = total
        if done == len(order):
            outs[k] = total.reshape(count, hi - lo)
            continue
        axis = STEPS.index(order[done])
        mine, other = lax.slice_in_dim(total, 0, 1, axis=axis), lax.slice_in_dim(total, 1, 2, axis=axis)
        state[k] = [exchange(other, order[done]), mine, done + 1]
    return jnp.concatenate(outs, axis=1)


def dense(tokens, expert_ids, gate_values, w_gate, w_up, w_down):
    experts = lax.axis_size("expert")
    count, width = tokens.shape
    weights = expert_weights(expert_ids, gate_values, experts)
    high = lax.reduce_precision(weights, 8, 7)
    packed = jnp.concatenate([high, weights - high], axis=1).astype(jnp.bfloat16)
    packed = jnp.pad(packed, ((0, 0), (0, -2 * experts % 128)))
    chunks = chunks_of(width, GATHER)
    gates, ups = [0.0, 0.0], [0.0, 0.0]
    for i, (lo, hi, order) in enumerate(chunks):
        block = tokens[:, lo:hi]
        last = i == len(chunks) - 1
        if last:
            block = jnp.concatenate([block, packed], axis=1)
        halves = gather_rows(block, order)
        if last:
            spread = [rows[:, hi - lo :] for rows in halves]
            halves = [rows[:, : hi - lo] for rows in halves]
        for j, rows in enumerate(halves):
            gates[j] = gates[j] + jnp.dot(rows, w_gate[0, lo:hi], preferred_element_type=jnp.float32)
            ups[j] = ups[j] + jnp.dot(rows, w_up[0, lo:hi], preferred_element_type=jnp.float32)
    hidden = [(jax.nn.silu(gate) * up).astype(jnp.bfloat16) for gate, up in zip(gates, ups)]
    me = lax.axis_index("expert")
    column = jnp.arange(spread[0].shape[1], dtype=jnp.int32)
    named = (column == me) | (column == me + experts)
    scale = [
        jnp.sum(jnp.where(named[None, :], rows.astype(jnp.float32), 0.0), axis=1, keepdims=True)
        for rows in spread
    ]
    return scatter_rows(hidden, scale, w_down[0], chunks_of(width, SCATTER))


def local(tokens, expert_ids, gate_values, w_gate, w_up, w_down):
    experts = lax.axis_size("expert")
    count, top = expert_ids.shape
    capacity = min(count, max(2, 2 * count * top // experts))
    if capacity < count or experts != 16 or lax.axis_size("tensor") != 2:
        return slotted(tokens, expert_ids, gate_values, w_gate, w_up, w_down, capacity)
    return dense(tokens, expert_ids, gate_values, w_gate, w_up, w_down)


def solution(mesh):
    return jax.shard_map(
        local,
        mesh=mesh,
        in_specs=(
            P(("expert", "tensor"), None),
            P(("expert", "tensor"), None),
            P(("expert", "tensor"), None),
            P("expert", None, "tensor"),
            P("expert", None, "tensor"),
            P("expert", "tensor", None),
        ),
        out_specs=P(("expert", "tensor"), None),
        check_vma=False,
    )
```

profile of v0, /device:TPU:0, one launch (start us, length us, event | category | flops | bytes accessed | tf_op | source)
XLA Modules:
  0.0 119.2 jit_solution(1134962121612618158)
XLA Ops:
  2.6 4.1 %collective-permute-start = (bf16[1,1,1,1,16,2176]{5,4,3,2,1,0:T(8,128)(2,1)S(1)}, bf16[1,1,1,1,16,2176]{5,4,3,2,1,0:T(8,128)(2,1)S(1)}, u32[]{:S(2)}, u32[]{:S(2)}) collective-permute-start(bf16[1,1,1,1,16,2176]{5,4,3,2,1,0:T(8,128)(2,1)S(1)} %maximum_bitcast_fusion), channel_id=1, source_target_pairs={{0,16},{1,17},{2,18},{3,19},{4,20},{5,21},{6,22},{7,23},{8,24},{9,... | collective-permute-start | bytes 208904 | tf_op jit(solution)/shard_map/ppermute | solution.py:77
  6.7 0.9 slice_bitcast_fusion.1
  7.6 1.6 %collective-permute-start.4 = (bf16[1,1,1,1,16,2560]{5,4,3,2,1,0:T(8,128)(2,1)S(1)}, bf16[1,1,1,1,16,2560]{5,4,3,2,1,0:T(8,128)(2,1)S(1)}, u32[]{:S(2)}, u32[]{:S(2)}) collective-permute-start(bf16[1,1,1,1,16,2560]{5,4,3,2,1,0:T(8,128)(2,1)S(1)} %get-tuple-element.37), channel_id=1, source_target_pairs={{0,8},{1,9},{2,10},{3,11},{4,12},{5,13},{6,14},{7,15},{8,0},{9,1},... | collective-permute-start | bytes 245768 | tf_op jit(solution)/shard_map/ppermute | solution.py:77
  9.9 2.0 %collective-permute-start.1 = (bf16[2,1,1,1,16,2176]{5,4,3,2,1,0:T(8,128)(2,1)S(1)}, bf16[2,1,1,1,16,2176]{5,4,3,2,1,0:T(8,128)(2,1)S(1)}, u32[]{:S(2)}, u32[]{:S(2)}) collective-permute-start(bf16[2,1,1,1,16,2176]{5,4,3,2,1,0:T(8,128)(2,1)S(1)} %pad_maximum_fusion.12), channel_id=1, source_target_pairs={{0,1},{1,0},{2,6},{3,7},{4,5},{5,4},{6,2},{7,3},{8,9},{9,8},{10,14... | collective-permute-start | bytes 417800 | tf_op jit(solution)/shard_map/ppermute | solution.py:77
  12.2 1.7 %collective-permute-start.5 = (bf16[1,2,1,1,16,2560]{5,4,3,2,1,0:T(8,128)(2,1)S(1)}, bf16[1,2,1,1,16,2560]{5,4,3,2,1,0:T(8,128)(2,1)S(1)}, u32[]{:S(2)}, u32[]{:S(2)}) collective-permute-start(bf16[1,2,1,1,16,2560]{5,4,3,2,1,0:T(8,128)(2,1)S(1)} %pad_maximum_fusion.10), channel_id=1, source_target_pairs={{0,16},{1,17},{2,18},{3,19},{4,20},{5,21},{6,22},{7,23},{8,24},{9,... | collective-permute-start | bytes 491528 | tf_op jit(solution)/shard_map/ppermute | solution.py:77
  13.9 4.3 %collective-permute-done.8 = bf16[1,1,1,1,16,2560]{5,4,3,2,1,0:T(8,128)(2,1)S(1)} collective-permute-done((bf16[1,1,1,1,16,2560]{5,4,3,2,1,0:T(8,128)(2,1)S(1)}, bf16[1,1,1,1,16,2560]{5,4,3,2,1,0:T(8,128)(2,1)S(1)}, u32[]{:S(2)}, u32[]{:S(2)}) %collective-permute-start.8) | collective-permute-done | bytes 81952 | tf_op jit(solution)/shard_map/ppermute | solution.py:77
  18.2 3.4 %collective-permute-start.9 = (bf16[2,1,1,1,16,2560]{5,4,3,2,1,0:T(8,128)(2,1)S(1)}, bf16[2,1,1,1,16,2560]{5,4,3,2,1,0:T(8,128)(2,1)S(1)}, u32[]{:S(2)}, u32[]{:S(2)}) collective-permute-start(bf16[2,1,1,1,16,2560]{5,4,3,2,1,0:T(8,128)(2,1)S(1)} %pad_maximum_fusion.11), channel_id=1, source_target_pairs={{0,1},{1,0},{2,6},{3,7},{4,5},{5,4},{6,2},{7,3},{8,9},{9,8},{10,14... | collective-permute-start | bytes 491528 | tf_op jit(solution)/shard_map/ppermute | solution.py:77
  22.7 1.5 %collective-permute-start.6 = (bf16[2,2,1,1,16,2560]{5,4,3,2,1,0:T(8,128)(2,1)S(1)}, bf16[2,2,1,1,16,2560]{5,4,3,2,1,0:T(8,128)(2,1)S(1)}, u32[]{:S(2)}, u32[]{:S(2)}) collective-permute-start(bf16[2,2,1,1,16,2560]{5,4,3,2,1,0:T(8,128)(2,1)S(1)} %pad_maximum_fusion.6), channel_id=1, source_target_pairs={{0,1},{1,0},{2,6},{3,7},{4,5},{5,4},{6,2},{7,3},{8,9},{9,8},{10,14... | collective-permute-start | bytes 983048 | tf_op jit(solution)/shard_map/ppermute | solution.py:77
  24.9 1.8 %collective-permute-start.10 = (bf16[2,1,1,2,16,2560]{5,4,3,2,1,0:T(8,128)(2,1)S(1)}, bf16[2,1,1,2,16,2560]{5,4,3,2,1,0:T(8,128)(2,1)S(1)}, u32[]{:S(2)}, u32[]{:S(2)}) collective-permute-start(bf16[2,1,1,2,16,2560]{5,4,3,2,1,0:T(8,128)(2,1)S(1)} %pad_maximum_fusion.7), channel_id=1, source_target_pairs={{0,4},{1,5},{2,3},{3,2},{4,0},{5,1},{6,7},{7,6},{8,12},{9,13},{10,... | collective-permute-start | bytes 983048 | tf_op jit(solution)/shard_map/ppermute | solution.py:77
  26.7 1.5 %collective-permute-done.2 = bf16[2,1,1,2,16,2176]{5,4,3,2,1,0:T(8,128)(2,1)S(1)} collective-permute-done((bf16[2,1,1,2,16,2176]{5,4,3,2,1,0:T(8,128)(2,1)S(1)}, bf16[2,1,1,2,16,2176]{5,4,3,2,1,0:T(8,128)(2,1)S(1)}, u32[]{:S(2)}, u32[]{:S(2)}) %collective-permute-start.2) | collective-permute-done | bytes 278560 | tf_op jit(solution)/shard_map/ppermute | solution.py:77
  28.3 1.6 %collective-permute-start.3 = (bf16[2,2,1,2,16,2176]{5,4,3,2,1,0:T(8,128)(2,1)S(1)}, bf16[2,2,1,2,16,2176]{5,4,3,2,1,0:T(8,128)(2,1)S(1)}, u32[]{:S(2)}, u32[]{:S(2)}) collective-permute-start(bf16[2,2,1,2,16,2176]{5,4,3,2,1,0:T(8,128)(2,1)S(1)} %pad_maximum_fusion.5), channel_id=1, source_target_pairs={{0,4},{1,5},{2,3},{3,2},{4,0},{5,1},{6,7},{7,6},{8,12},{9,13},{10,... | collective-permute-start | bytes 1671176 | tf_op jit(solution)/shard_map/ppermute | solution.py:77
  29.9 3.4 %collective-permute-done.6 = bf16[2,2,1,1,16,2560]{5,4,3,2,1,0:T(8,128)(2,1)S(1)} collective-permute-done((bf16[2,2,1,1,16,2560]{5,4,3,2,1,0:T(8,128)(2,1)S(1)}, bf16[2,2,1,1,16,2560]{5,4,3,2,1,0:T(8,128)(2,1)S(1)}, u32[]{:S(2)}, u32[]{:S(2)}) %collective-permute-start.6) | collective-permute-done | bytes 327712 | tf_op jit(solution)/shard_map/ppermute | solution.py:77
  33.3 1.7 %collective-permute-start.7 = (bf16[2,2,1,2,16,2560]{5,4,3,2,1,0:T(8,128)(2,1)S(1)}, bf16[2,2,1,2,16,2560]{5,4,3,2,1,0:T(8,128)(2,1)S(1)}, u32[]{:S(2)}, u32[]{:S(2)}) collective-permute-start(bf16[2,2,1,2,16,2560]{5,4,3,2,1,0:T(8,128)(2,1)S(1)} %pad_maximum_fusion.3), channel_id=1, source_target_pairs={{0,4},{1,5},{2,3},{3,2},{4,0},{5,1},{6,7},{7,6},{8,12},{9,13},{10,... | collective-permute-start | bytes 1966088 | tf_op jit(solution)/shard_map/ppermute | solution.py:77
  35.1 1.2 %collective-permute-start.11 = (bf16[2,1,2,2,16,2560]{5,4,3,2,1,0:T(8,128)(2,1)S(1)}, bf16[2,1,2,2,16,2560]{5,4,3,2,1,0:T(8,128)(2,1)S(1)}, u32[]{:S(2)}, u32[]{:S(2)}) collective-permute-start(bf16[2,1,2,2,16,2560]{5,4,3,2,1,0:T(8,128)(2,1)S(1)} %pad_maximum_fusion.4), channel_id=1, source_target_pairs={{0,8},{1,9},{2,10},{3,11},{4,12},{5,13},{6,14},{7,15},{8,0},{9,1},... | collective-permute-start | bytes 1966088 | tf_op jit(solution)/shard_map/ppermute | solution.py:77
  36.3 1.8 %collective-permute-done.3 = bf16[2,2,1,2,16,2176]{5,4,3,2,1,0:T(8,128)(2,1)S(1)} collective-permute-done((bf16[2,2,1,2,16,2176]{5,4,3,2,1,0:T(8,128)(2,1)S(1)}, bf16[2,2,1,2,16,2176]{5,4,3,2,1,0:T(8,128)(2,1)S(1)}, u32[]{:S(2)}, u32[]{:S(2)}) %collective-permute-start.3) | collective-permute-done | bytes 557088 | tf_op jit(solution)/shard_map/ppermute | solution.py:77
  39.1 2.3 %fusion.32 = f32[256,512]{1,0:T(8,128)S(1)} fusion(bf16[1,7168,512]{2,1,0:T(8,128)(2,1)} %param.10, bf16[256,2176]{1,0:T(8,128)(2,1)S(1)} %bitcast.92), kind=kOutput, calls=%fused_computation.39 | convolution fusion | flops 536870912 | bytes 3670016 | tf_op jit(solution)/shard_map/dot_general | solution.py:160
  42.1 7.1 %collective-permute-done.11 = bf16[2,1,2,2,16,2560]{5,4,3,2,1,0:T(8,128)(2,1)S(1)} collective-permute-done((bf16[2,1,2,2,16,2560]{5,4,3,2,1,0:T(8,128)(2,1)S(1)}, bf16[2,1,2,2,16,2560]{5,4,3,2,1,0:T(8,128)(2,1)S(1)}, u32[]{:S(2)}, u32[]{:S(2)}) %collective-permute-start.11) | collective-permute-done | bytes 655392 | tf_op jit(solution)/shard_map/ppermute | solution.py:77
  58.0 1.2 %slice-done.3 = s8[3145728]{0:T(1024)(128)(4,1)S(1)} async-done(((s8[7340032]{0:T(1024)(128)(4,1)}), s8[3145728]{0:T(1024)(128)(4,1)S(1)}, s32[]{:S(2)}) %slice-start.3) | async-done | bytes 3145752
  66.4 1.0 collective-permute-done.17
  68.3 1.1 collective-permute-start.20
  69.8 4.8 %collective-permute-done.16 = bf16[2,2,1,2,16,2048]{5,4,3,2,1,0:T(8,128)(2,1)S(1)} collective-permute-done((bf16[2,2,1,2,16,2048]{5,4,3,2,1,0:T(8,128)(2,1)S(1)}, bf16[2,2,1,2,16,2048]{5,4,3,2,1,0:T(8,128)(2,1)S(1)}, u32[]{:S(2)}, u32[]{:S(2)}) %collective-permute-start.16) | collective-permute-done | bytes 524320 | tf_op jit(solution)/shard_map/ppermute | solution.py:77
  74.7 1.3 %collective-permute-start.19 = (bf16[1,2,1,2,16,2048]{5,4,3,2,1,0:T(8,128)(2,1)S(1)}, bf16[1,2,1,2,16,2048]{5,4,3,2,1,0:T(8,128)(2,1)S(1)}, u32[]{:S(2)}, u32[]{:S(2)}) collective-permute-start(bf16[1,2,1,2,16,2048]{5,4,3,2,1,0:T(8,128)(2,1)S(1)} %slice.179), channel_id=1, source_target_pairs={{0,16},{1,17},{2,18},{3,19},{4,20},{5,21},{6,22},{7,23},{8,24},{9,... | collective-permute-start | bytes 786440 | tf_op jit(solution)/shard_map/ppermute | solution.py:77
  76.0 5.6 %collective-permute-done.20 = bf16[2,2,1,2,16,2560]{5,4,3,2,1,0:T(8,128)(2,1)S(1)} collective-permute-done((bf16[2,2,1,2,16,2560]{5,4,3,2,1,0:T(8,128)(2,1)S(1)}, bf16[2,2,1,2,16,2560]{5,4,3,2,1,0:T(8,128)(2,1)S(1)}, u32[]{:S(2)}, u32[]{:S(2)}) %collective-permute-start.20) | collective-permute-done | bytes 655392 | tf_op jit(solution)/shard_map/ppermute | solution.py:77
  81.8 10.5 %collective-permute-done.22 = bf16[2,1,2,2,16,2560]{5,4,3,2,1,0:T(8,128)(2,1)S(1)} collective-permute-done((bf16[2,1,2,2,16,2560]{5,4,3,2,1,0:T(8,128)(2,1)S(1)}, bf16[2,1,2,2,16,2560]{5,4,3,2,1,0:T(8,128)(2,1)S(1)}, u32[]{:S(2)}, u32[]{:S(2)}) %collective-permute-start.22) | collective-permute-done | bytes 655392 | tf_op jit(solution)/shard_map/ppermute | solution.py:77
  93.8 8.4 %collective-permute-done.21 = bf16[2,2,1,1,16,2560]{5,4,3,2,1,0:T(8,128)(2,1)S(1)} collective-permute-done((bf16[2,2,1,1,16,2560]{5,4,3,2,1,0:T(8,128)(2,1)S(1)}, bf16[2,2,1,1,16,2560]{5,4,3,2,1,0:T(8,128)(2,1)S(1)}, u32[]{:S(2)}, u32[]{:S(2)}) %collective-permute-start.21) | collective-permute-done | bytes 327712 | tf_op jit(solution)/shard_map/ppermute | solution.py:77
  102.7 1.8 %collective-permute-start.26 = (bf16[1,2,1,1,16,2560]{5,4,3,2,1,0:T(8,128)(2,1)S(1)}, bf16[1,2,1,1,16,2560]{5,4,3,2,1,0:T(8,128)(2,1)S(1)}, u32[]{:S(2)}, u32[]{:S(2)}) collective-permute-start(bf16[1,2,1,1,16,2560]{5,4,3,2,1,0:T(8,128)(2,1)S(1)} %slice.193), channel_id=1, source_target_pairs={{0,16},{1,17},{2,18},{3,19},{4,20},{5,21},{6,22},{7,23},{8,24},{9,... | collective-permute-start | bytes 491528 | tf_op jit(solution)/shard_map/ppermute | solution.py:77
  104.6 1.3 %collective-permute-start.27 = (bf16[2,1,1,1,16,2560]{5,4,3,2,1,0:T(8,128)(2,1)S(1)}, bf16[2,1,1,1,16,2560]{5,4,3,2,1,0:T(8,128)(2,1)S(1)}, u32[]{:S(2)}, u32[]{:S(2)}) collective-permute-start(bf16[2,1,1,1,16,2560]{5,4,3,2,1,0:T(8,128)(2,1)S(1)} %slice.195), channel_id=1, source_target_pairs={{0,1},{1,0},{2,6},{3,7},{4,5},{5,4},{6,2},{7,3},{8,9},{9,8},{10,14... | collective-permute-start | bytes 491528 | tf_op jit(solution)/shard_map/ppermute | solution.py:77
  106.0 1.4 %collective-permute-done.23 = bf16[1,2,1,1,16,2048]{5,4,3,2,1,0:T(8,128)(2,1)S(1)} collective-permute-done((bf16[1,2,1,1,16,2048]{5,4,3,2,1,0:T(8,128)(2,1)S(1)}, bf16[1,2,1,1,16,2048]{5,4,3,2,1,0:T(8,128)(2,1)S(1)}, u32[]{:S(2)}, u32[]{:S(2)}) %collective-permute-start.23) | collective-permute-done | bytes 131104 | tf_op jit(solution)/shard_map/ppermute | solution.py:77
  107.4 1.2 collective-permute-start.25
  108.6 1.4 %collective-permute-done.27 = bf16[2,1,1,1,16,2560]{5,4,3,2,1,0:T(8,128)(2,1)S(1)} collective-permute-done((bf16[2,1,1,1,16,2560]{5,4,3,2,1,0:T(8,128)(2,1)S(1)}, bf16[2,1,1,1,16,2560]{5,4,3,2,1,0:T(8,128)(2,1)S(1)}, u32[]{:S(2)}, u32[]{:S(2)}) %collective-permute-start.27) | collective-permute-done | bytes 163872 | tf_op jit(solution)/shard_map/ppermute | solution.py:77
  111.7 4.4 %collective-permute-start.29 = (bf16[1,1,1,1,16,2560]{5,4,3,2,1,0:T(8,128)(2,1)S(1)}, bf16[1,1,1,1,16,2560]{5,4,3,2,1,0:T(8,128)(2,1)S(1)}, u32[]{:S(2)}, u32[]{:S(2)}) collective-permute-start(bf16[1,1,1,1,16,2560]{5,4,3,2,1,0:T(8,128)(2,1)S(1)} %slice.199), channel_id=1, source_target_pairs={{0,8},{1,9},{2,10},{3,11},{4,12},{5,13},{6,14},{7,15},{8,0},{9,1},... | collective-permute-start | bytes 245768 | tf_op jit(solution)/shard_map/ppermute | solution.py:77
  116.3 2.2 %collective-permute-done.29 = bf16[1,1,1,1,16,2560]{5,4,3,2,1,0:T(8,128)(2,1)S(1)} collective-permute-done((bf16[1,1,1,1,16,2560]{5,4,3,2,1,0:T(8,128)(2,1)S(1)}, bf16[1,1,1,1,16,2560]{5,4,3,2,1,0:T(8,128)(2,1)S(1)}, u32[]{:S(2)}, u32[]{:S(2)}) %collective-permute-start.29) | collective-permute-done | bytes 81952 | tf_op jit(solution)/shard_map/ppermute | solution.py:77
  (105 shorter events, 29.4 us)
Async XLA Ops:
  2.6 7.3 %collective-permute-start = (bf16[1,1,1,1,16,2176]{5,4,3,2,1,0:T(8,128)(2,1)S(1)}, bf16[1,1,1,1,16,2176]{5,4,3,2,1,0:T(8,128)(2,1)S(1)}, u32[]{:S(2)}, u32[]{:S(2)}) collective-permute-start(bf16[1,1,1,1,16,2176]{5,4,3,2,1,0:T(8,128)(2,1)S(1)} %maximum_bitcast_fusion), channel_id=1, source_target_pairs={{0,16},{1,17},{2,18},{3,19},{4,20},{5,21},{6,22},{7,23},{8,24},{9,... | collective-permute-start | bytes 208904 | tf_op jit(solution)/shard_map/ppermute | solution.py:77
  7.6 4.6 %collective-permute-start.4 = (bf16[1,1,1,1,16,2560]{5,4,3,2,1,0:T(8,128)(2,1)S(1)}, bf16[1,1,1,1,16,2560]{5,4,3,2,1,0:T(8,128)(2,1)S(1)}, u32[]{:S(2)}, u32[]{:S(2)}) collective-permute-start(bf16[1,1,1,1,16,2560]{5,4,3,2,1,0:T(8,128)(2,1)S(1)} %get-tuple-element.37), channel_id=1, source_target_pairs={{0,8},{1,9},{2,10},{3,11},{4,12},{5,13},{6,14},{7,15},{8,0},{9,1},... | collective-permute-start | bytes 245768 | tf_op jit(solution)/shard_map/ppermute | solution.py:77
  9.3 8.9 %collective-permute-start.8 = (bf16[1,1,1,1,16,2560]{5,4,3,2,1,0:T(8,128)(2,1)S(1)}, bf16[1,1,1,1,16,2560]{5,4,3,2,1,0:T(8,128)(2,1)S(1)}, u32[]{:S(2)}, u32[]{:S(2)}) collective-permute-start(bf16[1,1,1,1,16,2560]{5,4,3,2,1,0:T(8,128)(2,1)S(1)} %get-tuple-element.38), channel_id=1, source_target_pairs={{0,16},{1,17},{2,18},{3,19},{4,20},{5,21},{6,22},{7,23},{8,24},{9,... | collective-permute-start | bytes 245768 | tf_op jit(solution)/shard_map/ppermute | solution.py:77
  9.9 11.7 %collective-permute-start.1 = (bf16[2,1,1,1,16,2176]{5,4,3,2,1,0:T(8,128)(2,1)S(1)}, bf16[2,1,1,1,16,2176]{5,4,3,2,1,0:T(8,128)(2,1)S(1)}, u32[]{:S(2)}, u32[]{:S(2)}) collective-permute-start(bf16[2,1,1,1,16,2176]{5,4,3,2,1,0:T(8,128)(2,1)S(1)} %pad_maximum_fusion.12), channel_id=1, source_target_pairs={{0,1},{1,0},{2,6},{3,7},{4,5},{5,4},{6,2},{7,3},{8,9},{9,8},{10,14... | collective-permute-start | bytes 417800 | tf_op jit(solution)/shard_map/ppermute | solution.py:77
  12.2 10.4 %collective-permute-start.5 = (bf16[1,2,1,1,16,2560]{5,4,3,2,1,0:T(8,128)(2,1)S(1)}, bf16[1,2,1,1,16,2560]{5,4,3,2,1,0:T(8,128)(2,1)S(1)}, u32[]{:S(2)}, u32[]{:S(2)}) collective-permute-start(bf16[1,2,1,1,16,2560]{5,4,3,2,1,0:T(8,128)(2,1)S(1)} %pad_maximum_fusion.10), channel_id=1, source_target_pairs={{0,16},{1,17},{2,18},{3,19},{4,20},{5,21},{6,22},{7,23},{8,24},{9,... | collective-permute-start | bytes 491528 | tf_op jit(solution)/shard_map/ppermute | solution.py:77
  18.2 6.7 %collective-permute-start.9 = (bf16[2,1,1,1,16,2560]{5,4,3,2,1,0:T(8,128)(2,1)S(1)}, bf16[2,1,1,1,16,2560]{5,4,3,2,1,0:T(8,128)(2,1)S(1)}, u32[]{:S(2)}, u32[]{:S(2)}) collective-permute-start(bf16[2,1,1,1,16,2560]{5,4,3,2,1,0:T(8,128)(2,1)S(1)} %pad_maximum_fusion.11), channel_id=1, source_target_pairs={{0,1},{1,0},{2,6},{3,7},{4,5},{5,4},{6,2},{7,3},{8,9},{9,8},{10,14... | collective-permute-start | bytes 491528 | tf_op jit(solution)/shard_map/ppermute | solution.py:77
  21.6 6.6 %collective-permute-start.2 = (bf16[2,1,1,2,16,2176]{5,4,3,2,1,0:T(8,128)(2,1)S(1)}, bf16[2,1,1,2,16,2176]{5,4,3,2,1,0:T(8,128)(2,1)S(1)}, u32[]{:S(2)}, u32[]{:S(2)}) collective-permute-start(bf16[2,1,1,2,16,2176]{5,4,3,2,1,0:T(8,128)(2,1)S(1)} %pad_maximum_fusion.8), channel_id=1, source_target_pairs={{0,8},{1,9},{2,10},{3,11},{4,12},{5,13},{6,14},{7,15},{8,0},{9,1},... | collective-permute-start | bytes 835592 | tf_op jit(solution)/shard_map/ppermute | solution.py:77
  22.7 10.6 %collective-permute-start.6 = (bf16[2,2,1,1,16,2560]{5,4,3,2,1,0:T(8,128)(2,1)S(1)}, bf16[2,2,1,1,16,2560]{5,4,3,2,1,0:T(8,128)(2,1)S(1)}, u32[]{:S(2)}, u32[]{:S(2)}) collective-permute-start(bf16[2,2,1,1,16,2560]{5,4,3,2,1,0:T(8,128)(2,1)S(1)} %pad_maximum_fusion.6), channel_id=1, source_target_pairs={{0,1},{1,0},{2,6},{3,7},{4,5},{5,4},{6,2},{7,3},{8,9},{9,8},{10,14... | collective-permute-start | bytes 983048 | tf_op jit(solution)/shard_map/ppermute | solution.py:77
  24.9 10.1 %collective-permute-start.10 = (bf16[2,1,1,2,16,2560]{5,4,3,2,1,0:T(8,128)(2,1)S(1)}, bf16[2,1,1,2,16,2560]{5,4,3,2,1,0:T(8,128)(2,1)S(1)}, u32[]{:S(2)}, u32[]{:S(2)}) collective-permute-start(bf16[2,1,1,2,16,2560]{5,4,3,2,1,0:T(8,128)(2,1)S(1)} %pad_maximum_fusion.7), channel_id=1, source_target_pairs={{0,4},{1,5},{2,3},{3,2},{4,0},{5,1},{6,7},{7,6},{8,12},{9,13},{10,... | collective-permute-start | bytes 983048 | tf_op jit(solution)/shard_map/ppermute | solution.py:77
  28.3 9.7 %collective-permute-start.3 = (bf16[2,2,1,2,16,2176]{5,4,3,2,1,0:T(8,128)(2,1)S(1)}, bf16[2,2,1,2,16,2176]{5,4,3,2,1,0:T(8,128)(2,1)S(1)}, u32[]{:S(2)}, u32[]{:S(2)}) collective-permute-start(bf16[2,2,1,2,16,2176]{5,4,3,2,1,0:T(8,128)(2,1)S(1)} %pad_maximum_fusion.5), channel_id=1, source_target_pairs={{0,4},{1,5},{2,3},{3,2},{4,0},{5,1},{6,7},{7,6},{8,12},{9,13},{10,... | collective-permute-start | bytes 1671176 | tf_op jit(solution)/shard_map/ppermute | solution.py:77
  33.3 16.1 %collective-permute-start.7 = (bf16[2,2,1,2,16,2560]{5,4,3,2,1,0:T(8,128)(2,1)S(1)}, bf16[2,2,1,2,16,2560]{5,4,3,2,1,0:T(8,128)(2,1)S(1)}, u32[]{:S(2)}, u32[]{:S(2)}) collective-permute-start(bf16[2,2,1,2,16,2560]{5,4,3,2,1,0:T(8,128)(2,1)S(1)} %pad_maximum_fusion.3), channel_id=1, source_target_pairs={{0,4},{1,5},{2,3},{3,2},{4,0},{5,1},{6,7},{7,6},{8,12},{9,13},{10,... | collective-permute-start | bytes 1966088 | tf_op jit(solution)/shard_map/ppermute | solution.py:77
  35.0 6.4 %copy-start = (bf16[1,7168,512]{2,1,0:T(8,128)(2,1)S(1)}, bf16[1,7168,512]{2,1,0:T(8,128)(2,1)}, u32[]{:S(2)}) copy-start(bf16[1,7168,512]{2,1,0:T(8,128)(2,1)} %param.9) | copy-start | bytes 22020100
  35.1 14.1 %collective-permute-start.11 = (bf16[2,1,2,2,16,2560]{5,4,3,2,1,0:T(8,128)(2,1)S(1)}, bf16[2,1,2,2,16,2560]{5,4,3,2,1,0:T(8,128)(2,1)S(1)}, u32[]{:S(2)}, u32[]{:S(2)}) collective-permute-start(bf16[2,1,2,2,16,2560]{5,4,3,2,1,0:T(8,128)(2,1)S(1)} %pad_maximum_fusion.4), channel_id=1, source_target_pairs={{0,8},{1,9},{2,10},{3,11},{4,12},{5,13},{6,14},{7,15},{8,0},{9,1},... | collective-permute-start | bytes 1966088 | tf_op jit(solution)/shard_map/ppermute | solution.py:77
  38.2 13.7 %collective-permute-start.12 = (bf16[256,2176]{1,0:T(8,128)(2,1)S(1)}, bf16[256,2176]{1,0:T(8,128)(2,1)S(1)}, u32[]{:S(2)}, u32[]{:S(2)}) collective-permute-start(bf16[256,2176]{1,0:T(8,128)(2,1)S(1)} %bitcast.91), channel_id=1, source_target_pairs={{0,2},{1,3},{2,0},{3,1},{4,6},{5,7},{6,4},{7,5},{8,10},{9,11},{10,... | collective-permute-start | bytes 3342344 | tf_op jit(solution)/shard_map/ppermute | solution.py:77
  49.3 4.7 %collective-permute-start.14 = (bf16[256,2560]{1,0:T(8,128)(2,1)S(1)}, bf16[256,2560]{1,0:T(8,128)(2,1)S(1)}, u32[]{:S(2)}, u32[]{:S(2)}) collective-permute-start(bf16[256,2560]{1,0:T(8,128)(2,1)S(1)} %bitcast.81), channel_id=1, source_target_pairs={{0,2},{1,3},{2,0},{3,1},{4,6},{5,7},{6,4},{7,5},{8,10},{9,11},{10,... | collective-permute-start | bytes 3932168 | tf_op jit(solution)/shard_map/ppermute | solution.py:77
  49.6 3.1 %slice-start.1 = ((s8[7340032]{0:T(1024)(128)(4,1)}), s8[3145728]{0:T(1024)(128)(4,1)S(1)}, s32[]{:S(2)}) async-start(s8[7340032]{0:T(1024)(128)(4,1)} %bitcast.99), calls=%async_computation.1 | async-start | bytes 6291456
  50.4 5.3 %collective-permute-start.13 = (bf16[256,2560]{1,0:T(8,128)(2,1)S(1)}, bf16[256,2560]{1,0:T(8,128)(2,1)S(1)}, u32[]{:S(2)}, u32[]{:S(2)}) collective-permute-start(bf16[256,2560]{1,0:T(8,128)(2,1)S(1)} %bitcast.84), channel_id=1, source_target_pairs={{0,2},{1,3},{2,0},{3,1},{4,6},{5,7},{6,4},{7,5},{8,10},{9,11},{10,... | collective-permute-start | bytes 3932168 | tf_op jit(solution)/shard_map/ppermute | solution.py:77
  60.8 3.8 %collective-permute-start.15 = (bf16[256,2048]{1,0:T(8,128)(2,1)S(1)}, bf16[256,2048]{1,0:T(8,128)(2,1)S(1)}, u32[]{:S(2)}, u32[]{:S(2)}) collective-permute-start(bf16[256,2048]{1,0:T(8,128)(2,1)S(1)} %multiply_convert_fusion), channel_id=1, source_target_pairs={{0,2},{1,3},{2,0},{3,1},{4,6},{5,7},{6,4},{7,5},{8,10},{9,11},{10,... | collective-permute-start | bytes 3145736 | tf_op jit(solution)/shard_map/ppermute | solution.py:77
  61.3 4.2 %collective-permute-start.18 = (bf16[256,2560]{1,0:T(8,128)(2,1)S(1)}, bf16[256,2560]{1,0:T(8,128)(2,1)S(1)}, u32[]{:S(2)}, u32[]{:S(2)}) collective-permute-start(bf16[256,2560]{1,0:T(8,128)(2,1)S(1)} %fusion.1), channel_id=1, source_target_pairs={{0,2},{1,3},{2,0},{3,1},{4,6},{5,7},{6,4},{7,5},{8,10},{9,11},{10,... | collective-permute-start | bytes 3932168 | tf_op jit(solution)/shard_map/ppermute | solution.py:77
  62.3 5.1 %collective-permute-start.17 = (bf16[256,2560]{1,0:T(8,128)(2,1)S(1)}, bf16[256,2560]{1,0:T(8,128)(2,1)S(1)}, u32[]{:S(2)}, u32[]{:S(2)}) collective-permute-start(bf16[256,2560]{1,0:T(8,128)(2,1)S(1)} %fusion), channel_id=1, source_target_pairs={{0,2},{1,3},{2,0},{3,1},{4,6},{5,7},{6,4},{7,5},{8,10},{9,11},{10,... | collective-permute-start | bytes 3932168 | tf_op jit(solution)/shard_map/ppermute | solution.py:77
  65.3 9.2 %collective-permute-start.16 = (bf16[2,2,1,2,16,2048]{5,4,3,2,1,0:T(8,128)(2,1)S(1)}, bf16[2,2,1,2,16,2048]{5,4,3,2,1,0:T(8,128)(2,1)S(1)}, u32[]{:S(2)}, u32[]{:S(2)}) collective-permute-start(bf16[2,2,1,2,16,2048]{5,4,3,2,1,0:T(8,128)(2,1)S(1)} %slice.175), channel_id=1, source_target_pairs={{0,4},{1,5},{2,3},{3,2},{4,0},{5,1},{6,7},{7,6},{8,12},{9,13},{10,... | collective-permute-start | bytes 1572872 | tf_op jit(solution)/shard_map/ppermute | solution.py:77
  68.3 13.3 %collective-permute-start.20 = (bf16[2,2,1,2,16,2560]{5,4,3,2,1,0:T(8,128)(2,1)S(1)}, bf16[2,2,1,2,16,2560]{5,4,3,2,1,0:T(8,128)(2,1)S(1)}, u32[]{:S(2)}, u32[]{:S(2)}) collective-permute-start(bf16[2,2,1,2,16,2560]{5,4,3,2,1,0:T(8,128)(2,1)S(1)} %slice.181), channel_id=1, source_target_pairs={{0,4},{1,5},{2,3},{3,2},{4,0},{5,1},{6,7},{7,6},{8,12},{9,13},{10,... | collective-permute-start | bytes 1966088 | tf_op jit(solution)/shard_map/ppermute | solution.py:77
  69.4 22.9 %collective-permute-start.22 = (bf16[2,1,2,2,16,2560]{5,4,3,2,1,0:T(8,128)(2,1)S(1)}, bf16[2,1,2,2,16,2560]{5,4,3,2,1,0:T(8,128)(2,1)S(1)}, u32[]{:S(2)}, u32[]{:S(2)}) collective-permute-start(bf16[2,1,2,2,16,2560]{5,4,3,2,1,0:T(8,128)(2,1)S(1)} %slice.185), channel_id=1, source_target_pairs={{0,8},{1,9},{2,10},{3,11},{4,12},{5,13},{6,14},{7,15},{8,0},{9,1},... | collective-permute-start | bytes 1966088 | tf_op jit(solution)/shard_map/ppermute | solution.py:77
  74.7 27.5 %collective-permute-start.19 = (bf16[1,2,1,2,16,2048]{5,4,3,2,1,0:T(8,128)(2,1)S(1)}, bf16[1,2,1,2,16,2048]{5,4,3,2,1,0:T(8,128)(2,1)S(1)}, u32[]{:S(2)}, u32[]{:S(2)}) collective-permute-start(bf16[1,2,1,2,16,2048]{5,4,3,2,1,0:T(8,128)(2,1)S(1)} %slice.179), channel_id=1, source_target_pairs={{0,16},{1,17},{2,18},{3,19},{4,20},{5,21},{6,22},{7,23},{8,24},{9,... | collective-permute-start | bytes 786440 | tf_op jit(solution)/shard_map/ppermute | solution.py:77
  92.3 9.8 %collective-permute-start.21 = (bf16[2,2,1,1,16,2560]{5,4,3,2,1,0:T(8,128)(2,1)S(1)}, bf16[2,2,1,1,16,2560]{5,4,3,2,1,0:T(8,128)(2,1)S(1)}, u32[]{:S(2)}, u32[]{:S(2)}) collective-permute-start(bf16[2,2,1,1,16,2560]{5,4,3,2,1,0:T(8,128)(2,1)S(1)} %slice.183), channel_id=1, source_target_pairs={{0,1},{1,0},{2,6},{3,7},{4,5},{5,4},{6,2},{7,3},{8,9},{9,8},{10,14... | collective-permute-start | bytes 983048 | tf_op jit(solution)/shard_map/ppermute | solution.py:77
  93.1 11.4 %collective-permute-start.24 = (bf16[2,1,1,2,16,2560]{5,4,3,2,1,0:T(8,128)(2,1)S(1)}, bf16[2,1,1,2,16,2560]{5,4,3,2,1,0:T(8,128)(2,1)S(1)}, u32[]{:S(2)}, u32[]{:S(2)}) collective-permute-start(bf16[2,1,1,2,16,2560]{5,4,3,2,1,0:T(8,128)(2,1)S(1)} %slice.189), channel_id=1, source_target_pairs={{0,4},{1,5},{2,3},{3,2},{4,0},{5,1},{6,7},{7,6},{8,12},{9,13},{10,... | collective-permute-start | bytes 983048 | tf_op jit(solution)/shard_map/ppermute | solution.py:77
  102.3 5.0 %collective-permute-start.23 = (bf16[1,2,1,1,16,2048]{5,4,3,2,1,0:T(8,128)(2,1)S(1)}, bf16[1,2,1,1,16,2048]{5,4,3,2,1,0:T(8,128)(2,1)S(1)}, u32[]{:S(2)}, u32[]{:S(2)}) collective-permute-start(bf16[1,2,1,1,16,2048]{5,4,3,2,1,0:T(8,128)(2,1)S(1)} %slice.187), channel_id=1, source_target_pairs={{0,1},{1,0},{2,6},{3,7},{4,5},{5,4},{6,2},{7,3},{8,9},{9,8},{10,14... | collective-permute-start | bytes 393224 | tf_op jit(solution)/shard_map/ppermute | solution.py:77
  102.7 8.1 %collective-permute-start.26 = (bf16[1,2,1,1,16,2560]{5,4,3,2,1,0:T(8,128)(2,1)S(1)}, bf16[1,2,1,1,16,2560]{5,4,3,2,1,0:T(8,128)(2,1)S(1)}, u32[]{:S(2)}, u32[]{:S(2)}) collective-permute-start(bf16[1,2,1,1,16,2560]{5,4,3,2,1,0:T(8,128)(2,1)S(1)} %slice.193), channel_id=1, source_target_pairs={{0,16},{1,17},{2,18},{3,19},{4,20},{5,21},{6,22},{7,23},{8,24},{9,... | collective-permute-start | bytes 491528 | tf_op jit(solution)/shard_map/ppermute | solution.py:77
  104.6 5.4 %collective-permute-start.27 = (bf16[2,1,1,1,16,2560]{5,4,3,2,1,0:T(8,128)(2,1)S(1)}, bf16[2,1,1,1,16,2560]{5,4,3,2,1,0:T(8,128)(2,1)S(1)}, u32[]{:S(2)}, u32[]{:S(2)}) collective-permute-start(bf16[2,1,1,1,16,2560]{5,4,3,2,1,0:T(8,128)(2,1)S(1)} %slice.195), channel_id=1, source_target_pairs={{0,1},{1,0},{2,6},{3,7},{4,5},{5,4},{6,2},{7,3},{8,9},{9,8},{10,14... | collective-permute-start | bytes 491528 | tf_op jit(solution)/shard_map/ppermute | solution.py:77
  107.4 8.6 %collective-permute-start.25 = (bf16[1,1,1,1,16,2048]{5,4,3,2,1,0:T(8,128)(2,1)S(1)}, bf16[1,1,1,1,16,2048]{5,4,3,2,1,0:T(8,128)(2,1)S(1)}, u32[]{:S(2)}, u32[]{:S(2)}) collective-permute-start(bf16[1,1,1,1,16,2048]{5,4,3,2,1,0:T(8,128)(2,1)S(1)} %slice.191), channel_id=1, source_target_pairs={{0,8},{1,9},{2,10},{3,11},{4,12},{5,13},{6,14},{7,15},{8,0},{9,1},... | collective-permute-start | bytes 196616 | tf_op jit(solution)/shard_map/ppermute | solution.py:77
  110.8 5.4 %collective-permute-start.28 = (bf16[1,1,1,1,16,2560]{5,4,3,2,1,0:T(8,128)(2,1)S(1)}, bf16[1,1,1,1,16,2560]{5,4,3,2,1,0:T(8,128)(2,1)S(1)}, u32[]{:S(2)}, u32[]{:S(2)}) collective-permute-start(bf16[1,1,1,1,16,2560]{5,4,3,2,1,0:T(8,128)(2,1)S(1)} %slice.197), channel_id=1, source_target_pairs={{0,16},{1,17},{2,18},{3,19},{4,20},{5,21},{6,22},{7,23},{8,24},{9,... | collective-permute-start | bytes 245768 | tf_op jit(solution)/shard_map/ppermute | solution.py:77
  111.7 6.8 %collective-permute-start.29 = (bf16[1,1,1,1,16,2560]{5,4,3,2,1,0:T(8,128)(2,1)S(1)}, bf16[1,1,1,1,16,2560]{5,4,3,2,1,0:T(8,128)(2,1)S(1)}, u32[]{:S(2)}, u32[]{:S(2)}) collective-permute-start(bf16[1,1,1,1,16,2560]{5,4,3,2,1,0:T(8,128)(2,1)S(1)} %slice.199), channel_id=1, source_target_pairs={{0,8},{1,9},{2,10},{3,11},{4,12},{5,13},{6,14},{7,15},{8,0},{9,1},... | collective-permute-start | bytes 245768 | tf_op jit(solution)/shard_map/ppermute | solution.py:77
  (3 other events, 7.3 us)
where the time goes:
time: 120 us; the launch traced here: 119 us
  waiting for transfers between devices  56.5 us (47%)
  starting transfers between devices  37.5 us (31%)
  matrix products  16.2 us (14%)
  local copies, waits for them, and re-layouts  5.84 us (5%)
  other arithmetic  2.68 us (2%)
    ppermute x30, waiting for transfers between devices, exchange(): return lax.ppermute(block, AXES, perm)  56.5 us
    ppermute x30, starting transfers between devices, exchange(): return lax.ppermute(block, AXES, perm)  37.5 us
    dot_general x6, matrix products, dense(): jnp.dot(rows, w_up[0, lo:hi], preferred_element_type=jnp.float32)  6.5 us
    dot_general x6, matrix products, product(): jnp.dot(hidden[j], w_down[:, lo:hi], preferred_element_type=jnp.float32)  4.98 us
    dot_general x6, matrix products, dense(): jnp.dot(rows, w_gate[0, lo:hi], preferred_element_type=jnp.float32)  4.76 us
    unnamed x12, local copies, waits for them, and re-layouts  3.8 us
  transfers between devices with their start and end apart: 30, of which 20 were waited for; matrix products, arithmetic and copies ran while one was open for 13% of the time, Pallas kernels for 0%

commit v1 on v0

--- a/solution.py
+++ b/solution.py
@@ -60,10 +60,8 @@
 def partner(step, e, t):
     if step == "core":
         return e ^ 1, t
-    if step == "far":
-        return e ^ 8, t
-    if step == "near":
-        return e ^ 4, t
+    if step in ("far", "near"):
+        return (e ^ 4, t) if (e & 1) == (step == "far") else (e ^ 8, t)
     return (e, t ^ 1) if (e & 1) == (step == "late") else (e ^ 2, t)
 
 
@@ -79,16 +77,18 @@
 
 STEPS = ("far", "near", "late", "early")
 GATHER = (
-    (20, ("near", "far", "early", "late")),
-    (20, ("far", "early", "late", "near")),
-    (16, ("far", "early", "near", "late")),
+    (18, ("near", "far", "early", "late")),
+    (20, ("early", "near", "far", "late")),
+    (18, ("near", "early", "late", "far")),
 )
 SCATTER = (
-    (16, ("late", "far", "early", "near")),
+    (20, ("late", "early", "near", "far")),
     (20, ("near", "late", "early", "far")),
-    (20, ("late", "early", "far", "near")),
+    (16, ("late", "early", "far", "near")),
 )
-TURNS = (0, 1, 2, 0, 2, 1, 2, 0, 1, 0, 1, 2, 0, 1, 2)
+GATHER_TURNS = (10, 11, 12, 10, 11, 12, 12, 10, 11, 12, 10, 11, 10, 10, 10, 11, 11, 12, 12, 11, 12)
+SCATTER_TURNS = (0, 1, 2, 0, 2, 1, 0, 2, 1, 0, 2, 1, 0, 2, 1)
+PACKED = 2
 
 
 def chunks_of(width, plan):
@@ -100,13 +100,46 @@
     return [(lo, hi, order) for lo, hi, (_, order) in zip(edges[:-1], edges[1:], plan)]
 
 
-def gather_rows(block, order):
-    count, width = block.shape
-    rows = block.reshape(1, 1, 1, 1, count, width)
-    for step in order:
-        rows = jnp.concatenate([rows, exchange(rows, step)], axis=STEPS.index(step))
-    rows = rows.reshape(-1, width)
-    return rows, exchange(rows, "core")
+def gather_rows(tokens, packed, w_gate, w_up, chunks):
+    count, width = tokens.shape
+    blocks = [tokens[:, lo:hi] for lo, hi, _ in chunks]
+    blocks[PACKED] = jnp.concatenate([blocks[PACKED], packed], axis=1)
+    state = [[block.reshape(1, 1, 1, 1, count, -1), None, 0] for block in blocks]
+    before = tokens
+    gates, ups, spread = [0.0, 0.0], [0.0, 0.0], [None, None]
+
+    def products(k, j, rows):
+        lo, hi, _ = chunks[k]
+        if k == PACKED:
+            spread[j], rows = rows[:, hi - lo :], rows[:, : hi - lo]
+        gates[j] = gates[j] + jnp.dot(rows, w_gate[lo:hi], preferred_element_type=jnp.float32)
+        ups[j] = ups[j] + jnp.dot(rows, w_up[lo:hi], preferred_element_type=jnp.float32)
+        return ups[j]
+
+    for k in GATHER_TURNS:
+        free, k = k >= 10, k % 10
+        rows, arrived, done = state[k]
+        order = chunks[k][2]
+        if free:
+            pass
+        elif done > 0 and done != len(order) + 1:
+            arrived, before = lax.optimization_barrier((arrived, before))
+        elif done > 0:
+            rows, before = lax.optimization_barrier((rows, before))
+        if 0 < done <= len(order):
+            rows = jnp.concatenate([rows, arrived], axis=STEPS.index(order[done - 1]))
+            before = rows
+        if done < len(order):
+            arrived = exchange(rows, order[done])
+        elif done == len(order):
+            rows = rows.reshape(16 * count, -1)
+            arrived = exchange(rows, "core")
+        elif done == len(order) + 1:
+            before = products(k, 0, rows)
+        else:
+            before = products(k, 1, arrived)
+        state[k] = [rows, arrived, done + 1]
+    return gates, ups, spread
 
 
 def scatter_rows(hidden, scale, w_down, chunks):
@@ -118,10 +151,12 @@
     before = hidden[0]
     count = hidden[0].shape[0] // 16
     outs = [None] * len(chunks)
-    for k in TURNS:
+    for k in SCATTER_TURNS:
+        free, k = k >= 10, k % 10
         arrived, mine, done = state[k]
         lo, hi, order = chunks[k]
-        arrived, before = lax.optimization_barrier((arrived, before))
+        if not free:
+            arrived, before = lax.optimization_barrier((arrived, before))
         if done == 0:
             total = product(0, chunks[k]) + arrived.astype(jnp.float32)
             total = total.reshape(2, 2, 2, 2, count, hi - lo).astype(jnp.bfloat16)
@@ -144,20 +179,7 @@
     high = lax.reduce_precision(weights, 8, 7)
     packed = jnp.concatenate([high, weights - high], axis=1).astype(jnp.bfloat16)
     packed = jnp.pad(packed, ((0, 0), (0, -2 * experts % 128)))
-    chunks = chunks_of(width, GATHER)
-    gates, ups = [0.0, 0.0], [0.0, 0.0]
-    for i, (lo, hi, order) in enumerate(chunks):
-        block = tokens[:, lo:hi]
-        last = i == len(chunks) - 1
-        if last:
-            block = jnp.concatenate([block, packed], axis=1)
-        halves = gather_rows(block, order)
-        if last:
-            spread = [rows[:, hi - lo :] for rows in halves]
-            halves = [rows[:, : hi - lo] for rows in halves]
-        for j, rows in enumerate(halves):
-            gates[j] = gates[j] + jnp.dot(rows, w_gate[0, lo:hi], preferred_element_type=jnp.float32)
-            ups[j] = ups[j] + jnp.dot(rows, w_up[0, lo:hi], preferred_element_type=jnp.float32)
+    gates, ups, spread = gather_rows(tokens, packed, w_gate[0], w_up[0], chunks_of(width, GATHER))
     hidden = [(jax.nn.silu(gate) * up).astype(jnp.bfloat16) for gate, up in zip(gates, ups)]
     me = lax.axis_index("expert")
     column = jnp.arange(spread[0].shape[1], dtype=jnp.int32)

time: 120 us -> 114 us (0.950)
  starting transfers between devices: 37.5 us -> 31.5 us
  waiting for transfers between devices: 56.5 us -> 58.4 us
  matrix products: 16.2 us -> 14.7 us
    ppermute x30, starting transfers between devices: 37.5 us -> 31.5 us  [exchange(): return lax.ppermute(block, AXES, perm)]
    ppermute x30, waiting for transfers between devices: 56.5 us -> 58.4 us  [exchange(): return lax.ppermute(block, AXES, perm)]
    dot_general x12, matrix products: 11.3 us -> 9.66 us  [the longest x6 4.9 us: products(): jnp.dot(rows, w_up[lo:hi], preferred_element_type=jnp.float32)]
  transfers between devices with their start and end apart: 30 -> 30, of which waited for: 20 -> 15; matrix products, arithmetic and copies ran while one was open for 13% -> 15% of each run, Pallas kernels for 0% -> 0%
where the time goes in v1:
time: 114 us; the launch traced here: 113 us
  waiting for transfers between devices  58.4 us (51%)
  starting transfers between devices  31.5 us (28%)
  matrix products  14.7 us (13%)
  local copies, waits for them, and re-layouts  5.32 us (5%)
  other arithmetic  2.7 us (2%)
    ppermute x30, waiting for transfers between devices, exchange(): return lax.ppermute(block, AXES, perm)  58.4 us
    ppermute x30, starting transfers between devices, exchange(): return lax.ppermute(block, AXES, perm)  31.5 us
    dot_general x6, matrix products, product(): jnp.dot(hidden[j], w_down[:, lo:hi], preferred_element_type=jnp.float32)  5.08 us
    dot_general x6, matrix products, products(): jnp.dot(rows, w_up[lo:hi], preferred_element_type=jnp.float32)  4.9 us
    dot_general x6, matrix products, products(): jnp.dot(rows, w_gate[lo:hi], preferred_element_type=jnp.float32)  4.76 us
    unnamed x12, local copies, waits for them, and re-layouts  3.25 us
  transfers between devices with their start and end apart: 30, of which 15 were waited for; matrix products, arithmetic and copies ran while one was open for 15% of the time, Pallas kernels for 0%

profile of v1, /device:TPU:0, one launch (start us, length us, event | category | flops | bytes accessed | tf_op | source)
XLA Modules:
  0.0 113.3 jit_solution(15904310240886414860)
XLA Ops:
  0.0 0.9 slice_bitcast_fusion
  0.9 2.9 %collective-permute-start.8 = (bf16[1,1,1,1,16,2560]{5,4,3,2,1,0:T(8,128)(2,1)S(1)}, bf16[1,1,1,1,16,2560]{5,4,3,2,1,0:T(8,128)(2,1)S(1)}, u32[]{:S(2)}, u32[]{:S(2)}) collective-permute-start(bf16[1,1,1,1,16,2560]{5,4,3,2,1,0:T(8,128)(2,1)S(1)} %slice_bitcast_fusion), channel_id=1, source_target_pairs={{0,1},{1,0},{2,6},{3,7},{4,5},{5,4},{6,2},{7,3},{8,9},{9,8},{10,14... | collective-permute-start | bytes 245768 | tf_op jit(solution)/shard_map/ppermute | solution.py:75
  3.8 0.9 slice_bitcast_fusion.1
  4.8 1.6 %collective-permute-start.4 = (bf16[1,1,1,1,16,2304]{5,4,3,2,1,0:T(8,128)(2,1)S(1)}, bf16[1,1,1,1,16,2304]{5,4,3,2,1,0:T(8,128)(2,1)S(1)}, u32[]{:S(2)}, u32[]{:S(2)}) collective-permute-start(bf16[1,1,1,1,16,2304]{5,4,3,2,1,0:T(8,128)(2,1)S(1)} %get-tuple-element.37), channel_id=1, source_target_pairs={{0,8},{1,9},{2,18},{3,19},{4,12},{5,13},{6,22},{7,23},{8,0},{9,1},... | collective-permute-start | bytes 221192 | tf_op jit(solution)/shard_map/ppermute | solution.py:75
  9.5 2.4 %collective-permute-start.5 = (bf16[1,2,1,1,16,2304]{5,4,3,2,1,0:T(8,128)(2,1)S(1)}, bf16[1,2,1,1,16,2304]{5,4,3,2,1,0:T(8,128)(2,1)S(1)}, u32[]{:S(2)}, u32[]{:S(2)}) collective-permute-start(bf16[1,2,1,1,16,2304]{5,4,3,2,1,0:T(8,128)(2,1)S(1)} %pad_maximum_fusion.12), channel_id=1, source_target_pairs={{0,16},{1,17},{2,10},{3,11},{4,20},{5,21},{6,14},{7,15},{8,24},{9,... | collective-permute-start | bytes 442376 | tf_op jit(solution)/shard_map/ppermute | solution.py:75
  11.9 3.8 %collective-permute-done = bf16[1,1,1,1,16,2432]{5,4,3,2,1,0:T(8,128)(2,1)S(1)} collective-permute-done((bf16[1,1,1,1,16,2432]{5,4,3,2,1,0:T(8,128)(2,1)S(1)}, bf16[1,1,1,1,16,2432]{5,4,3,2,1,0:T(8,128)(2,1)S(1)}, u32[]{:S(2)}, u32[]{:S(2)}) %collective-permute-start) | collective-permute-done | bytes 77856 | tf_op jit(solution)/shard_map/ppermute | solution.py:75
  15.9 2.1 %collective-permute-start.6 = (bf16[2,2,1,1,16,2304]{5,4,3,2,1,0:T(8,128)(2,1)S(1)}, bf16[2,2,1,1,16,2304]{5,4,3,2,1,0:T(8,128)(2,1)S(1)}, u32[]{:S(2)}, u32[]{:S(2)}) collective-permute-start(bf16[2,2,1,1,16,2304]{5,4,3,2,1,0:T(8,128)(2,1)S(1)} %pad_maximum_fusion.8), channel_id=1, source_target_pairs={{0,1},{1,0},{2,6},{3,7},{4,5},{5,4},{6,2},{7,3},{8,9},{9,8},{10,14... | collective-permute-start | bytes 884744 | tf_op jit(solution)/shard_map/ppermute | solution.py:75
  18.0 4.1 %collective-permute-done.1 = bf16[1,2,1,1,16,2432]{5,4,3,2,1,0:T(8,128)(2,1)S(1)} collective-permute-done((bf16[1,2,1,1,16,2432]{5,4,3,2,1,0:T(8,128)(2,1)S(1)}, bf16[1,2,1,1,16,2432]{5,4,3,2,1,0:T(8,128)(2,1)S(1)}, u32[]{:S(2)}, u32[]{:S(2)}) %collective-permute-start.1) | collective-permute-done | bytes 155680 | tf_op jit(solution)/shard_map/ppermute | solution.py:75
  23.1 5.3 %collective-permute-done.6 = bf16[2,2,1,1,16,2304]{5,4,3,2,1,0:T(8,128)(2,1)S(1)} collective-permute-done((bf16[2,2,1,1,16,2304]{5,4,3,2,1,0:T(8,128)(2,1)S(1)}, bf16[2,2,1,1,16,2304]{5,4,3,2,1,0:T(8,128)(2,1)S(1)}, u32[]{:S(2)}, u32[]{:S(2)}) %collective-permute-start.6) | collective-permute-done | bytes 294944 | tf_op jit(solution)/shard_map/ppermute | solution.py:75
  29.2 0.9 collective-permute-start.3
  30.1 4.1 %collective-permute-done.10 = bf16[1,2,1,2,16,2560]{5,4,3,2,1,0:T(8,128)(2,1)S(1)} collective-permute-done((bf16[1,2,1,2,16,2560]{5,4,3,2,1,0:T(8,128)(2,1)S(1)}, bf16[1,2,1,2,16,2560]{5,4,3,2,1,0:T(8,128)(2,1)S(1)}, u32[]{:S(2)}, u32[]{:S(2)}) %collective-permute-start.10) | collective-permute-done | bytes 327712 | tf_op jit(solution)/shard_map/ppermute | solution.py:75
  34.2 1.7 %collective-permute-start.11 = (bf16[2,2,1,2,16,2560]{5,4,3,2,1,0:T(8,128)(2,1)S(1)}, bf16[2,2,1,2,16,2560]{5,4,3,2,1,0:T(8,128)(2,1)S(1)}, u32[]{:S(2)}, u32[]{:S(2)}) collective-permute-start(bf16[2,2,1,2,16,2560]{5,4,3,2,1,0:T(8,128)(2,1)S(1)} %pad_maximum_fusion.3), channel_id=1, source_target_pairs={{0,4},{1,5},{2,3},{3,2},{4,0},{5,1},{6,7},{7,6},{8,12},{9,13},{10,... | collective-permute-start | bytes 1966088 | tf_op jit(solution)/shard_map/ppermute | solution.py:75
  35.9 2.6 %collective-permute-done.7 = bf16[2,2,1,2,16,2304]{5,4,3,2,1,0:T(8,128)(2,1)S(1)} collective-permute-done((bf16[2,2,1,2,16,2304]{5,4,3,2,1,0:T(8,128)(2,1)S(1)}, bf16[2,2,1,2,16,2304]{5,4,3,2,1,0:T(8,128)(2,1)S(1)}, u32[]{:S(2)}, u32[]{:S(2)}) %collective-permute-start.7) | collective-permute-done | bytes 589856 | tf_op jit(solution)/shard_map/ppermute | solution.py:75
  38.7 8.9 %collective-permute-done.3 = bf16[1,2,2,2,16,2432]{5,4,3,2,1,0:T(8,128)(2,1)S(1)} collective-permute-done((bf16[1,2,2,2,16,2432]{5,4,3,2,1,0:T(8,128)(2,1)S(1)}, bf16[1,2,2,2,16,2432]{5,4,3,2,1,0:T(8,128)(2,1)S(1)}, u32[]{:S(2)}, u32[]{:S(2)}) %collective-permute-start.3) | collective-permute-done | bytes 622624 | tf_op jit(solution)/shard_map/ppermute | solution.py:75
  55.9 0.8 multiply_convert_fusion.1
  57.3 1.2 %slice-done.3 = s8[3145728]{0:T(1024)(128)(4,1)S(1)} async-done(((s8[7340032]{0:T(1024)(128)(4,1)}), s8[3145728]{0:T(1024)(128)(4,1)S(1)}, s32[]{:S(2)}) %slice-start.3) | async-done | bytes 3145752
  58.5 0.9 fusion
  59.5 0.9 fusion.1
  63.5 0.9 add_convert_fusion.1
  64.4 1.6 %collective-permute-start.16 = (bf16[2,2,1,2,16,2560]{5,4,3,2,1,0:T(8,128)(2,1)S(1)}, bf16[2,2,1,2,16,2560]{5,4,3,2,1,0:T(8,128)(2,1)S(1)}, u32[]{:S(2)}, u32[]{:S(2)}) collective-permute-start(bf16[2,2,1,2,16,2560]{5,4,3,2,1,0:T(8,128)(2,1)S(1)} %slice.199), channel_id=1, source_target_pairs={{0,4},{1,5},{2,3},{3,2},{4,0},{5,1},{6,7},{7,6},{8,12},{9,13},{10,... | collective-permute-start | bytes 1966088 | tf_op jit(solution)/shard_map/ppermute | solution.py:75
  66.0 0.9 add_convert_fusion
  69.0 6.0 %collective-permute-done.16 = bf16[2,2,1,2,16,2560]{5,4,3,2,1,0:T(8,128)(2,1)S(1)} collective-permute-done((bf16[2,2,1,2,16,2560]{5,4,3,2,1,0:T(8,128)(2,1)S(1)}, bf16[2,2,1,2,16,2560]{5,4,3,2,1,0:T(8,128)(2,1)S(1)}, u32[]{:S(2)}, u32[]{:S(2)}) %collective-permute-start.16) | collective-permute-done | bytes 655392 | tf_op jit(solution)/shard_map/ppermute | solution.py:75
  75.2 2.1 %collective-permute-start.19 = (bf16[2,2,1,1,16,2560]{5,4,3,2,1,0:T(8,128)(2,1)S(1)}, bf16[2,2,1,1,16,2560]{5,4,3,2,1,0:T(8,128)(2,1)S(1)}, u32[]{:S(2)}, u32[]{:S(2)}) collective-permute-start(bf16[2,2,1,1,16,2560]{5,4,3,2,1,0:T(8,128)(2,1)S(1)} %slice.203), channel_id=1, source_target_pairs={{0,1},{1,0},{2,6},{3,7},{4,5},{5,4},{6,2},{7,3},{8,9},{9,8},{10,14... | collective-permute-start | bytes 983048 | tf_op jit(solution)/shard_map/ppermute | solution.py:75
  77.3 6.2 %collective-permute-done.21 = bf16[2,2,1,2,16,2048]{5,4,3,2,1,0:T(8,128)(2,1)S(1)} collective-permute-done((bf16[2,2,1,2,16,2048]{5,4,3,2,1,0:T(8,128)(2,1)S(1)}, bf16[2,2,1,2,16,2048]{5,4,3,2,1,0:T(8,128)(2,1)S(1)}, u32[]{:S(2)}, u32[]{:S(2)}) %collective-permute-start.21) | collective-permute-done | bytes 524320 | tf_op jit(solution)/shard_map/ppermute | solution.py:75
  83.7 2.3 %collective-permute-start.24 = (bf16[2,2,1,1,16,2048]{5,4,3,2,1,0:T(8,128)(2,1)S(1)}, bf16[2,2,1,1,16,2048]{5,4,3,2,1,0:T(8,128)(2,1)S(1)}, u32[]{:S(2)}, u32[]{:S(2)}) collective-permute-start(bf16[2,2,1,1,16,2048]{5,4,3,2,1,0:T(8,128)(2,1)S(1)} %slice.213), channel_id=1, source_target_pairs={{0,1},{1,0},{2,6},{3,7},{4,5},{5,4},{6,2},{7,3},{8,9},{9,8},{10,14... | collective-permute-start | bytes 786440 | tf_op jit(solution)/shard_map/ppermute | solution.py:75
  87.0 5.4 %collective-permute-done.24 = bf16[2,2,1,1,16,2048]{5,4,3,2,1,0:T(8,128)(2,1)S(1)} collective-permute-done((bf16[2,2,1,1,16,2048]{5,4,3,2,1,0:T(8,128)(2,1)S(1)}, bf16[2,2,1,1,16,2048]{5,4,3,2,1,0:T(8,128)(2,1)S(1)}, u32[]{:S(2)}, u32[]{:S(2)}) %collective-permute-start.24) | collective-permute-done | bytes 262176 | tf_op jit(solution)/shard_map/ppermute | solution.py:75
  92.6 4.8 %collective-permute-start.22 = (bf16[2,1,1,1,16,2560]{5,4,3,2,1,0:T(8,128)(2,1)S(1)}, bf16[2,1,1,1,16,2560]{5,4,3,2,1,0:T(8,128)(2,1)S(1)}, u32[]{:S(2)}, u32[]{:S(2)}) collective-permute-start(bf16[2,1,1,1,16,2560]{5,4,3,2,1,0:T(8,128)(2,1)S(1)} %slice.209), channel_id=1, source_target_pairs={{0,8},{1,9},{2,18},{3,19},{4,12},{5,13},{6,22},{7,23},{8,0},{9,1},... | collective-permute-start | bytes 491528 | tf_op jit(solution)/shard_map/ppermute | solution.py:75
  97.5 5.4 %collective-permute-done.22 = bf16[2,1,1,1,16,2560]{5,4,3,2,1,0:T(8,128)(2,1)S(1)} collective-permute-done((bf16[2,1,1,1,16,2560]{5,4,3,2,1,0:T(8,128)(2,1)S(1)}, bf16[2,1,1,1,16,2560]{5,4,3,2,1,0:T(8,128)(2,1)S(1)}, u32[]{:S(2)}, u32[]{:S(2)}) %collective-permute-start.22) | collective-permute-done | bytes 163872 | tf_op jit(solution)/shard_map/ppermute | solution.py:75
  103.1 1.4 %collective-permute-start.29 = (bf16[1,1,1,1,16,2048]{5,4,3,2,1,0:T(8,128)(2,1)S(1)}, bf16[1,1,1,1,16,2048]{5,4,3,2,1,0:T(8,128)(2,1)S(1)}, u32[]{:S(2)}, u32[]{:S(2)}) collective-permute-start(bf16[1,1,1,1,16,2048]{5,4,3,2,1,0:T(8,128)(2,1)S(1)} %slice.223), channel_id=1, source_target_pairs={{0,8},{1,9},{2,18},{3,19},{4,12},{5,13},{6,22},{7,23},{8,0},{9,1},... | collective-permute-start | bytes 196616 | tf_op jit(solution)/shard_map/ppermute | solution.py:75
  104.5 2.2 %collective-permute-start.25 = (bf16[1,1,1,1,16,2560]{5,4,3,2,1,0:T(8,128)(2,1)S(1)}, bf16[1,1,1,1,16,2560]{5,4,3,2,1,0:T(8,128)(2,1)S(1)}, u32[]{:S(2)}, u32[]{:S(2)}) collective-permute-start(bf16[1,1,1,1,16,2560]{5,4,3,2,1,0:T(8,128)(2,1)S(1)} %slice.215), channel_id=1, source_target_pairs={{0,16},{1,17},{2,10},{3,11},{4,20},{5,21},{6,14},{7,15},{8,24},{9,... | collective-permute-start | bytes 245768 | tf_op jit(solution)/shard_map/ppermute | solution.py:75
  107.5 3.2 %collective-permute-done.25 = bf16[1,1,1,1,16,2560]{5,4,3,2,1,0:T(8,128)(2,1)S(1)} collective-permute-done((bf16[1,1,1,1,16,2560]{5,4,3,2,1,0:T(8,128)(2,1)S(1)}, bf16[1,1,1,1,16,2560]{5,4,3,2,1,0:T(8,128)(2,1)S(1)}, u32[]{:S(2)}, u32[]{:S(2)}) %collective-permute-start.25) | collective-permute-done | bytes 81952 | tf_op jit(solution)/shard_map/ppermute | solution.py:75
  110.8 1.8 %collective-permute-done.28 = bf16[1,1,1,1,16,2560]{5,4,3,2,1,0:T(8,128)(2,1)S(1)} collective-permute-done((bf16[1,1,1,1,16,2560]{5,4,3,2,1,0:T(8,128)(2,1)S(1)}, bf16[1,1,1,1,16,2560]{5,4,3,2,1,0:T(8,128)(2,1)S(1)}, u32[]{:S(2)}, u32[]{:S(2)}) %collective-permute-start.28) | collective-permute-done | bytes 81952 | tf_op jit(solution)/shard_map/ppermute | solution.py:75
  (105 shorter events, 22.8 us)
Async XLA Ops:
  0.9 14.9 %collective-permute-start.8 = (bf16[1,1,1,1,16,2560]{5,4,3,2,1,0:T(8,128)(2,1)S(1)}, bf16[1,1,1,1,16,2560]{5,4,3,2,1,0:T(8,128)(2,1)S(1)}, u32[]{:S(2)}, u32[]{:S(2)}) collective-permute-start(bf16[1,1,1,1,16,2560]{5,4,3,2,1,0:T(8,128)(2,1)S(1)} %slice_bitcast_fusion), channel_id=1, source_target_pairs={{0,1},{1,0},{2,6},{3,7},{4,5},{5,4},{6,2},{7,3},{8,9},{9,8},{10,14... | collective-permute-start | bytes 245768 | tf_op jit(solution)/shard_map/ppermute | solution.py:75
  4.8 4.7 %collective-permute-start.4 = (bf16[1,1,1,1,16,2304]{5,4,3,2,1,0:T(8,128)(2,1)S(1)}, bf16[1,1,1,1,16,2304]{5,4,3,2,1,0:T(8,128)(2,1)S(1)}, u32[]{:S(2)}, u32[]{:S(2)}) collective-permute-start(bf16[1,1,1,1,16,2304]{5,4,3,2,1,0:T(8,128)(2,1)S(1)} %get-tuple-element.37), channel_id=1, source_target_pairs={{0,8},{1,9},{2,18},{3,19},{4,12},{5,13},{6,22},{7,23},{8,0},{9,1},... | collective-permute-start | bytes 221192 | tf_op jit(solution)/shard_map/ppermute | solution.py:75
  8.1 7.5 %collective-permute-start = (bf16[1,1,1,1,16,2432]{5,4,3,2,1,0:T(8,128)(2,1)S(1)}, bf16[1,1,1,1,16,2432]{5,4,3,2,1,0:T(8,128)(2,1)S(1)}, u32[]{:S(2)}, u32[]{:S(2)}) collective-permute-start(bf16[1,1,1,1,16,2432]{5,4,3,2,1,0:T(8,128)(2,1)S(1)} %maximum_bitcast_fusion), channel_id=1, source_target_pairs={{0,8},{1,9},{2,18},{3,19},{4,12},{5,13},{6,22},{7,23},{8,0},{9,1},... | collective-permute-start | bytes 233480 | tf_op jit(solution)/shard_map/ppermute | solution.py:75
  9.5 6.4 %collective-permute-start.5 = (bf16[1,2,1,1,16,2304]{5,4,3,2,1,0:T(8,128)(2,1)S(1)}, bf16[1,2,1,1,16,2304]{5,4,3,2,1,0:T(8,128)(2,1)S(1)}, u32[]{:S(2)}, u32[]{:S(2)}) collective-permute-start(bf16[1,2,1,1,16,2304]{5,4,3,2,1,0:T(8,128)(2,1)S(1)} %pad_maximum_fusion.12), channel_id=1, source_target_pairs={{0,16},{1,17},{2,10},{3,11},{4,20},{5,21},{6,14},{7,15},{8,24},{9,... | collective-permute-start | bytes 442376 | tf_op jit(solution)/shard_map/ppermute | solution.py:75
  15.7 6.4 %collective-permute-start.1 = (bf16[1,2,1,1,16,2432]{5,4,3,2,1,0:T(8,128)(2,1)S(1)}, bf16[1,2,1,1,16,2432]{5,4,3,2,1,0:T(8,128)(2,1)S(1)}, u32[]{:S(2)}, u32[]{:S(2)}) collective-permute-start(bf16[1,2,1,1,16,2432]{5,4,3,2,1,0:T(8,128)(2,1)S(1)} %pad_maximum_fusion.11), channel_id=1, source_target_pairs={{0,1},{1,0},{2,6},{3,7},{4,5},{5,4},{6,2},{7,3},{8,9},{9,8},{10,14... | collective-permute-start | bytes 466952 | tf_op jit(solution)/shard_map/ppermute | solution.py:75
  15.8 6.8 %collective-permute-start.9 = (bf16[1,1,1,2,16,2560]{5,4,3,2,1,0:T(8,128)(2,1)S(1)}, bf16[1,1,1,2,16,2560]{5,4,3,2,1,0:T(8,128)(2,1)S(1)}, u32[]{:S(2)}, u32[]{:S(2)}) collective-permute-start(bf16[1,1,1,2,16,2560]{5,4,3,2,1,0:T(8,128)(2,1)S(1)} %pad_maximum_fusion.10), channel_id=1, source_target_pairs={{0,8},{1,9},{2,18},{3,19},{4,12},{5,13},{6,22},{7,23},{8,0},{9,1},... | collective-permute-start | bytes 491528 | tf_op jit(solution)/shard_map/ppermute | solution.py:75
  15.9 12.5 %collective-permute-start.6 = (bf16[2,2,1,1,16,2304]{5,4,3,2,1,0:T(8,128)(2,1)S(1)}, bf16[2,2,1,1,16,2304]{5,4,3,2,1,0:T(8,128)(2,1)S(1)}, u32[]{:S(2)}, u32[]{:S(2)}) collective-permute-start(bf16[2,2,1,1,16,2304]{5,4,3,2,1,0:T(8,128)(2,1)S(1)} %pad_maximum_fusion.8), channel_id=1, source_target_pairs={{0,1},{1,0},{2,6},{3,7},{4,5},{5,4},{6,2},{7,3},{8,9},{9,8},{10,14... | collective-permute-start | bytes 884744 | tf_op jit(solution)/shard_map/ppermute | solution.py:75
  22.2 7.0 %collective-permute-start.2 = (bf16[1,2,1,2,16,2432]{5,4,3,2,1,0:T(8,128)(2,1)S(1)}, bf16[1,2,1,2,16,2432]{5,4,3,2,1,0:T(8,128)(2,1)S(1)}, u32[]{:S(2)}, u32[]{:S(2)}) collective-permute-start(bf16[1,2,1,2,16,2432]{5,4,3,2,1,0:T(8,128)(2,1)S(1)} %pad_maximum_fusion.7), channel_id=1, source_target_pairs={{0,4},{1,5},{2,3},{3,2},{4,0},{5,1},{6,7},{7,6},{8,12},{9,13},{10,... | collective-permute-start | bytes 933896 | tf_op jit(solution)/shard_map/ppermute | solution.py:75
  22.6 25.2 %copy-start = (bf16[1,7168,512]{2,1,0:T(8,128)(2,1)S(1)}, bf16[1,7168,512]{2,1,0:T(8,128)(2,1)}, u32[]{:S(2)}) copy-start(bf16[1,7168,512]{2,1,0:T(8,128)(2,1)} %param.10) | copy-start | bytes 22020100
  22.7 11.5 %collective-permute-start.10 = (bf16[1,2,1,2,16,2560]{5,4,3,2,1,0:T(8,128)(2,1)S(1)}, bf16[1,2,1,2,16,2560]{5,4,3,2,1,0:T(8,128)(2,1)S(1)}, u32[]{:S(2)}, u32[]{:S(2)}) collective-permute-start(bf16[1,2,1,2,16,2560]{5,4,3,2,1,0:T(8,128)(2,1)S(1)} %pad_maximum_fusion.6), channel_id=1, source_target_pairs={{0,16},{1,17},{2,10},{3,11},{4,20},{5,21},{6,14},{7,15},{8,24},{9,... | collective-permute-start | bytes 983048 | tf_op jit(solution)/shard_map/ppermute | solution.py:75
  28.4 20.1 %slice-start = ((s8[7340032]{0:T(1024)(128)(4,1)}), s8[4194304]{0:T(1024)(128)(4,1)S(1)}, s32[]{:S(2)}) async-start(s8[7340032]{0:T(1024)(128)(4,1)} %bitcast.99), calls=%async_computation | async-start | bytes 8388608
  28.5 9.9 %collective-permute-start.7 = (bf16[2,2,1,2,16,2304]{5,4,3,2,1,0:T(8,128)(2,1)S(1)}, bf16[2,2,1,2,16,2304]{5,4,3,2,1,0:T(8,128)(2,1)S(1)}, u32[]{:S(2)}, u32[]{:S(2)}) collective-permute-start(bf16[2,2,1,2,16,2304]{5,4,3,2,1,0:T(8,128)(2,1)S(1)} %pad_maximum_fusion.5), channel_id=1, source_target_pairs={{0,4},{1,5},{2,3},{3,2},{4,0},{5,1},{6,7},{7,6},{8,12},{9,13},{10,... | collective-permute-start | bytes 1769480 | tf_op jit(solution)/shard_map/ppermute | solution.py:75
  29.2 18.3 %collective-permute-start.3 = (bf16[1,2,2,2,16,2432]{5,4,3,2,1,0:T(8,128)(2,1)S(1)}, bf16[1,2,2,2,16,2432]{5,4,3,2,1,0:T(8,128)(2,1)S(1)}, u32[]{:S(2)}, u32[]{:S(2)}) collective-permute-start(bf16[1,2,2,2,16,2432]{5,4,3,2,1,0:T(8,128)(2,1)S(1)} %pad_maximum_fusion.4), channel_id=1, source_target_pairs={{0,16},{1,17},{2,10},{3,11},{4,20},{5,21},{6,14},{7,15},{8,24},{9,... | collective-permute-start | bytes 1867784 | tf_op jit(solution)/shard_map/ppermute | solution.py:75
  34.2 15.1 %collective-permute-start.11 = (bf16[2,2,1,2,16,2560]{5,4,3,2,1,0:T(8,128)(2,1)S(1)}, bf16[2,2,1,2,16,2560]{5,4,3,2,1,0:T(8,128)(2,1)S(1)}, u32[]{:S(2)}, u32[]{:S(2)}) collective-permute-start(bf16[2,2,1,2,16,2560]{5,4,3,2,1,0:T(8,128)(2,1)S(1)} %pad_maximum_fusion.3), channel_id=1, source_target_pairs={{0,4},{1,5},{2,3},{3,2},{4,0},{5,1},{6,7},{7,6},{8,12},{9,13},{10,... | collective-permute-start | bytes 1966088 | tf_op jit(solution)/shard_map/ppermute | solution.py:75
  38.6 16.5 %collective-permute-start.13 = (bf16[256,2304]{1,0:T(8,128)(2,1)S(1)}, bf16[256,2304]{1,0:T(8,128)(2,1)S(1)}, u32[]{:S(2)}, u32[]{:S(2)}) collective-permute-start(bf16[256,2304]{1,0:T(8,128)(2,1)S(1)} %bitcast.92), channel_id=1, source_target_pairs={{0,2},{1,3},{2,0},{3,1},{4,6},{5,7},{6,4},{7,5},{8,10},{9,11},{10,... | collective-permute-start | bytes 3538952 | tf_op jit(solution)/shard_map/ppermute | solution.py:75
  47.7 4.0 %collective-permute-start.12 = (bf16[256,2432]{1,0:T(8,128)(2,1)S(1)}, bf16[256,2432]{1,0:T(8,128)(2,1)S(1)}, u32[]{:S(2)}, u32[]{:S(2)}) collective-permute-start(bf16[256,2432]{1,0:T(8,128)(2,1)S(1)} %bitcast.81), channel_id=1, source_target_pairs={{0,2},{1,3},{2,0},{3,1},{4,6},{5,7},{6,4},{7,5},{8,10},{9,11},{10,... | collective-permute-start | bytes 3735560 | tf_op jit(solution)/shard_map/ppermute | solution.py:75
  49.5 3.9 %collective-permute-start.14 = (bf16[256,2560]{1,0:T(8,128)(2,1)S(1)}, bf16[256,2560]{1,0:T(8,128)(2,1)S(1)}, u32[]{:S(2)}, u32[]{:S(2)}) collective-permute-start(bf16[256,2560]{1,0:T(8,128)(2,1)S(1)} %bitcast.85), channel_id=1, source_target_pairs={{0,2},{1,3},{2,0},{3,1},{4,6},{5,7},{6,4},{7,5},{8,10},{9,11},{10,... | collective-permute-start | bytes 3932168 | tf_op jit(solution)/shard_map/ppermute | solution.py:75
  59.4 4.1 %collective-permute-start.15 = (bf16[256,2560]{1,0:T(8,128)(2,1)S(1)}, bf16[256,2560]{1,0:T(8,128)(2,1)S(1)}, u32[]{:S(2)}, u32[]{:S(2)}) collective-permute-start(bf16[256,2560]{1,0:T(8,128)(2,1)S(1)} %fusion), channel_id=1, source_target_pairs={{0,2},{1,3},{2,0},{3,1},{4,6},{5,7},{6,4},{7,5},{8,10},{9,11},{10,... | collective-permute-start | bytes 3932168 | tf_op jit(solution)/shard_map/ppermute | solution.py:75
  60.4 5.6 %collective-permute-start.18 = (bf16[256,2560]{1,0:T(8,128)(2,1)S(1)}, bf16[256,2560]{1,0:T(8,128)(2,1)S(1)}, u32[]{:S(2)}, u32[]{:S(2)}) collective-permute-start(bf16[256,2560]{1,0:T(8,128)(2,1)S(1)} %fusion.1), channel_id=1, source_target_pairs={{0,2},{1,3},{2,0},{3,1},{4,6},{5,7},{6,4},{7,5},{8,10},{9,11},{10,... | collective-permute-start | bytes 3932168 | tf_op jit(solution)/shard_map/ppermute | solution.py:75
  62.5 4.4 %collective-permute-start.17 = (bf16[256,2048]{1,0:T(8,128)(2,1)S(1)}, bf16[256,2048]{1,0:T(8,128)(2,1)S(1)}, u32[]{:S(2)}, u32[]{:S(2)}) collective-permute-start(bf16[256,2048]{1,0:T(8,128)(2,1)S(1)} %multiply_convert_fusion), channel_id=1, source_target_pairs={{0,2},{1,3},{2,0},{3,1},{4,6},{5,7},{6,4},{7,5},{8,10},{9,11},{10,... | collective-permute-start | bytes 3145736 | tf_op jit(solution)/shard_map/ppermute | solution.py:75
  64.4 10.7 %collective-permute-start.16 = (bf16[2,2,1,2,16,2560]{5,4,3,2,1,0:T(8,128)(2,1)S(1)}, bf16[2,2,1,2,16,2560]{5,4,3,2,1,0:T(8,128)(2,1)S(1)}, u32[]{:S(2)}, u32[]{:S(2)}) collective-permute-start(bf16[2,2,1,2,16,2560]{5,4,3,2,1,0:T(8,128)(2,1)S(1)} %slice.199), channel_id=1, source_target_pairs={{0,4},{1,5},{2,3},{3,2},{4,0},{5,1},{6,7},{7,6},{8,12},{9,13},{10,... | collective-permute-start | bytes 1966088 | tf_op jit(solution)/shard_map/ppermute | solution.py:75
  67.8 15.7 %collective-permute-start.21 = (bf16[2,2,1,2,16,2048]{5,4,3,2,1,0:T(8,128)(2,1)S(1)}, bf16[2,2,1,2,16,2048]{5,4,3,2,1,0:T(8,128)(2,1)S(1)}, u32[]{:S(2)}, u32[]{:S(2)}) collective-permute-start(bf16[2,2,1,2,16,2048]{5,4,3,2,1,0:T(8,128)(2,1)S(1)} %slice.207), channel_id=1, source_target_pairs={{0,4},{1,5},{2,3},{3,2},{4,0},{5,1},{6,7},{7,6},{8,12},{9,13},{10,... | collective-permute-start | bytes 1572872 | tf_op jit(solution)/shard_map/ppermute | solution.py:75
  68.3 17.7 %collective-permute-start.20 = (bf16[2,1,2,2,16,2560]{5,4,3,2,1,0:T(8,128)(2,1)S(1)}, bf16[2,1,2,2,16,2560]{5,4,3,2,1,0:T(8,128)(2,1)S(1)}, u32[]{:S(2)}, u32[]{:S(2)}) collective-permute-start(bf16[2,1,2,2,16,2560]{5,4,3,2,1,0:T(8,128)(2,1)S(1)} %slice.205), channel_id=1, source_target_pairs={{0,8},{1,9},{2,18},{3,19},{4,12},{5,13},{6,22},{7,23},{8,0},{9,1},... | collective-permute-start | bytes 1966088 | tf_op jit(solution)/shard_map/ppermute | solution.py:75
  75.2 11.7 %collective-permute-start.19 = (bf16[2,2,1,1,16,2560]{5,4,3,2,1,0:T(8,128)(2,1)S(1)}, bf16[2,2,1,1,16,2560]{5,4,3,2,1,0:T(8,128)(2,1)S(1)}, u32[]{:S(2)}, u32[]{:S(2)}) collective-permute-start(bf16[2,2,1,1,16,2560]{5,4,3,2,1,0:T(8,128)(2,1)S(1)} %slice.203), channel_id=1, source_target_pairs={{0,1},{1,0},{2,6},{3,7},{4,5},{5,4},{6,2},{7,3},{8,9},{9,8},{10,14... | collective-permute-start | bytes 983048 | tf_op jit(solution)/shard_map/ppermute | solution.py:75
  83.7 8.7 %collective-permute-start.24 = (bf16[2,2,1,1,16,2048]{5,4,3,2,1,0:T(8,128)(2,1)S(1)}, bf16[2,2,1,1,16,2048]{5,4,3,2,1,0:T(8,128)(2,1)S(1)}, u32[]{:S(2)}, u32[]{:S(2)}) collective-permute-start(bf16[2,2,1,1,16,2048]{5,4,3,2,1,0:T(8,128)(2,1)S(1)} %slice.213), channel_id=1, source_target_pairs={{0,1},{1,0},{2,6},{3,7},{4,5},{5,4},{6,2},{7,3},{8,9},{9,8},{10,14... | collective-permute-start | bytes 786440 | tf_op jit(solution)/shard_map/ppermute | solution.py:75
  86.2 11.1 %collective-permute-start.23 = (bf16[2,1,1,2,16,2560]{5,4,3,2,1,0:T(8,128)(2,1)S(1)}, bf16[2,1,1,2,16,2560]{5,4,3,2,1,0:T(8,128)(2,1)S(1)}, u32[]{:S(2)}, u32[]{:S(2)}) collective-permute-start(bf16[2,1,1,2,16,2560]{5,4,3,2,1,0:T(8,128)(2,1)S(1)} %slice.211), channel_id=1, source_target_pairs={{0,4},{1,5},{2,3},{3,2},{4,0},{5,1},{6,7},{7,6},{8,12},{9,13},{10,... | collective-permute-start | bytes 983048 | tf_op jit(solution)/shard_map/ppermute | solution.py:75
  92.5 10.5 %collective-permute-start.27 = (bf16[1,2,1,1,16,2048]{5,4,3,2,1,0:T(8,128)(2,1)S(1)}, bf16[1,2,1,1,16,2048]{5,4,3,2,1,0:T(8,128)(2,1)S(1)}, u32[]{:S(2)}, u32[]{:S(2)}) collective-permute-start(bf16[1,2,1,1,16,2048]{5,4,3,2,1,0:T(8,128)(2,1)S(1)} %slice.219), channel_id=1, source_target_pairs={{0,16},{1,17},{2,10},{3,11},{4,20},{5,21},{6,14},{7,15},{8,24},{9,... | collective-permute-start | bytes 393224 | tf_op jit(solution)/shard_map/ppermute | solution.py:75
  92.6 10.4 %collective-permute-start.22 = (bf16[2,1,1,1,16,2560]{5,4,3,2,1,0:T(8,128)(2,1)S(1)}, bf16[2,1,1,1,16,2560]{5,4,3,2,1,0:T(8,128)(2,1)S(1)}, u32[]{:S(2)}, u32[]{:S(2)}) collective-permute-start(bf16[2,1,1,1,16,2560]{5,4,3,2,1,0:T(8,128)(2,1)S(1)} %slice.209), channel_id=1, source_target_pairs={{0,8},{1,9},{2,18},{3,19},{4,12},{5,13},{6,22},{7,23},{8,0},{9,1},... | collective-permute-start | bytes 491528 | tf_op jit(solution)/shard_map/ppermute | solution.py:75
  97.5 9.2 %collective-permute-start.26 = (bf16[2,1,1,1,16,2560]{5,4,3,2,1,0:T(8,128)(2,1)S(1)}, bf16[2,1,1,1,16,2560]{5,4,3,2,1,0:T(8,128)(2,1)S(1)}, u32[]{:S(2)}, u32[]{:S(2)}) collective-permute-start(bf16[2,1,1,1,16,2560]{5,4,3,2,1,0:T(8,128)(2,1)S(1)} %slice.217), channel_id=1, source_target_pairs={{0,1},{1,0},{2,6},{3,7},{4,5},{5,4},{6,2},{7,3},{8,9},{9,8},{10,14... | collective-permute-start | bytes 491528 | tf_op jit(solution)/shard_map/ppermute | solution.py:75
  103.1 7.6 %collective-permute-start.29 = (bf16[1,1,1,1,16,2048]{5,4,3,2,1,0:T(8,128)(2,1)S(1)}, bf16[1,1,1,1,16,2048]{5,4,3,2,1,0:T(8,128)(2,1)S(1)}, u32[]{:S(2)}, u32[]{:S(2)}) collective-permute-start(bf16[1,1,1,1,16,2048]{5,4,3,2,1,0:T(8,128)(2,1)S(1)} %slice.223), channel_id=1, source_target_pairs={{0,8},{1,9},{2,18},{3,19},{4,12},{5,13},{6,22},{7,23},{8,0},{9,1},... | collective-permute-start | bytes 196616 | tf_op jit(solution)/shard_map/ppermute | solution.py:75
  104.5 6.2 %collective-permute-start.25 = (bf16[1,1,1,1,16,2560]{5,4,3,2,1,0:T(8,128)(2,1)S(1)}, bf16[1,1,1,1,16,2560]{5,4,3,2,1,0:T(8,128)(2,1)S(1)}, u32[]{:S(2)}, u32[]{:S(2)}) collective-permute-start(bf16[1,1,1,1,16,2560]{5,4,3,2,1,0:T(8,128)(2,1)S(1)} %slice.215), channel_id=1, source_target_pairs={{0,16},{1,17},{2,10},{3,11},{4,20},{5,21},{6,14},{7,15},{8,24},{9,... | collective-permute-start | bytes 245768 | tf_op jit(solution)/shard_map/ppermute | solution.py:75
  106.7 5.8 %collective-permute-start.28 = (bf16[1,1,1,1,16,2560]{5,4,3,2,1,0:T(8,128)(2,1)S(1)}, bf16[1,1,1,1,16,2560]{5,4,3,2,1,0:T(8,128)(2,1)S(1)}, u32[]{:S(2)}, u32[]{:S(2)}) collective-permute-start(bf16[1,1,1,1,16,2560]{5,4,3,2,1,0:T(8,128)(2,1)S(1)} %slice.221), channel_id=1, source_target_pairs={{0,16},{1,17},{2,10},{3,11},{4,20},{5,21},{6,14},{7,15},{8,24},{9,... | collective-permute-start | bytes 245768 | tf_op jit(solution)/shard_map/ppermute | solution.py:75
  (3 other events, 14.8 us)

commit v2 on v1

--- a/solution.py
+++ b/solution.py
@@ -77,17 +77,17 @@
 
 STEPS = ("far", "near", "late", "early")
 GATHER = (
-    (18, ("near", "far", "early", "late")),
-    (20, ("early", "near", "far", "late")),
-    (18, ("near", "early", "late", "far")),
+    (22, ("near", "far", "early", "late")),
+    (16, ("near", "early", "far", "late")),
+    (18, ("far", "early", "late", "near")),
 )
 SCATTER = (
-    (20, ("late", "early", "near", "far")),
-    (20, ("near", "late", "early", "far")),
-    (16, ("late", "early", "far", "near")),
+    (19, ("late", "early", "far", "near")),
+    (18, ("near", "late", "early", "far")),
+    (19, ("late", "early", "near", "far")),
 )
-GATHER_TURNS = (10, 11, 12, 10, 11, 12, 12, 10, 11, 12, 10, 11, 10, 10, 10, 11, 11, 12, 12, 11, 12)
-SCATTER_TURNS = (0, 1, 2, 0, 2, 1, 0, 2, 1, 0, 2, 1, 0, 2, 1)
+GATHER_TURNS = (10, 1, 12, 10, 11, 2, 10, 11, 12, 10, 12, 11, 10, 10, 10, 12, 11, 11, 12, 11, 12)
+SCATTER_TURNS = (0, 11, 2, 0, 2, 0, 1, 2, 0, 1, 2, 0, 1, 2, 11)
 PACKED = 2
 
 

time: 114 us -> 112 us (0.982)
  waiting for transfers between devices: 58.4 us -> 40.6 us
  starting transfers between devices: 31.5 us -> 45.6 us
  matrix products: 14.7 us -> 16.8 us
    ppermute x30, waiting for transfers between devices: 58.4 us -> 40.6 us  [exchange(): return lax.ppermute(block, AXES, perm)]
    ppermute x30, starting transfers between devices: 31.5 us -> 45.6 us  [exchange(): return lax.ppermute(block, AXES, perm)]
    dot_general x6, matrix products: 4.76 us -> 6.73 us  [products(): jnp.dot(rows, w_gate[lo:hi], preferred_element_type=jnp.float32)]
  transfers between devices with their start and end apart: 30 -> 30, of which waited for: 15 -> 14; matrix products, arithmetic and copies ran while one was open for 15% -> 17% of each run, Pallas kernels for 0% -> 0%
where the time goes in v2:
time: 112 us
  starting transfers between devices  45.6 us (41%)
  waiting for transfers between devices  40.6 us (36%)
  matrix products  16.8 us (15%)
  local copies, waits for them, and re-layouts  5.9 us (5%)
  other arithmetic  2.67 us (2%)
    ppermute x30, starting transfers between devices, exchange(): return lax.ppermute(block, AXES, perm)  45.6 us
    ppermute x30, waiting for transfers between devices, exchange(): return lax.ppermute(block, AXES, perm)  40.6 us
    dot_general x6, matrix products, products(): jnp.dot(rows, w_gate[lo:hi], preferred_element_type=jnp.float32)  6.73 us
    dot_general x6, matrix products, product(): jnp.dot(hidden[j], w_down[:, lo:hi], preferred_element_type=jnp.float32)  5.23 us
    dot_general x6, matrix products, products(): jnp.dot(rows, w_up[lo:hi], preferred_element_type=jnp.float32)  4.87 us
    unnamed x12, local copies, waits for them, and re-layouts  3.02 us
  transfers between devices with their start and end apart: 30, of which 14 were waited for; matrix products, arithmetic and copies ran while one was open for 17% of the time, Pallas kernels for 0%

profile of v2, /device:TPU:0, one launch (start us, length us, event | category | flops | bytes accessed | tf_op | source)
XLA Modules:
  0.0 112.1 jit_solution(3191180041926079183)
XLA Ops:
  0.8 3.0 %collective-permute-start.1 = (bf16[1,1,1,1,16,2048]{5,4,3,2,1,0:T(8,128)(2,1)S(1)}, bf16[1,1,1,1,16,2048]{5,4,3,2,1,0:T(8,128)(2,1)S(1)}, u32[]{:S(2)}, u32[]{:S(2)}) collective-permute-start(bf16[1,1,1,1,16,2048]{5,4,3,2,1,0:T(8,128)(2,1)S(1)} %slice_bitcast_fusion.1), channel_id=1, source_target_pairs={{0,8},{1,9},{2,18},{3,19},{4,12},{5,13},{6,22},{7,23},{8,0},{9,1},... | collective-permute-start | bytes 196616 | tf_op jit(solution)/shard_map/ppermute | solution.py:75
  6.5 2.7 %collective-permute-start = (bf16[1,1,1,1,16,2432]{5,4,3,2,1,0:T(8,128)(2,1)S(1)}, bf16[1,1,1,1,16,2432]{5,4,3,2,1,0:T(8,128)(2,1)S(1)}, u32[]{:S(2)}, u32[]{:S(2)}) collective-permute-start(bf16[1,1,1,1,16,2432]{5,4,3,2,1,0:T(8,128)(2,1)S(1)} %maximum_bitcast_fusion), channel_id=1, source_target_pairs={{0,16},{1,17},{2,10},{3,11},{4,20},{5,21},{6,14},{7,15},{8,24},{9,... | collective-permute-start | bytes 233480 | tf_op jit(solution)/shard_map/ppermute | solution.py:75
  10.5 1.6 %collective-permute-start.9 = (bf16[1,2,1,1,16,2048]{5,4,3,2,1,0:T(8,128)(2,1)S(1)}, bf16[1,2,1,1,16,2048]{5,4,3,2,1,0:T(8,128)(2,1)S(1)}, u32[]{:S(2)}, u32[]{:S(2)}) collective-permute-start(bf16[1,2,1,1,16,2048]{5,4,3,2,1,0:T(8,128)(2,1)S(1)} %pad_maximum_fusion.12), channel_id=1, source_target_pairs={{0,1},{1,0},{2,6},{3,7},{4,5},{5,4},{6,2},{7,3},{8,9},{9,8},{10,14... | collective-permute-start | bytes 393224 | tf_op jit(solution)/shard_map/ppermute | solution.py:75
  12.3 1.9 %collective-permute-start.2 = (bf16[2,1,1,1,16,2432]{5,4,3,2,1,0:T(8,128)(2,1)S(1)}, bf16[2,1,1,1,16,2432]{5,4,3,2,1,0:T(8,128)(2,1)S(1)}, u32[]{:S(2)}, u32[]{:S(2)}) collective-permute-start(bf16[2,1,1,1,16,2432]{5,4,3,2,1,0:T(8,128)(2,1)S(1)} %pad_maximum_fusion.11), channel_id=1, source_target_pairs={{0,1},{1,0},{2,6},{3,7},{4,5},{5,4},{6,2},{7,3},{8,9},{9,8},{10,14... | collective-permute-start | bytes 466952 | tf_op jit(solution)/shard_map/ppermute | solution.py:75
  14.2 1.2 %collective-permute-done.5 = bf16[1,1,1,1,16,2816]{5,4,3,2,1,0:T(8,128)(2,1)S(1)} collective-permute-done((bf16[1,1,1,1,16,2816]{5,4,3,2,1,0:T(8,128)(2,1)S(1)}, bf16[1,1,1,1,16,2816]{5,4,3,2,1,0:T(8,128)(2,1)S(1)}, u32[]{:S(2)}, u32[]{:S(2)}) %collective-permute-start.5) | collective-permute-done | bytes 90144 | tf_op jit(solution)/shard_map/ppermute | solution.py:75
  15.4 1.3 %collective-permute-start.6 = (bf16[1,2,1,1,16,2816]{5,4,3,2,1,0:T(8,128)(2,1)S(1)}, bf16[1,2,1,1,16,2816]{5,4,3,2,1,0:T(8,128)(2,1)S(1)}, u32[]{:S(2)}, u32[]{:S(2)}) collective-permute-start(bf16[1,2,1,1,16,2816]{5,4,3,2,1,0:T(8,128)(2,1)S(1)} %pad_maximum_fusion.10), channel_id=1, source_target_pairs={{0,16},{1,17},{2,10},{3,11},{4,20},{5,21},{6,14},{7,15},{8,24},{9,... | collective-permute-start | bytes 540680 | tf_op jit(solution)/shard_map/ppermute | solution.py:75
  16.8 1.8 %collective-permute-start.10 = (bf16[1,2,1,2,16,2048]{5,4,3,2,1,0:T(8,128)(2,1)S(1)}, bf16[1,2,1,2,16,2048]{5,4,3,2,1,0:T(8,128)(2,1)S(1)}, u32[]{:S(2)}, u32[]{:S(2)}) collective-permute-start(bf16[1,2,1,2,16,2048]{5,4,3,2,1,0:T(8,128)(2,1)S(1)} %pad_maximum_fusion.8), channel_id=1, source_target_pairs={{0,16},{1,17},{2,10},{3,11},{4,20},{5,21},{6,14},{7,15},{8,24},{9,... | collective-permute-start | bytes 786440 | tf_op jit(solution)/shard_map/ppermute | solution.py:75
  18.6 1.6 %collective-permute-start.3 = (bf16[2,1,1,2,16,2432]{5,4,3,2,1,0:T(8,128)(2,1)S(1)}, bf16[2,1,1,2,16,2432]{5,4,3,2,1,0:T(8,128)(2,1)S(1)}, u32[]{:S(2)}, u32[]{:S(2)}) collective-permute-start(bf16[2,1,1,2,16,2432]{5,4,3,2,1,0:T(8,128)(2,1)S(1)} %pad_maximum_fusion.7), channel_id=1, source_target_pairs={{0,4},{1,5},{2,3},{3,2},{4,0},{5,1},{6,7},{7,6},{8,12},{9,13},{10,... | collective-permute-start | bytes 933896 | tf_op jit(solution)/shard_map/ppermute | solution.py:75
  20.1 3.7 %collective-permute-done.6 = bf16[1,2,1,1,16,2816]{5,4,3,2,1,0:T(8,128)(2,1)S(1)} collective-permute-done((bf16[1,2,1,1,16,2816]{5,4,3,2,1,0:T(8,128)(2,1)S(1)}, bf16[1,2,1,1,16,2816]{5,4,3,2,1,0:T(8,128)(2,1)S(1)}, u32[]{:S(2)}, u32[]{:S(2)}) %collective-permute-start.6) | collective-permute-done | bytes 180256 | tf_op jit(solution)/shard_map/ppermute | solution.py:75
  23.9 1.6 %collective-permute-start.7 = (bf16[2,2,1,1,16,2816]{5,4,3,2,1,0:T(8,128)(2,1)S(1)}, bf16[2,2,1,1,16,2816]{5,4,3,2,1,0:T(8,128)(2,1)S(1)}, u32[]{:S(2)}, u32[]{:S(2)}) collective-permute-start(bf16[2,2,1,1,16,2816]{5,4,3,2,1,0:T(8,128)(2,1)S(1)} %pad_maximum_fusion.6), channel_id=1, source_target_pairs={{0,1},{1,0},{2,6},{3,7},{4,5},{5,4},{6,2},{7,3},{8,9},{9,8},{10,14... | collective-permute-start | bytes 1081352 | tf_op jit(solution)/shard_map/ppermute | solution.py:75
  25.4 4.2 %collective-permute-done.10 = bf16[1,2,1,2,16,2048]{5,4,3,2,1,0:T(8,128)(2,1)S(1)} collective-permute-done((bf16[1,2,1,2,16,2048]{5,4,3,2,1,0:T(8,128)(2,1)S(1)}, bf16[1,2,1,2,16,2048]{5,4,3,2,1,0:T(8,128)(2,1)S(1)}, u32[]{:S(2)}, u32[]{:S(2)}) %collective-permute-start.10) | collective-permute-done | bytes 262176 | tf_op jit(solution)/shard_map/ppermute | solution.py:75
  29.7 1.6 %collective-permute-start.11 = (bf16[2,2,1,2,16,2048]{5,4,3,2,1,0:T(8,128)(2,1)S(1)}, bf16[2,2,1,2,16,2048]{5,4,3,2,1,0:T(8,128)(2,1)S(1)}, u32[]{:S(2)}, u32[]{:S(2)}) collective-permute-start(bf16[2,2,1,2,16,2048]{5,4,3,2,1,0:T(8,128)(2,1)S(1)} %pad_maximum_fusion.5), channel_id=1, source_target_pairs={{0,4},{1,5},{2,3},{3,2},{4,0},{5,1},{6,7},{7,6},{8,12},{9,13},{10,... | collective-permute-start | bytes 1572872 | tf_op jit(solution)/shard_map/ppermute | solution.py:75
  31.4 7.0 %collective-permute-start.4 = (bf16[2,1,2,2,16,2432]{5,4,3,2,1,0:T(8,128)(2,1)S(1)}, bf16[2,1,2,2,16,2432]{5,4,3,2,1,0:T(8,128)(2,1)S(1)}, u32[]{:S(2)}, u32[]{:S(2)}) collective-permute-start(bf16[2,1,2,2,16,2432]{5,4,3,2,1,0:T(8,128)(2,1)S(1)} %pad_maximum_fusion.4), channel_id=1, source_target_pairs={{0,8},{1,9},{2,18},{3,19},{4,12},{5,13},{6,22},{7,23},{8,0},{9,1},... | collective-permute-start | bytes 1867784 | tf_op jit(solution)/shard_map/ppermute | solution.py:75
  39.9 2.7 %fusion.32 = f32[256,512]{1,0:T(8,128)S(1)} fusion(bf16[256,2048]{1,0:T(8,128)(2,1)S(1)} %bitcast.97, bf16[1,7168,512]{2,1,0:T(8,128)(2,1)} %param.9), kind=kOutput, calls=%fused_computation.41 | convolution fusion | flops 536870912 | bytes 3670016 | tf_op jit(solution)/shard_map/dot_general | solution.py:115
  42.6 6.8 %collective-permute-done.4 = bf16[2,1,2,2,16,2432]{5,4,3,2,1,0:T(8,128)(2,1)S(1)} collective-permute-done((bf16[2,1,2,2,16,2432]{5,4,3,2,1,0:T(8,128)(2,1)S(1)}, bf16[2,1,2,2,16,2432]{5,4,3,2,1,0:T(8,128)(2,1)S(1)}, u32[]{:S(2)}, u32[]{:S(2)}) %collective-permute-start.4) | collective-permute-done | bytes 622624 | tf_op jit(solution)/shard_map/ppermute | solution.py:75
  57.3 1.2 %slice-done.3 = s8[3145728]{0:T(1024)(128)(4,1)S(1)} async-done(((s8[7340032]{0:T(1024)(128)(4,1)}), s8[3145728]{0:T(1024)(128)(4,1)S(1)}, s32[]{:S(2)}) %slice-start.3) | async-done | bytes 3145752
  64.6 1.6 %collective-permute-start.16 = (bf16[2,2,1,2,16,2432]{5,4,3,2,1,0:T(8,128)(2,1)S(1)}, bf16[2,2,1,2,16,2432]{5,4,3,2,1,0:T(8,128)(2,1)S(1)}, u32[]{:S(2)}, u32[]{:S(2)}) collective-permute-start(bf16[2,2,1,2,16,2432]{5,4,3,2,1,0:T(8,128)(2,1)S(1)} %slice.199), channel_id=1, source_target_pairs={{0,4},{1,5},{2,3},{3,2},{4,0},{5,1},{6,7},{7,6},{8,12},{9,13},{10,... | collective-permute-start | bytes 1867784 | tf_op jit(solution)/shard_map/ppermute | solution.py:75
  67.1 2.3 %collective-permute-start.23 = (bf16[2,1,2,2,16,2304]{5,4,3,2,1,0:T(8,128)(2,1)S(1)}, bf16[2,1,2,2,16,2304]{5,4,3,2,1,0:T(8,128)(2,1)S(1)}, u32[]{:S(2)}, u32[]{:S(2)}) collective-permute-start(bf16[2,1,2,2,16,2304]{5,4,3,2,1,0:T(8,128)(2,1)S(1)} %slice.211), channel_id=1, source_target_pairs={{0,8},{1,9},{2,18},{3,19},{4,12},{5,13},{6,22},{7,23},{8,0},{9,1},... | collective-permute-start | bytes 1769480 | tf_op jit(solution)/shard_map/ppermute | solution.py:75
  69.4 1.1 add_convert_fusion
  70.9 4.1 %collective-permute-done.16 = bf16[2,2,1,2,16,2432]{5,4,3,2,1,0:T(8,128)(2,1)S(1)} collective-permute-done((bf16[2,2,1,2,16,2432]{5,4,3,2,1,0:T(8,128)(2,1)S(1)}, bf16[2,2,1,2,16,2432]{5,4,3,2,1,0:T(8,128)(2,1)S(1)}, u32[]{:S(2)}, u32[]{:S(2)}) %collective-permute-start.16) | collective-permute-done | bytes 622624 | tf_op jit(solution)/shard_map/ppermute | solution.py:75
  75.1 3.7 %collective-permute-start.19 = (bf16[2,2,1,1,16,2432]{5,4,3,2,1,0:T(8,128)(2,1)S(1)}, bf16[2,2,1,1,16,2432]{5,4,3,2,1,0:T(8,128)(2,1)S(1)}, u32[]{:S(2)}, u32[]{:S(2)}) collective-permute-start(bf16[2,2,1,1,16,2432]{5,4,3,2,1,0:T(8,128)(2,1)S(1)} %slice.203), channel_id=1, source_target_pairs={{0,1},{1,0},{2,6},{3,7},{4,5},{5,4},{6,2},{7,3},{8,9},{9,8},{10,14... | collective-permute-start | bytes 933896 | tf_op jit(solution)/shard_map/ppermute | solution.py:75
  78.8 5.4 %collective-permute-done.20 = bf16[2,2,1,2,16,2432]{5,4,3,2,1,0:T(8,128)(2,1)S(1)} collective-permute-done((bf16[2,2,1,2,16,2432]{5,4,3,2,1,0:T(8,128)(2,1)S(1)}, bf16[2,2,1,2,16,2432]{5,4,3,2,1,0:T(8,128)(2,1)S(1)}, u32[]{:S(2)}, u32[]{:S(2)}) %collective-permute-start.20) | collective-permute-done | bytes 622624 | tf_op jit(solution)/shard_map/ppermute | solution.py:75
  84.4 4.5 %collective-permute-start.22 = (bf16[2,2,1,1,16,2432]{5,4,3,2,1,0:T(8,128)(2,1)S(1)}, bf16[2,2,1,1,16,2432]{5,4,3,2,1,0:T(8,128)(2,1)S(1)}, u32[]{:S(2)}, u32[]{:S(2)}) collective-permute-start(bf16[2,2,1,1,16,2432]{5,4,3,2,1,0:T(8,128)(2,1)S(1)} %slice.209), channel_id=1, source_target_pairs={{0,1},{1,0},{2,6},{3,7},{4,5},{5,4},{6,2},{7,3},{8,9},{9,8},{10,14... | collective-permute-start | bytes 933896 | tf_op jit(solution)/shard_map/ppermute | solution.py:75
  89.2 1.6 %collective-permute-start.26 = (bf16[2,1,1,2,16,2304]{5,4,3,2,1,0:T(8,128)(2,1)S(1)}, bf16[2,1,1,2,16,2304]{5,4,3,2,1,0:T(8,128)(2,1)S(1)}, u32[]{:S(2)}, u32[]{:S(2)}) collective-permute-start(bf16[2,1,1,2,16,2304]{5,4,3,2,1,0:T(8,128)(2,1)S(1)} %slice.217), channel_id=1, source_target_pairs={{0,4},{1,5},{2,3},{3,2},{4,0},{5,1},{6,7},{7,6},{8,12},{9,13},{10,... | collective-permute-start | bytes 884744 | tf_op jit(solution)/shard_map/ppermute | solution.py:75
  90.8 5.2 %collective-permute-done.22 = bf16[2,2,1,1,16,2432]{5,4,3,2,1,0:T(8,128)(2,1)S(1)} collective-permute-done((bf16[2,2,1,1,16,2432]{5,4,3,2,1,0:T(8,128)(2,1)S(1)}, bf16[2,2,1,1,16,2432]{5,4,3,2,1,0:T(8,128)(2,1)S(1)}, u32[]{:S(2)}, u32[]{:S(2)}) %collective-permute-start.22) | collective-permute-done | bytes 311328 | tf_op jit(solution)/shard_map/ppermute | solution.py:75
  96.1 1.1 %collective-permute-start.25 = (bf16[2,1,1,1,16,2432]{5,4,3,2,1,0:T(8,128)(2,1)S(1)}, bf16[2,1,1,1,16,2432]{5,4,3,2,1,0:T(8,128)(2,1)S(1)}, u32[]{:S(2)}, u32[]{:S(2)}) collective-permute-start(bf16[2,1,1,1,16,2432]{5,4,3,2,1,0:T(8,128)(2,1)S(1)} %slice.215), channel_id=1, source_target_pairs={{0,8},{1,9},{2,18},{3,19},{4,12},{5,13},{6,22},{7,23},{8,0},{9,1},... | collective-permute-start | bytes 466952 | tf_op jit(solution)/shard_map/ppermute | solution.py:75
  97.2 2.5 %collective-permute-done.21 = bf16[1,2,1,1,16,2432]{5,4,3,2,1,0:T(8,128)(2,1)S(1)} collective-permute-done((bf16[1,2,1,1,16,2432]{5,4,3,2,1,0:T(8,128)(2,1)S(1)}, bf16[1,2,1,1,16,2432]{5,4,3,2,1,0:T(8,128)(2,1)S(1)}, u32[]{:S(2)}, u32[]{:S(2)}) %collective-permute-start.21) | collective-permute-done | bytes 155680 | tf_op jit(solution)/shard_map/ppermute | solution.py:75
  100.9 1.9 %collective-permute-done.25 = bf16[2,1,1,1,16,2432]{5,4,3,2,1,0:T(8,128)(2,1)S(1)} collective-permute-done((bf16[2,1,1,1,16,2432]{5,4,3,2,1,0:T(8,128)(2,1)S(1)}, bf16[2,1,1,1,16,2432]{5,4,3,2,1,0:T(8,128)(2,1)S(1)}, u32[]{:S(2)}, u32[]{:S(2)}) %collective-permute-start.25) | collective-permute-done | bytes 155680 | tf_op jit(solution)/shard_map/ppermute | solution.py:75
  102.8 1.9 %collective-permute-done.24 = bf16[1,1,1,1,16,2432]{5,4,3,2,1,0:T(8,128)(2,1)S(1)} collective-permute-done((bf16[1,1,1,1,16,2432]{5,4,3,2,1,0:T(8,128)(2,1)S(1)}, bf16[1,1,1,1,16,2432]{5,4,3,2,1,0:T(8,128)(2,1)S(1)}, u32[]{:S(2)}, u32[]{:S(2)}) %collective-permute-start.24) | collective-permute-done | bytes 77856 | tf_op jit(solution)/shard_map/ppermute | solution.py:75
  104.8 1.1 collective-permute-start.29
  105.9 2.1 %collective-permute-start.28 = (bf16[1,1,1,1,16,2304]{5,4,3,2,1,0:T(8,128)(2,1)S(1)}, bf16[1,1,1,1,16,2304]{5,4,3,2,1,0:T(8,128)(2,1)S(1)}, u32[]{:S(2)}, u32[]{:S(2)}) collective-permute-start(bf16[1,1,1,1,16,2304]{5,4,3,2,1,0:T(8,128)(2,1)S(1)} %slice.221), channel_id=1, source_target_pairs={{0,16},{1,17},{2,10},{3,11},{4,20},{5,21},{6,14},{7,15},{8,24},{9,... | collective-permute-start | bytes 221192 | tf_op jit(solution)/shard_map/ppermute | solution.py:75
  108.1 2.5 %collective-permute-done.29 = bf16[1,1,1,1,16,2432]{5,4,3,2,1,0:T(8,128)(2,1)S(1)} collective-permute-done((bf16[1,1,1,1,16,2432]{5,4,3,2,1,0:T(8,128)(2,1)S(1)}, bf16[1,1,1,1,16,2432]{5,4,3,2,1,0:T(8,128)(2,1)S(1)}, u32[]{:S(2)}, u32[]{:S(2)}) %collective-permute-start.29) | collective-permute-done | bytes 77856 | tf_op jit(solution)/shard_map/ppermute | solution.py:75
  (106 shorter events, 25.4 us)
Async XLA Ops:
  0.8 9.7 %collective-permute-start.1 = (bf16[1,1,1,1,16,2048]{5,4,3,2,1,0:T(8,128)(2,1)S(1)}, bf16[1,1,1,1,16,2048]{5,4,3,2,1,0:T(8,128)(2,1)S(1)}, u32[]{:S(2)}, u32[]{:S(2)}) collective-permute-start(bf16[1,1,1,1,16,2048]{5,4,3,2,1,0:T(8,128)(2,1)S(1)} %slice_bitcast_fusion.1), channel_id=1, source_target_pairs={{0,8},{1,9},{2,18},{3,19},{4,12},{5,13},{6,22},{7,23},{8,0},{9,1},... | collective-permute-start | bytes 196616 | tf_op jit(solution)/shard_map/ppermute | solution.py:75
  6.5 5.7 %collective-permute-start = (bf16[1,1,1,1,16,2432]{5,4,3,2,1,0:T(8,128)(2,1)S(1)}, bf16[1,1,1,1,16,2432]{5,4,3,2,1,0:T(8,128)(2,1)S(1)}, u32[]{:S(2)}, u32[]{:S(2)}) collective-permute-start(bf16[1,1,1,1,16,2432]{5,4,3,2,1,0:T(8,128)(2,1)S(1)} %maximum_bitcast_fusion), channel_id=1, source_target_pairs={{0,16},{1,17},{2,10},{3,11},{4,20},{5,21},{6,14},{7,15},{8,24},{9,... | collective-permute-start | bytes 233480 | tf_op jit(solution)/shard_map/ppermute | solution.py:75
  10.0 5.4 %collective-permute-start.5 = (bf16[1,1,1,1,16,2816]{5,4,3,2,1,0:T(8,128)(2,1)S(1)}, bf16[1,1,1,1,16,2816]{5,4,3,2,1,0:T(8,128)(2,1)S(1)}, u32[]{:S(2)}, u32[]{:S(2)}) collective-permute-start(bf16[1,1,1,1,16,2816]{5,4,3,2,1,0:T(8,128)(2,1)S(1)} %slice_bitcast_fusion), channel_id=1, source_target_pairs={{0,8},{1,9},{2,18},{3,19},{4,12},{5,13},{6,22},{7,23},{8,0},{9,1},... | collective-permute-start | bytes 270344 | tf_op jit(solution)/shard_map/ppermute | solution.py:75
  10.5 6.2 %collective-permute-start.9 = (bf16[1,2,1,1,16,2048]{5,4,3,2,1,0:T(8,128)(2,1)S(1)}, bf16[1,2,1,1,16,2048]{5,4,3,2,1,0:T(8,128)(2,1)S(1)}, u32[]{:S(2)}, u32[]{:S(2)}) collective-permute-start(bf16[1,2,1,1,16,2048]{5,4,3,2,1,0:T(8,128)(2,1)S(1)} %pad_maximum_fusion.12), channel_id=1, source_target_pairs={{0,1},{1,0},{2,6},{3,7},{4,5},{5,4},{6,2},{7,3},{8,9},{9,8},{10,14... | collective-permute-start | bytes 393224 | tf_op jit(solution)/shard_map/ppermute | solution.py:75
  12.3 6.3 %collective-permute-start.2 = (bf16[2,1,1,1,16,2432]{5,4,3,2,1,0:T(8,128)(2,1)S(1)}, bf16[2,1,1,1,16,2432]{5,4,3,2,1,0:T(8,128)(2,1)S(1)}, u32[]{:S(2)}, u32[]{:S(2)}) collective-permute-start(bf16[2,1,1,1,16,2432]{5,4,3,2,1,0:T(8,128)(2,1)S(1)} %pad_maximum_fusion.11), channel_id=1, source_target_pairs={{0,1},{1,0},{2,6},{3,7},{4,5},{5,4},{6,2},{7,3},{8,9},{9,8},{10,14... | collective-permute-start | bytes 466952 | tf_op jit(solution)/shard_map/ppermute | solution.py:75
  15.4 8.4 %collective-permute-start.6 = (bf16[1,2,1,1,16,2816]{5,4,3,2,1,0:T(8,128)(2,1)S(1)}, bf16[1,2,1,1,16,2816]{5,4,3,2,1,0:T(8,128)(2,1)S(1)}, u32[]{:S(2)}, u32[]{:S(2)}) collective-permute-start(bf16[1,2,1,1,16,2816]{5,4,3,2,1,0:T(8,128)(2,1)S(1)} %pad_maximum_fusion.10), channel_id=1, source_target_pairs={{0,16},{1,17},{2,10},{3,11},{4,20},{5,21},{6,14},{7,15},{8,24},{9,... | collective-permute-start | bytes 540680 | tf_op jit(solution)/shard_map/ppermute | solution.py:75
  16.7 22.4 %copy-start = (bf16[1,7168,512]{2,1,0:T(8,128)(2,1)S(1)}, bf16[1,7168,512]{2,1,0:T(8,128)(2,1)}, u32[]{:S(2)}) copy-start(bf16[1,7168,512]{2,1,0:T(8,128)(2,1)} %param.10) | copy-start | bytes 22020100
  16.8 12.9 %collective-permute-start.10 = (bf16[1,2,1,2,16,2048]{5,4,3,2,1,0:T(8,128)(2,1)S(1)}, bf16[1,2,1,2,16,2048]{5,4,3,2,1,0:T(8,128)(2,1)S(1)}, u32[]{:S(2)}, u32[]{:S(2)}) collective-permute-start(bf16[1,2,1,2,16,2048]{5,4,3,2,1,0:T(8,128)(2,1)S(1)} %pad_maximum_fusion.8), channel_id=1, source_target_pairs={{0,16},{1,17},{2,10},{3,11},{4,20},{5,21},{6,14},{7,15},{8,24},{9,... | collective-permute-start | bytes 786440 | tf_op jit(solution)/shard_map/ppermute | solution.py:75
  18.6 12.7 %collective-permute-start.3 = (bf16[2,1,1,2,16,2432]{5,4,3,2,1,0:T(8,128)(2,1)S(1)}, bf16[2,1,1,2,16,2432]{5,4,3,2,1,0:T(8,128)(2,1)S(1)}, u32[]{:S(2)}, u32[]{:S(2)}) collective-permute-start(bf16[2,1,1,2,16,2432]{5,4,3,2,1,0:T(8,128)(2,1)S(1)} %pad_maximum_fusion.7), channel_id=1, source_target_pairs={{0,4},{1,5},{2,3},{3,2},{4,0},{5,1},{6,7},{7,6},{8,12},{9,13},{10,... | collective-permute-start | bytes 933896 | tf_op jit(solution)/shard_map/ppermute | solution.py:75
  23.9 14.5 %collective-permute-start.7 = (bf16[2,2,1,1,16,2816]{5,4,3,2,1,0:T(8,128)(2,1)S(1)}, bf16[2,2,1,1,16,2816]{5,4,3,2,1,0:T(8,128)(2,1)S(1)}, u32[]{:S(2)}, u32[]{:S(2)}) collective-permute-start(bf16[2,2,1,1,16,2816]{5,4,3,2,1,0:T(8,128)(2,1)S(1)} %pad_maximum_fusion.6), channel_id=1, source_target_pairs={{0,1},{1,0},{2,6},{3,7},{4,5},{5,4},{6,2},{7,3},{8,9},{9,8},{10,14... | collective-permute-start | bytes 1081352 | tf_op jit(solution)/shard_map/ppermute | solution.py:75
  29.7 9.2 %collective-permute-start.11 = (bf16[2,2,1,2,16,2048]{5,4,3,2,1,0:T(8,128)(2,1)S(1)}, bf16[2,2,1,2,16,2048]{5,4,3,2,1,0:T(8,128)(2,1)S(1)}, u32[]{:S(2)}, u32[]{:S(2)}) collective-permute-start(bf16[2,2,1,2,16,2048]{5,4,3,2,1,0:T(8,128)(2,1)S(1)} %pad_maximum_fusion.5), channel_id=1, source_target_pairs={{0,4},{1,5},{2,3},{3,2},{4,0},{5,1},{6,7},{7,6},{8,12},{9,13},{10,... | collective-permute-start | bytes 1572872 | tf_op jit(solution)/shard_map/ppermute | solution.py:75
  31.4 18.0 %collective-permute-start.4 = (bf16[2,1,2,2,16,2432]{5,4,3,2,1,0:T(8,128)(2,1)S(1)}, bf16[2,1,2,2,16,2432]{5,4,3,2,1,0:T(8,128)(2,1)S(1)}, u32[]{:S(2)}, u32[]{:S(2)}) collective-permute-start(bf16[2,1,2,2,16,2432]{5,4,3,2,1,0:T(8,128)(2,1)S(1)} %pad_maximum_fusion.4), channel_id=1, source_target_pairs={{0,8},{1,9},{2,18},{3,19},{4,12},{5,13},{6,22},{7,23},{8,0},{9,1},... | collective-permute-start | bytes 1867784 | tf_op jit(solution)/shard_map/ppermute | solution.py:75
  38.4 12.8 %collective-permute-start.8 = (bf16[2,2,1,2,16,2816]{5,4,3,2,1,0:T(8,128)(2,1)S(1)}, bf16[2,2,1,2,16,2816]{5,4,3,2,1,0:T(8,128)(2,1)S(1)}, u32[]{:S(2)}, u32[]{:S(2)}) collective-permute-start(bf16[2,2,1,2,16,2816]{5,4,3,2,1,0:T(8,128)(2,1)S(1)} %pad_maximum_fusion.3), channel_id=1, source_target_pairs={{0,4},{1,5},{2,3},{3,2},{4,0},{5,1},{6,7},{7,6},{8,12},{9,13},{10,... | collective-permute-start | bytes 2162696 | tf_op jit(solution)/shard_map/ppermute | solution.py:75
  39.1 12.9 %collective-permute-start.14 = (bf16[256,2048]{1,0:T(8,128)(2,1)S(1)}, bf16[256,2048]{1,0:T(8,128)(2,1)S(1)}, u32[]{:S(2)}, u32[]{:S(2)}) collective-permute-start(bf16[256,2048]{1,0:T(8,128)(2,1)S(1)} %bitcast.95), channel_id=1, source_target_pairs={{0,2},{1,3},{2,0},{3,1},{4,6},{5,7},{6,4},{7,5},{8,10},{9,11},{10,... | collective-permute-start | bytes 3145736 | tf_op jit(solution)/shard_map/ppermute | solution.py:75
  39.2 11.3 %slice-start = ((s8[7340032]{0:T(1024)(128)(4,1)}), s8[4194304]{0:T(1024)(128)(4,1)S(1)}, s32[]{:S(2)}) async-start(s8[7340032]{0:T(1024)(128)(4,1)} %bitcast.99), calls=%async_computation | async-start | bytes 8388608
  49.6 3.8 %collective-permute-start.12 = (bf16[256,2432]{1,0:T(8,128)(2,1)S(1)}, bf16[256,2432]{1,0:T(8,128)(2,1)S(1)}, u32[]{:S(2)}, u32[]{:S(2)}) collective-permute-start(bf16[256,2432]{1,0:T(8,128)(2,1)S(1)} %bitcast.85), channel_id=1, source_target_pairs={{0,2},{1,3},{2,0},{3,1},{4,6},{5,7},{6,4},{7,5},{8,10},{9,11},{10,... | collective-permute-start | bytes 3735560 | tf_op jit(solution)/shard_map/ppermute | solution.py:75
  51.4 3.7 %collective-permute-start.13 = (bf16[256,2816]{1,0:T(8,128)(2,1)S(1)}, bf16[256,2816]{1,0:T(8,128)(2,1)S(1)}, u32[]{:S(2)}, u32[]{:S(2)}) collective-permute-start(bf16[256,2816]{1,0:T(8,128)(2,1)S(1)} %bitcast.82), channel_id=1, source_target_pairs={{0,2},{1,3},{2,0},{3,1},{4,6},{5,7},{6,4},{7,5},{8,10},{9,11},{10,... | collective-permute-start | bytes 4325384 | tf_op jit(solution)/shard_map/ppermute | solution.py:75
  59.3 4.4 %collective-permute-start.15 = (bf16[256,2432]{1,0:T(8,128)(2,1)S(1)}, bf16[256,2432]{1,0:T(8,128)(2,1)S(1)}, u32[]{:S(2)}, u32[]{:S(2)}) collective-permute-start(bf16[256,2432]{1,0:T(8,128)(2,1)S(1)} %fusion), channel_id=1, source_target_pairs={{0,2},{1,3},{2,0},{3,1},{4,6},{5,7},{6,4},{7,5},{8,10},{9,11},{10,... | collective-permute-start | bytes 3735560 | tf_op jit(solution)/shard_map/ppermute | solution.py:75
  60.3 5.9 %collective-permute-start.18 = (bf16[256,2304]{1,0:T(8,128)(2,1)S(1)}, bf16[256,2304]{1,0:T(8,128)(2,1)S(1)}, u32[]{:S(2)}, u32[]{:S(2)}) collective-permute-start(bf16[256,2304]{1,0:T(8,128)(2,1)S(1)} %multiply_convert_fusion), channel_id=1, source_target_pairs={{0,2},{1,3},{2,0},{3,1},{4,6},{5,7},{6,4},{7,5},{8,10},{9,11},{10,... | collective-permute-start | bytes 3538952 | tf_op jit(solution)/shard_map/ppermute | solution.py:75
  61.6 7.8 %collective-permute-start.17 = (bf16[256,2432]{1,0:T(8,128)(2,1)S(1)}, bf16[256,2432]{1,0:T(8,128)(2,1)S(1)}, u32[]{:S(2)}, u32[]{:S(2)}) collective-permute-start(bf16[256,2432]{1,0:T(8,128)(2,1)S(1)} %fusion.1), channel_id=1, source_target_pairs={{0,2},{1,3},{2,0},{3,1},{4,6},{5,7},{6,4},{7,5},{8,10},{9,11},{10,... | collective-permute-start | bytes 3735560 | tf_op jit(solution)/shard_map/ppermute | solution.py:75
  64.6 10.3 %collective-permute-start.16 = (bf16[2,2,1,2,16,2432]{5,4,3,2,1,0:T(8,128)(2,1)S(1)}, bf16[2,2,1,2,16,2432]{5,4,3,2,1,0:T(8,128)(2,1)S(1)}, u32[]{:S(2)}, u32[]{:S(2)}) collective-permute-start(bf16[2,2,1,2,16,2432]{5,4,3,2,1,0:T(8,128)(2,1)S(1)} %slice.199), channel_id=1, source_target_pairs={{0,4},{1,5},{2,3},{3,2},{4,0},{5,1},{6,7},{7,6},{8,12},{9,13},{10,... | collective-permute-start | bytes 1867784 | tf_op jit(solution)/shard_map/ppermute | solution.py:75
  67.1 21.9 %collective-permute-start.23 = (bf16[2,1,2,2,16,2304]{5,4,3,2,1,0:T(8,128)(2,1)S(1)}, bf16[2,1,2,2,16,2304]{5,4,3,2,1,0:T(8,128)(2,1)S(1)}, u32[]{:S(2)}, u32[]{:S(2)}) collective-permute-start(bf16[2,1,2,2,16,2304]{5,4,3,2,1,0:T(8,128)(2,1)S(1)} %slice.211), channel_id=1, source_target_pairs={{0,8},{1,9},{2,18},{3,19},{4,12},{5,13},{6,22},{7,23},{8,0},{9,1},... | collective-permute-start | bytes 1769480 | tf_op jit(solution)/shard_map/ppermute | solution.py:75
  70.5 13.7 %collective-permute-start.20 = (bf16[2,2,1,2,16,2432]{5,4,3,2,1,0:T(8,128)(2,1)S(1)}, bf16[2,2,1,2,16,2432]{5,4,3,2,1,0:T(8,128)(2,1)S(1)}, u32[]{:S(2)}, u32[]{:S(2)}) collective-permute-start(bf16[2,2,1,2,16,2432]{5,4,3,2,1,0:T(8,128)(2,1)S(1)} %slice.205), channel_id=1, source_target_pairs={{0,4},{1,5},{2,3},{3,2},{4,0},{5,1},{6,7},{7,6},{8,12},{9,13},{10,... | collective-permute-start | bytes 1867784 | tf_op jit(solution)/shard_map/ppermute | solution.py:75
  75.1 13.7 %collective-permute-start.19 = (bf16[2,2,1,1,16,2432]{5,4,3,2,1,0:T(8,128)(2,1)S(1)}, bf16[2,2,1,1,16,2432]{5,4,3,2,1,0:T(8,128)(2,1)S(1)}, u32[]{:S(2)}, u32[]{:S(2)}) collective-permute-start(bf16[2,2,1,1,16,2432]{5,4,3,2,1,0:T(8,128)(2,1)S(1)} %slice.203), channel_id=1, source_target_pairs={{0,1},{1,0},{2,6},{3,7},{4,5},{5,4},{6,2},{7,3},{8,9},{9,8},{10,14... | collective-permute-start | bytes 933896 | tf_op jit(solution)/shard_map/ppermute | solution.py:75
  84.4 11.6 %collective-permute-start.22 = (bf16[2,2,1,1,16,2432]{5,4,3,2,1,0:T(8,128)(2,1)S(1)}, bf16[2,2,1,1,16,2432]{5,4,3,2,1,0:T(8,128)(2,1)S(1)}, u32[]{:S(2)}, u32[]{:S(2)}) collective-permute-start(bf16[2,2,1,1,16,2432]{5,4,3,2,1,0:T(8,128)(2,1)S(1)} %slice.209), channel_id=1, source_target_pairs={{0,1},{1,0},{2,6},{3,7},{4,5},{5,4},{6,2},{7,3},{8,9},{9,8},{10,14... | collective-permute-start | bytes 933896 | tf_op jit(solution)/shard_map/ppermute | solution.py:75
  89.1 10.6 %collective-permute-start.21 = (bf16[1,2,1,1,16,2432]{5,4,3,2,1,0:T(8,128)(2,1)S(1)}, bf16[1,2,1,1,16,2432]{5,4,3,2,1,0:T(8,128)(2,1)S(1)}, u32[]{:S(2)}, u32[]{:S(2)}) collective-permute-start(bf16[1,2,1,1,16,2432]{5,4,3,2,1,0:T(8,128)(2,1)S(1)} %slice.207), channel_id=1, source_target_pairs={{0,16},{1,17},{2,10},{3,11},{4,20},{5,21},{6,14},{7,15},{8,24},{9,... | collective-permute-start | bytes 466952 | tf_op jit(solution)/shard_map/ppermute | solution.py:75
  89.2 10.6 %collective-permute-start.26 = (bf16[2,1,1,2,16,2304]{5,4,3,2,1,0:T(8,128)(2,1)S(1)}, bf16[2,1,1,2,16,2304]{5,4,3,2,1,0:T(8,128)(2,1)S(1)}, u32[]{:S(2)}, u32[]{:S(2)}) collective-permute-start(bf16[2,1,1,2,16,2304]{5,4,3,2,1,0:T(8,128)(2,1)S(1)} %slice.217), channel_id=1, source_target_pairs={{0,4},{1,5},{2,3},{3,2},{4,0},{5,1},{6,7},{7,6},{8,12},{9,13},{10,... | collective-permute-start | bytes 884744 | tf_op jit(solution)/shard_map/ppermute | solution.py:75
  96.1 6.7 %collective-permute-start.25 = (bf16[2,1,1,1,16,2432]{5,4,3,2,1,0:T(8,128)(2,1)S(1)}, bf16[2,1,1,1,16,2432]{5,4,3,2,1,0:T(8,128)(2,1)S(1)}, u32[]{:S(2)}, u32[]{:S(2)}) collective-permute-start(bf16[2,1,1,1,16,2432]{5,4,3,2,1,0:T(8,128)(2,1)S(1)} %slice.215), channel_id=1, source_target_pairs={{0,8},{1,9},{2,18},{3,19},{4,12},{5,13},{6,22},{7,23},{8,0},{9,1},... | collective-permute-start | bytes 466952 | tf_op jit(solution)/shard_map/ppermute | solution.py:75
  99.8 5.0 %collective-permute-start.24 = (bf16[1,1,1,1,16,2432]{5,4,3,2,1,0:T(8,128)(2,1)S(1)}, bf16[1,1,1,1,16,2432]{5,4,3,2,1,0:T(8,128)(2,1)S(1)}, u32[]{:S(2)}, u32[]{:S(2)}) collective-permute-start(bf16[1,1,1,1,16,2432]{5,4,3,2,1,0:T(8,128)(2,1)S(1)} %slice.213), channel_id=1, source_target_pairs={{0,8},{1,9},{2,18},{3,19},{4,12},{5,13},{6,22},{7,23},{8,0},{9,1},... | collective-permute-start | bytes 233480 | tf_op jit(solution)/shard_map/ppermute | solution.py:75
  100.0 5.9 %collective-permute-start.27 = (bf16[2,1,1,1,16,2304]{5,4,3,2,1,0:T(8,128)(2,1)S(1)}, bf16[2,1,1,1,16,2304]{5,4,3,2,1,0:T(8,128)(2,1)S(1)}, u32[]{:S(2)}, u32[]{:S(2)}) collective-permute-start(bf16[2,1,1,1,16,2304]{5,4,3,2,1,0:T(8,128)(2,1)S(1)} %slice.219), channel_id=1, source_target_pairs={{0,1},{1,0},{2,6},{3,7},{4,5},{5,4},{6,2},{7,3},{8,9},{9,8},{10,14... | collective-permute-start | bytes 442376 | tf_op jit(solution)/shard_map/ppermute | solution.py:75
  104.8 5.8 %collective-permute-start.29 = (bf16[1,1,1,1,16,2432]{5,4,3,2,1,0:T(8,128)(2,1)S(1)}, bf16[1,1,1,1,16,2432]{5,4,3,2,1,0:T(8,128)(2,1)S(1)}, u32[]{:S(2)}, u32[]{:S(2)}) collective-permute-start(bf16[1,1,1,1,16,2432]{5,4,3,2,1,0:T(8,128)(2,1)S(1)} %slice.223), channel_id=1, source_target_pairs={{0,16},{1,17},{2,10},{3,11},{4,20},{5,21},{6,14},{7,15},{8,24},{9,... | collective-permute-start | bytes 233480 | tf_op jit(solution)/shard_map/ppermute | solution.py:75
  105.9 5.5 %collective-permute-start.28 = (bf16[1,1,1,1,16,2304]{5,4,3,2,1,0:T(8,128)(2,1)S(1)}, bf16[1,1,1,1,16,2304]{5,4,3,2,1,0:T(8,128)(2,1)S(1)}, u32[]{:S(2)}, u32[]{:S(2)}) collective-permute-start(bf16[1,1,1,1,16,2304]{5,4,3,2,1,0:T(8,128)(2,1)S(1)} %slice.221), channel_id=1, source_target_pairs={{0,16},{1,17},{2,10},{3,11},{4,20},{5,21},{6,14},{7,15},{8,24},{9,... | collective-permute-start | bytes 221192 | tf_op jit(solution)/shard_map/ppermute | solution.py:75
  (3 other events, 15.2 us)

commit v3 on v2

--- a/solution.py
+++ b/solution.py
@@ -87,8 +87,8 @@
     (19, ("late", "early", "near", "far")),
 )
 GATHER_TURNS = (10, 1, 12, 10, 11, 2, 10, 11, 12, 10, 12, 11, 10, 10, 10, 12, 11, 11, 12, 11, 12)
-SCATTER_TURNS = (0, 11, 2, 0, 2, 0, 1, 2, 0, 1, 2, 0, 1, 2, 11)
-PACKED = 2
+SCATTER_TURNS = (0, 11, 12, 0, 2, 10, 1, 2, 10, 1, 0, 2, 1, 2, 11)
+PACKED = 1
 
 
 def chunks_of(width, plan):
@@ -142,10 +142,10 @@
     return gates, ups, spread
 
 
-def scatter_rows(hidden, scale, w_down, chunks):
+def scatter_rows(hidden, w_down, chunks):
     def product(j, chunk):
         lo, hi, _ = chunk
-        return scale[j] * jnp.dot(hidden[j], w_down[:, lo:hi], preferred_element_type=jnp.float32)
+        return jnp.dot(hidden[j], w_down[:, lo:hi], preferred_element_type=jnp.float32)
 
     state = [[exchange(product(1, chunk).astype(jnp.bfloat16), "core"), None, 0] for chunk in chunks]
     before = hidden[0]
@@ -180,15 +180,14 @@
     packed = jnp.concatenate([high, weights - high], axis=1).astype(jnp.bfloat16)
     packed = jnp.pad(packed, ((0, 0), (0, -2 * experts % 128)))
     gates, ups, spread = gather_rows(tokens, packed, w_gate[0], w_up[0], chunks_of(width, GATHER))
-    hidden = [(jax.nn.silu(gate) * up).astype(jnp.bfloat16) for gate, up in zip(gates, ups)]
     me = lax.axis_index("expert")
     column = jnp.arange(spread[0].shape[1], dtype=jnp.int32)
     named = (column == me) | (column == me + experts)
-    scale = [
-        jnp.sum(jnp.where(named[None, :], rows.astype(jnp.float32), 0.0), axis=1, keepdims=True)
-        for rows in spread
-    ]
-    return scatter_rows(hidden, scale, w_down[0], chunks_of(width, SCATTER))
+    hidden = []
+    for gate, up, rows in zip(gates, ups, spread):
+        scale = jnp.sum(jnp.where(named[None, :], rows.astype(jnp.float32), 0.0), axis=1, keepdims=True)
+        hidden.append((scale * (jax.nn.silu(gate) * up)).astype(jnp.bfloat16))
+    return scatter_rows(hidden, w_down[0], chunks_of(width, SCATTER))
 
 
 def local(tokens, expert_ids, gate_values, w_gate, w_up, w_down):

time: 112 us -> 114 us (1.018)
  starting transfers between devices: 45.6 us -> 51 us
  waiting for transfers between devices: 40.6 us -> 36.2 us
    ppermute x30, starting transfers between devices: 45.6 us -> 51 us  [exchange(): return lax.ppermute(block, AXES, perm)]
    ppermute x30, waiting for transfers between devices: 40.6 us -> 36.2 us  [exchange(): return lax.ppermute(block, AXES, perm)]
    dot_general x6, matrix products: 6.73 us -> 4.79 us  [products(): jnp.dot(rows, w_gate[lo:hi], preferred_element_type=jnp.float32)]
    dot_general x6, matrix products: 4.87 us -> 6.67 us  [products(): jnp.dot(rows, w_up[lo:hi], preferred_element_type=jnp.float32)]
  transfers between devices with their start and end apart: 30 -> 30, of which waited for: 14 -> 13; matrix products, arithmetic and copies ran while one was open for 17% -> 16% of each run, Pallas kernels for 0% -> 0%
where the time goes in v3:
time: 114 us; the launch traced here: 113 us
  starting transfers between devices  51 us (45%)
  waiting for transfers between devices  36.2 us (32%)
  matrix products  16.7 us (15%)
  local copies, waits for them, and re-layouts  6.17 us (5%)
  other arithmetic  2.67 us (2%)
    ppermute x30, starting transfers between devices, exchange(): return lax.ppermute(block, AXES, perm)  51 us
    ppermute x30, waiting for transfers between devices, exchange(): return lax.ppermute(block, AXES, perm)  36.2 us
    dot_general x6, matrix products, products(): jnp.dot(rows, w_up[lo:hi], preferred_element_type=jnp.float32)  6.67 us
    dot_general x6, matrix products, product(): jnp.dot(hidden[j], w_down[:, lo:hi], preferred_element_type=jnp.float32)  5.22 us
    dot_general x6, matrix products, products(): jnp.dot(rows, w_gate[lo:hi], preferred_element_type=jnp.float32)  4.79 us
    unnamed x12, local copies, waits for them, and re-layouts  3.28 us
  transfers between devices with their start and end apart: 30, of which 13 were waited for; matrix products, arithmetic and copies ran while one was open for 16% of the time, Pallas kernels for 0%

profile of v3, /device:TPU:0, one launch (start us, length us, event | category | flops | bytes accessed | tf_op | source)
XLA Modules:
  0.0 113.3 jit_solution(5231823538496139415)
XLA Ops:
  2.6 3.1 %collective-permute-start = (bf16[1,1,1,1,16,2176]{5,4,3,2,1,0:T(8,128)(2,1)S(1)}, bf16[1,1,1,1,16,2176]{5,4,3,2,1,0:T(8,128)(2,1)S(1)}, u32[]{:S(2)}, u32[]{:S(2)}) collective-permute-start(bf16[1,1,1,1,16,2176]{5,4,3,2,1,0:T(8,128)(2,1)S(1)} %maximum_bitcast_fusion), channel_id=1, source_target_pairs={{0,8},{1,9},{2,18},{3,19},{4,12},{5,13},{6,22},{7,23},{8,0},{9,1},... | collective-permute-start | bytes 208904 | tf_op jit(solution)/shard_map/ppermute | solution.py:75
  6.5 2.6 %collective-permute-start.8 = (bf16[1,1,1,1,16,2304]{5,4,3,2,1,0:T(8,128)(2,1)S(1)}, bf16[1,1,1,1,16,2304]{5,4,3,2,1,0:T(8,128)(2,1)S(1)}, u32[]{:S(2)}, u32[]{:S(2)}) collective-permute-start(bf16[1,1,1,1,16,2304]{5,4,3,2,1,0:T(8,128)(2,1)S(1)} %slice_bitcast_fusion.1), channel_id=1, source_target_pairs={{0,16},{1,17},{2,10},{3,11},{4,20},{5,21},{6,14},{7,15},{8,24},{9,... | collective-permute-start | bytes 221192 | tf_op jit(solution)/shard_map/ppermute | solution.py:75
  10.5 1.6 %collective-permute-start.1 = (bf16[1,2,1,1,16,2176]{5,4,3,2,1,0:T(8,128)(2,1)S(1)}, bf16[1,2,1,1,16,2176]{5,4,3,2,1,0:T(8,128)(2,1)S(1)}, u32[]{:S(2)}, u32[]{:S(2)}) collective-permute-start(bf16[1,2,1,1,16,2176]{5,4,3,2,1,0:T(8,128)(2,1)S(1)} %pad_maximum_fusion.12), channel_id=1, source_target_pairs={{0,1},{1,0},{2,6},{3,7},{4,5},{5,4},{6,2},{7,3},{8,9},{9,8},{10,14... | collective-permute-start | bytes 417800 | tf_op jit(solution)/shard_map/ppermute | solution.py:75
  12.6 1.6 %collective-permute-start.9 = (bf16[2,1,1,1,16,2304]{5,4,3,2,1,0:T(8,128)(2,1)S(1)}, bf16[2,1,1,1,16,2304]{5,4,3,2,1,0:T(8,128)(2,1)S(1)}, u32[]{:S(2)}, u32[]{:S(2)}) collective-permute-start(bf16[2,1,1,1,16,2304]{5,4,3,2,1,0:T(8,128)(2,1)S(1)} %pad_maximum_fusion.11), channel_id=1, source_target_pairs={{0,1},{1,0},{2,6},{3,7},{4,5},{5,4},{6,2},{7,3},{8,9},{9,8},{10,14... | collective-permute-start | bytes 442376 | tf_op jit(solution)/shard_map/ppermute | solution.py:75
  14.2 1.2 %collective-permute-done.4 = bf16[1,1,1,1,16,2816]{5,4,3,2,1,0:T(8,128)(2,1)S(1)} collective-permute-done((bf16[1,1,1,1,16,2816]{5,4,3,2,1,0:T(8,128)(2,1)S(1)}, bf16[1,1,1,1,16,2816]{5,4,3,2,1,0:T(8,128)(2,1)S(1)}, u32[]{:S(2)}, u32[]{:S(2)}) %collective-permute-start.4) | collective-permute-done | bytes 90144 | tf_op jit(solution)/shard_map/ppermute | solution.py:75
  15.4 1.2 %collective-permute-start.5 = (bf16[1,2,1,1,16,2816]{5,4,3,2,1,0:T(8,128)(2,1)S(1)}, bf16[1,2,1,1,16,2816]{5,4,3,2,1,0:T(8,128)(2,1)S(1)}, u32[]{:S(2)}, u32[]{:S(2)}) collective-permute-start(bf16[1,2,1,1,16,2816]{5,4,3,2,1,0:T(8,128)(2,1)S(1)} %pad_maximum_fusion.10), channel_id=1, source_target_pairs={{0,16},{1,17},{2,10},{3,11},{4,20},{5,21},{6,14},{7,15},{8,24},{9,... | collective-permute-start | bytes 540680 | tf_op jit(solution)/shard_map/ppermute | solution.py:75
  16.7 1.8 %collective-permute-start.2 = (bf16[1,2,1,2,16,2176]{5,4,3,2,1,0:T(8,128)(2,1)S(1)}, bf16[1,2,1,2,16,2176]{5,4,3,2,1,0:T(8,128)(2,1)S(1)}, u32[]{:S(2)}, u32[]{:S(2)}) collective-permute-start(bf16[1,2,1,2,16,2176]{5,4,3,2,1,0:T(8,128)(2,1)S(1)} %pad_maximum_fusion.8), channel_id=1, source_target_pairs={{0,16},{1,17},{2,10},{3,11},{4,20},{5,21},{6,14},{7,15},{8,24},{9,... | collective-permute-start | bytes 835592 | tf_op jit(solution)/shard_map/ppermute | solution.py:75
  18.6 1.6 %collective-permute-start.10 = (bf16[2,1,1,2,16,2304]{5,4,3,2,1,0:T(8,128)(2,1)S(1)}, bf16[2,1,1,2,16,2304]{5,4,3,2,1,0:T(8,128)(2,1)S(1)}, u32[]{:S(2)}, u32[]{:S(2)}) collective-permute-start(bf16[2,1,1,2,16,2304]{5,4,3,2,1,0:T(8,128)(2,1)S(1)} %pad_maximum_fusion.7), channel_id=1, source_target_pairs={{0,4},{1,5},{2,3},{3,2},{4,0},{5,1},{6,7},{7,6},{8,12},{9,13},{10,... | collective-permute-start | bytes 884744 | tf_op jit(solution)/shard_map/ppermute | solution.py:75
  20.1 3.7 %collective-permute-done.5 = bf16[1,2,1,1,16,2816]{5,4,3,2,1,0:T(8,128)(2,1)S(1)} collective-permute-done((bf16[1,2,1,1,16,2816]{5,4,3,2,1,0:T(8,128)(2,1)S(1)}, bf16[1,2,1,1,16,2816]{5,4,3,2,1,0:T(8,128)(2,1)S(1)}, u32[]{:S(2)}, u32[]{:S(2)}) %collective-permute-start.5) | collective-permute-done | bytes 180256 | tf_op jit(solution)/shard_map/ppermute | solution.py:75
  23.8 1.6 %collective-permute-start.6 = (bf16[2,2,1,1,16,2816]{5,4,3,2,1,0:T(8,128)(2,1)S(1)}, bf16[2,2,1,1,16,2816]{5,4,3,2,1,0:T(8,128)(2,1)S(1)}, u32[]{:S(2)}, u32[]{:S(2)}) collective-permute-start(bf16[2,2,1,1,16,2816]{5,4,3,2,1,0:T(8,128)(2,1)S(1)} %pad_maximum_fusion.6), channel_id=1, source_target_pairs={{0,1},{1,0},{2,6},{3,7},{4,5},{5,4},{6,2},{7,3},{8,9},{9,8},{10,14... | collective-permute-start | bytes 1081352 | tf_op jit(solution)/shard_map/ppermute | solution.py:75
  25.4 4.6 %collective-permute-done.2 = bf16[1,2,1,2,16,2176]{5,4,3,2,1,0:T(8,128)(2,1)S(1)} collective-permute-done((bf16[1,2,1,2,16,2176]{5,4,3,2,1,0:T(8,128)(2,1)S(1)}, bf16[1,2,1,2,16,2176]{5,4,3,2,1,0:T(8,128)(2,1)S(1)}, u32[]{:S(2)}, u32[]{:S(2)}) %collective-permute-start.2) | collective-permute-done | bytes 278560 | tf_op jit(solution)/shard_map/ppermute | solution.py:75
  30.0 1.6 %collective-permute-start.3 = (bf16[2,2,1,2,16,2176]{5,4,3,2,1,0:T(8,128)(2,1)S(1)}, bf16[2,2,1,2,16,2176]{5,4,3,2,1,0:T(8,128)(2,1)S(1)}, u32[]{:S(2)}, u32[]{:S(2)}) collective-permute-start(bf16[2,2,1,2,16,2176]{5,4,3,2,1,0:T(8,128)(2,1)S(1)} %pad_maximum_fusion.5), channel_id=1, source_target_pairs={{0,4},{1,5},{2,3},{3,2},{4,0},{5,1},{6,7},{7,6},{8,12},{9,13},{10,... | collective-permute-start | bytes 1671176 | tf_op jit(solution)/shard_map/ppermute | solution.py:75
  31.7 6.4 %collective-permute-start.11 = (bf16[2,1,2,2,16,2304]{5,4,3,2,1,0:T(8,128)(2,1)S(1)}, bf16[2,1,2,2,16,2304]{5,4,3,2,1,0:T(8,128)(2,1)S(1)}, u32[]{:S(2)}, u32[]{:S(2)}) collective-permute-start(bf16[2,1,2,2,16,2304]{5,4,3,2,1,0:T(8,128)(2,1)S(1)} %pad_maximum_fusion.4), channel_id=1, source_target_pairs={{0,8},{1,9},{2,18},{3,19},{4,12},{5,13},{6,22},{7,23},{8,0},{9,1},... | collective-permute-start | bytes 1769480 | tf_op jit(solution)/shard_map/ppermute | solution.py:75
  40.6 2.4 %fusion.30 = f32[256,512]{1,0:T(8,128)S(1)} fusion(bf16[1,7168,512]{2,1,0:T(8,128)(2,1)} %param.10, bf16[256,2176]{1,0:T(8,128)(2,1)S(1)} %bitcast.87), kind=kOutput, calls=%fused_computation.34 | convolution fusion | flops 536870912 | bytes 3670016 | tf_op jit(solution)/shard_map/dot_general | solution.py:116
  43.0 5.7 %collective-permute-done.11 = bf16[2,1,2,2,16,2304]{5,4,3,2,1,0:T(8,128)(2,1)S(1)} collective-permute-done((bf16[2,1,2,2,16,2304]{5,4,3,2,1,0:T(8,128)(2,1)S(1)}, bf16[2,1,2,2,16,2304]{5,4,3,2,1,0:T(8,128)(2,1)S(1)}, u32[]{:S(2)}, u32[]{:S(2)}) %collective-permute-start.11) | collective-permute-done | bytes 589856 | tf_op jit(solution)/shard_map/ppermute | solution.py:75
  55.6 1.0 multiply_convert_fusion
  56.8 1.2 %slice-done.3 = s8[3145728]{0:T(1024)(128)(4,1)S(1)} async-done(((s8[7340032]{0:T(1024)(128)(4,1)}), s8[3145728]{0:T(1024)(128)(4,1)S(1)}, s32[]{:S(2)}) %slice-start.3) | async-done | bytes 3145752
  64.2 1.6 %collective-permute-start.16 = (bf16[2,2,1,2,16,2432]{5,4,3,2,1,0:T(8,128)(2,1)S(1)}, bf16[2,2,1,2,16,2432]{5,4,3,2,1,0:T(8,128)(2,1)S(1)}, u32[]{:S(2)}, u32[]{:S(2)}) collective-permute-start(bf16[2,2,1,2,16,2432]{5,4,3,2,1,0:T(8,128)(2,1)S(1)} %slice.199), channel_id=1, source_target_pairs={{0,4},{1,5},{2,3},{3,2},{4,0},{5,1},{6,7},{7,6},{8,12},{9,13},{10,... | collective-permute-start | bytes 1867784 | tf_op jit(solution)/shard_map/ppermute | solution.py:75
  66.7 3.7 %collective-permute-start.22 = (bf16[2,1,2,2,16,2304]{5,4,3,2,1,0:T(8,128)(2,1)S(1)}, bf16[2,1,2,2,16,2304]{5,4,3,2,1,0:T(8,128)(2,1)S(1)}, u32[]{:S(2)}, u32[]{:S(2)}) collective-permute-start(bf16[2,1,2,2,16,2304]{5,4,3,2,1,0:T(8,128)(2,1)S(1)} %slice.209), channel_id=1, source_target_pairs={{0,8},{1,9},{2,18},{3,19},{4,12},{5,13},{6,22},{7,23},{8,0},{9,1},... | collective-permute-start | bytes 1769480 | tf_op jit(solution)/shard_map/ppermute | solution.py:75
  72.2 2.3 %collective-permute-done.16 = bf16[2,2,1,2,16,2432]{5,4,3,2,1,0:T(8,128)(2,1)S(1)} collective-permute-done((bf16[2,2,1,2,16,2432]{5,4,3,2,1,0:T(8,128)(2,1)S(1)}, bf16[2,2,1,2,16,2432]{5,4,3,2,1,0:T(8,128)(2,1)S(1)}, u32[]{:S(2)}, u32[]{:S(2)}) %collective-permute-start.16) | collective-permute-done | bytes 622624 | tf_op jit(solution)/shard_map/ppermute | solution.py:75
  74.7 5.4 %collective-permute-start.18 = (bf16[2,2,1,1,16,2432]{5,4,3,2,1,0:T(8,128)(2,1)S(1)}, bf16[2,2,1,1,16,2432]{5,4,3,2,1,0:T(8,128)(2,1)S(1)}, u32[]{:S(2)}, u32[]{:S(2)}) collective-permute-start(bf16[2,2,1,1,16,2432]{5,4,3,2,1,0:T(8,128)(2,1)S(1)} %slice.202), channel_id=1, source_target_pairs={{0,1},{1,0},{2,6},{3,7},{4,5},{5,4},{6,2},{7,3},{8,9},{9,8},{10,14... | collective-permute-start | bytes 933896 | tf_op jit(solution)/shard_map/ppermute | solution.py:75
  80.1 3.1 %collective-permute-done.25 = bf16[2,2,1,2,16,2432]{5,4,3,2,1,0:T(8,128)(2,1)S(1)} collective-permute-done((bf16[2,2,1,2,16,2432]{5,4,3,2,1,0:T(8,128)(2,1)S(1)}, bf16[2,2,1,2,16,2432]{5,4,3,2,1,0:T(8,128)(2,1)S(1)}, u32[]{:S(2)}, u32[]{:S(2)}) %collective-permute-start.25) | collective-permute-done | bytes 622624 | tf_op jit(solution)/shard_map/ppermute | solution.py:75
  83.4 6.7 %collective-permute-start.26 = (bf16[2,2,1,1,16,2432]{5,4,3,2,1,0:T(8,128)(2,1)S(1)}, bf16[2,2,1,1,16,2432]{5,4,3,2,1,0:T(8,128)(2,1)S(1)}, u32[]{:S(2)}, u32[]{:S(2)}) collective-permute-start(bf16[2,2,1,1,16,2432]{5,4,3,2,1,0:T(8,128)(2,1)S(1)} %slice.217), channel_id=1, source_target_pairs={{0,1},{1,0},{2,6},{3,7},{4,5},{5,4},{6,2},{7,3},{8,9},{9,8},{10,14... | collective-permute-start | bytes 933896 | tf_op jit(solution)/shard_map/ppermute | solution.py:75
  90.5 1.6 %collective-permute-start.23 = (bf16[2,1,1,2,16,2304]{5,4,3,2,1,0:T(8,128)(2,1)S(1)}, bf16[2,1,1,2,16,2304]{5,4,3,2,1,0:T(8,128)(2,1)S(1)}, u32[]{:S(2)}, u32[]{:S(2)}) collective-permute-start(bf16[2,1,1,2,16,2304]{5,4,3,2,1,0:T(8,128)(2,1)S(1)} %slice.211), channel_id=1, source_target_pairs={{0,4},{1,5},{2,3},{3,2},{4,0},{5,1},{6,7},{7,6},{8,12},{9,13},{10,... | collective-permute-start | bytes 884744 | tf_op jit(solution)/shard_map/ppermute | solution.py:75
  92.1 5.1 %collective-permute-done.26 = bf16[2,2,1,1,16,2432]{5,4,3,2,1,0:T(8,128)(2,1)S(1)} collective-permute-done((bf16[2,2,1,1,16,2432]{5,4,3,2,1,0:T(8,128)(2,1)S(1)}, bf16[2,2,1,1,16,2432]{5,4,3,2,1,0:T(8,128)(2,1)S(1)}, u32[]{:S(2)}, u32[]{:S(2)}) %collective-permute-start.26) | collective-permute-done | bytes 311328 | tf_op jit(solution)/shard_map/ppermute | solution.py:75
  97.3 1.3 %collective-permute-start.27 = (bf16[2,1,1,1,16,2432]{5,4,3,2,1,0:T(8,128)(2,1)S(1)}, bf16[2,1,1,1,16,2432]{5,4,3,2,1,0:T(8,128)(2,1)S(1)}, u32[]{:S(2)}, u32[]{:S(2)}) collective-permute-start(bf16[2,1,1,1,16,2432]{5,4,3,2,1,0:T(8,128)(2,1)S(1)} %slice.219), channel_id=1, source_target_pairs={{0,8},{1,9},{2,18},{3,19},{4,12},{5,13},{6,22},{7,23},{8,0},{9,1},... | collective-permute-start | bytes 466952 | tf_op jit(solution)/shard_map/ppermute | solution.py:75
  98.5 2.2 %collective-permute-done.19 = bf16[1,2,1,1,16,2432]{5,4,3,2,1,0:T(8,128)(2,1)S(1)} collective-permute-done((bf16[1,2,1,1,16,2432]{5,4,3,2,1,0:T(8,128)(2,1)S(1)}, bf16[1,2,1,1,16,2432]{5,4,3,2,1,0:T(8,128)(2,1)S(1)}, u32[]{:S(2)}, u32[]{:S(2)}) %collective-permute-start.19) | collective-permute-done | bytes 155680 | tf_op jit(solution)/shard_map/ppermute | solution.py:75
  101.0 1.1 collective-permute-start.24
  102.1 3.6 %collective-permute-done.20 = bf16[1,1,1,1,16,2432]{5,4,3,2,1,0:T(8,128)(2,1)S(1)} collective-permute-done((bf16[1,1,1,1,16,2432]{5,4,3,2,1,0:T(8,128)(2,1)S(1)}, bf16[1,1,1,1,16,2432]{5,4,3,2,1,0:T(8,128)(2,1)S(1)}, u32[]{:S(2)}, u32[]{:S(2)}) %collective-permute-start.20) | collective-permute-done | bytes 77856 | tf_op jit(solution)/shard_map/ppermute | solution.py:75
  105.8 1.2 %collective-permute-start.29 = (bf16[1,1,1,1,16,2432]{5,4,3,2,1,0:T(8,128)(2,1)S(1)}, bf16[1,1,1,1,16,2432]{5,4,3,2,1,0:T(8,128)(2,1)S(1)}, u32[]{:S(2)}, u32[]{:S(2)}) collective-permute-start(bf16[1,1,1,1,16,2432]{5,4,3,2,1,0:T(8,128)(2,1)S(1)} %slice.223), channel_id=1, source_target_pairs={{0,16},{1,17},{2,10},{3,11},{4,20},{5,21},{6,14},{7,15},{8,24},{9,... | collective-permute-start | bytes 233480 | tf_op jit(solution)/shard_map/ppermute | solution.py:75
  107.1 2.1 %collective-permute-start.28 = (bf16[1,1,1,1,16,2304]{5,4,3,2,1,0:T(8,128)(2,1)S(1)}, bf16[1,1,1,1,16,2304]{5,4,3,2,1,0:T(8,128)(2,1)S(1)}, u32[]{:S(2)}, u32[]{:S(2)}) collective-permute-start(bf16[1,1,1,1,16,2304]{5,4,3,2,1,0:T(8,128)(2,1)S(1)} %slice.221), channel_id=1, source_target_pairs={{0,16},{1,17},{2,10},{3,11},{4,20},{5,21},{6,14},{7,15},{8,24},{9,... | collective-permute-start | bytes 221192 | tf_op jit(solution)/shard_map/ppermute | solution.py:75
  109.2 2.6 %collective-permute-done.29 = bf16[1,1,1,1,16,2432]{5,4,3,2,1,0:T(8,128)(2,1)S(1)} collective-permute-done((bf16[1,1,1,1,16,2432]{5,4,3,2,1,0:T(8,128)(2,1)S(1)}, bf16[1,1,1,1,16,2432]{5,4,3,2,1,0:T(8,128)(2,1)S(1)}, u32[]{:S(2)}, u32[]{:S(2)}) %collective-permute-start.29) | collective-permute-done | bytes 77856 | tf_op jit(solution)/shard_map/ppermute | solution.py:75
  (106 shorter events, 26.4 us)
Async XLA Ops:
  2.6 7.9 %collective-permute-start = (bf16[1,1,1,1,16,2176]{5,4,3,2,1,0:T(8,128)(2,1)S(1)}, bf16[1,1,1,1,16,2176]{5,4,3,2,1,0:T(8,128)(2,1)S(1)}, u32[]{:S(2)}, u32[]{:S(2)}) collective-permute-start(bf16[1,1,1,1,16,2176]{5,4,3,2,1,0:T(8,128)(2,1)S(1)} %maximum_bitcast_fusion), channel_id=1, source_target_pairs={{0,8},{1,9},{2,18},{3,19},{4,12},{5,13},{6,22},{7,23},{8,0},{9,1},... | collective-permute-start | bytes 208904 | tf_op jit(solution)/shard_map/ppermute | solution.py:75
  6.5 6.0 %collective-permute-start.8 = (bf16[1,1,1,1,16,2304]{5,4,3,2,1,0:T(8,128)(2,1)S(1)}, bf16[1,1,1,1,16,2304]{5,4,3,2,1,0:T(8,128)(2,1)S(1)}, u32[]{:S(2)}, u32[]{:S(2)}) collective-permute-start(bf16[1,1,1,1,16,2304]{5,4,3,2,1,0:T(8,128)(2,1)S(1)} %slice_bitcast_fusion.1), channel_id=1, source_target_pairs={{0,16},{1,17},{2,10},{3,11},{4,20},{5,21},{6,14},{7,15},{8,24},{9,... | collective-permute-start | bytes 221192 | tf_op jit(solution)/shard_map/ppermute | solution.py:75
  10.0 5.4 %collective-permute-start.4 = (bf16[1,1,1,1,16,2816]{5,4,3,2,1,0:T(8,128)(2,1)S(1)}, bf16[1,1,1,1,16,2816]{5,4,3,2,1,0:T(8,128)(2,1)S(1)}, u32[]{:S(2)}, u32[]{:S(2)}) collective-permute-start(bf16[1,1,1,1,16,2816]{5,4,3,2,1,0:T(8,128)(2,1)S(1)} %slice_bitcast_fusion), channel_id=1, source_target_pairs={{0,8},{1,9},{2,18},{3,19},{4,12},{5,13},{6,22},{7,23},{8,0},{9,1},... | collective-permute-start | bytes 270344 | tf_op jit(solution)/shard_map/ppermute | solution.py:75
  10.5 6.1 %collective-permute-start.1 = (bf16[1,2,1,1,16,2176]{5,4,3,2,1,0:T(8,128)(2,1)S(1)}, bf16[1,2,1,1,16,2176]{5,4,3,2,1,0:T(8,128)(2,1)S(1)}, u32[]{:S(2)}, u32[]{:S(2)}) collective-permute-start(bf16[1,2,1,1,16,2176]{5,4,3,2,1,0:T(8,128)(2,1)S(1)} %pad_maximum_fusion.12), channel_id=1, source_target_pairs={{0,1},{1,0},{2,6},{3,7},{4,5},{5,4},{6,2},{7,3},{8,9},{9,8},{10,14... | collective-permute-start | bytes 417800 | tf_op jit(solution)/shard_map/ppermute | solution.py:75
  12.6 5.9 %collective-permute-start.9 = (bf16[2,1,1,1,16,2304]{5,4,3,2,1,0:T(8,128)(2,1)S(1)}, bf16[2,1,1,1,16,2304]{5,4,3,2,1,0:T(8,128)(2,1)S(1)}, u32[]{:S(2)}, u32[]{:S(2)}) collective-permute-start(bf16[2,1,1,1,16,2304]{5,4,3,2,1,0:T(8,128)(2,1)S(1)} %pad_maximum_fusion.11), channel_id=1, source_target_pairs={{0,1},{1,0},{2,6},{3,7},{4,5},{5,4},{6,2},{7,3},{8,9},{9,8},{10,14... | collective-permute-start | bytes 442376 | tf_op jit(solution)/shard_map/ppermute | solution.py:75
  15.4 8.4 %collective-permute-start.5 = (bf16[1,2,1,1,16,2816]{5,4,3,2,1,0:T(8,128)(2,1)S(1)}, bf16[1,2,1,1,16,2816]{5,4,3,2,1,0:T(8,128)(2,1)S(1)}, u32[]{:S(2)}, u32[]{:S(2)}) collective-permute-start(bf16[1,2,1,1,16,2816]{5,4,3,2,1,0:T(8,128)(2,1)S(1)} %pad_maximum_fusion.10), channel_id=1, source_target_pairs={{0,16},{1,17},{2,10},{3,11},{4,20},{5,21},{6,14},{7,15},{8,24},{9,... | collective-permute-start | bytes 540680 | tf_op jit(solution)/shard_map/ppermute | solution.py:75
  16.7 23.2 %copy-start = (bf16[1,7168,512]{2,1,0:T(8,128)(2,1)S(1)}, bf16[1,7168,512]{2,1,0:T(8,128)(2,1)}, u32[]{:S(2)}) copy-start(bf16[1,7168,512]{2,1,0:T(8,128)(2,1)} %param.9) | copy-start | bytes 22020100
  16.7 13.2 %collective-permute-start.2 = (bf16[1,2,1,2,16,2176]{5,4,3,2,1,0:T(8,128)(2,1)S(1)}, bf16[1,2,1,2,16,2176]{5,4,3,2,1,0:T(8,128)(2,1)S(1)}, u32[]{:S(2)}, u32[]{:S(2)}) collective-permute-start(bf16[1,2,1,2,16,2176]{5,4,3,2,1,0:T(8,128)(2,1)S(1)} %pad_maximum_fusion.8), channel_id=1, source_target_pairs={{0,16},{1,17},{2,10},{3,11},{4,20},{5,21},{6,14},{7,15},{8,24},{9,... | collective-permute-start | bytes 835592 | tf_op jit(solution)/shard_map/ppermute | solution.py:75
  18.6 13.1 %collective-permute-start.10 = (bf16[2,1,1,2,16,2304]{5,4,3,2,1,0:T(8,128)(2,1)S(1)}, bf16[2,1,1,2,16,2304]{5,4,3,2,1,0:T(8,128)(2,1)S(1)}, u32[]{:S(2)}, u32[]{:S(2)}) collective-permute-start(bf16[2,1,1,2,16,2304]{5,4,3,2,1,0:T(8,128)(2,1)S(1)} %pad_maximum_fusion.7), channel_id=1, source_target_pairs={{0,4},{1,5},{2,3},{3,2},{4,0},{5,1},{6,7},{7,6},{8,12},{9,13},{10,... | collective-permute-start | bytes 884744 | tf_op jit(solution)/shard_map/ppermute | solution.py:75
  23.8 14.2 %collective-permute-start.6 = (bf16[2,2,1,1,16,2816]{5,4,3,2,1,0:T(8,128)(2,1)S(1)}, bf16[2,2,1,1,16,2816]{5,4,3,2,1,0:T(8,128)(2,1)S(1)}, u32[]{:S(2)}, u32[]{:S(2)}) collective-permute-start(bf16[2,2,1,1,16,2816]{5,4,3,2,1,0:T(8,128)(2,1)S(1)} %pad_maximum_fusion.6), channel_id=1, source_target_pairs={{0,1},{1,0},{2,6},{3,7},{4,5},{5,4},{6,2},{7,3},{8,9},{9,8},{10,14... | collective-permute-start | bytes 1081352 | tf_op jit(solution)/shard_map/ppermute | solution.py:75
  30.0 9.6 %collective-permute-start.3 = (bf16[2,2,1,2,16,2176]{5,4,3,2,1,0:T(8,128)(2,1)S(1)}, bf16[2,2,1,2,16,2176]{5,4,3,2,1,0:T(8,128)(2,1)S(1)}, u32[]{:S(2)}, u32[]{:S(2)}) collective-permute-start(bf16[2,2,1,2,16,2176]{5,4,3,2,1,0:T(8,128)(2,1)S(1)} %pad_maximum_fusion.5), channel_id=1, source_target_pairs={{0,4},{1,5},{2,3},{3,2},{4,0},{5,1},{6,7},{7,6},{8,12},{9,13},{10,... | collective-permute-start | bytes 1671176 | tf_op jit(solution)/shard_map/ppermute | solution.py:75
  31.7 17.0 %collective-permute-start.11 = (bf16[2,1,2,2,16,2304]{5,4,3,2,1,0:T(8,128)(2,1)S(1)}, bf16[2,1,2,2,16,2304]{5,4,3,2,1,0:T(8,128)(2,1)S(1)}, u32[]{:S(2)}, u32[]{:S(2)}) collective-permute-start(bf16[2,1,2,2,16,2304]{5,4,3,2,1,0:T(8,128)(2,1)S(1)} %pad_maximum_fusion.4), channel_id=1, source_target_pairs={{0,8},{1,9},{2,18},{3,19},{4,12},{5,13},{6,22},{7,23},{8,0},{9,1},... | collective-permute-start | bytes 1769480 | tf_op jit(solution)/shard_map/ppermute | solution.py:75
  38.1 11.5 %collective-permute-start.7 = (bf16[2,2,1,2,16,2816]{5,4,3,2,1,0:T(8,128)(2,1)S(1)}, bf16[2,2,1,2,16,2816]{5,4,3,2,1,0:T(8,128)(2,1)S(1)}, u32[]{:S(2)}, u32[]{:S(2)}) collective-permute-start(bf16[2,2,1,2,16,2816]{5,4,3,2,1,0:T(8,128)(2,1)S(1)} %pad_maximum_fusion.3), channel_id=1, source_target_pairs={{0,4},{1,5},{2,3},{3,2},{4,0},{5,1},{6,7},{7,6},{8,12},{9,13},{10,... | collective-permute-start | bytes 2162696 | tf_op jit(solution)/shard_map/ppermute | solution.py:75
  39.8 11.7 %collective-permute-start.12 = (bf16[256,2176]{1,0:T(8,128)(2,1)S(1)}, bf16[256,2176]{1,0:T(8,128)(2,1)S(1)}, u32[]{:S(2)}, u32[]{:S(2)}) collective-permute-start(bf16[256,2176]{1,0:T(8,128)(2,1)S(1)} %bitcast.85), channel_id=1, source_target_pairs={{0,2},{1,3},{2,0},{3,1},{4,6},{5,7},{6,4},{7,5},{8,10},{9,11},{10,... | collective-permute-start | bytes 3342344 | tf_op jit(solution)/shard_map/ppermute | solution.py:75
  40.6 9.8 %slice-start = ((s8[7340032]{0:T(1024)(128)(4,1)}), s8[4194304]{0:T(1024)(128)(4,1)S(1)}, s32[]{:S(2)}) async-start(s8[7340032]{0:T(1024)(128)(4,1)} %bitcast.99), calls=%async_computation | async-start | bytes 8388608
  48.8 4.2 %collective-permute-start.14 = (bf16[256,2304]{1,0:T(8,128)(2,1)S(1)}, bf16[256,2304]{1,0:T(8,128)(2,1)S(1)}, u32[]{:S(2)}, u32[]{:S(2)}) collective-permute-start(bf16[256,2304]{1,0:T(8,128)(2,1)S(1)} %bitcast.95), channel_id=1, source_target_pairs={{0,2},{1,3},{2,0},{3,1},{4,6},{5,7},{6,4},{7,5},{8,10},{9,11},{10,... | collective-permute-start | bytes 3538952 | tf_op jit(solution)/shard_map/ppermute | solution.py:75
  49.8 4.8 %collective-permute-start.13 = (bf16[256,2816]{1,0:T(8,128)(2,1)S(1)}, bf16[256,2816]{1,0:T(8,128)(2,1)S(1)}, u32[]{:S(2)}, u32[]{:S(2)}) collective-permute-start(bf16[256,2816]{1,0:T(8,128)(2,1)S(1)} %bitcast.82), channel_id=1, source_target_pairs={{0,2},{1,3},{2,0},{3,1},{4,6},{5,7},{6,4},{7,5},{8,10},{9,11},{10,... | collective-permute-start | bytes 4325384 | tf_op jit(solution)/shard_map/ppermute | solution.py:75
  58.9 4.3 %collective-permute-start.15 = (bf16[256,2432]{1,0:T(8,128)(2,1)S(1)}, bf16[256,2432]{1,0:T(8,128)(2,1)S(1)}, u32[]{:S(2)}, u32[]{:S(2)}) collective-permute-start(bf16[256,2432]{1,0:T(8,128)(2,1)S(1)} %convolution_convert_fusion.2), channel_id=1, source_target_pairs={{0,2},{1,3},{2,0},{3,1},{4,6},{5,7},{6,4},{7,5},{8,10},{9,11},{10,... | collective-permute-start | bytes 3735560 | tf_op jit(solution)/shard_map/ppermute | solution.py:75
  59.9 10.5 %collective-permute-start.17 = (bf16[256,2432]{1,0:T(8,128)(2,1)S(1)}, bf16[256,2432]{1,0:T(8,128)(2,1)S(1)}, u32[]{:S(2)}, u32[]{:S(2)}) collective-permute-start(bf16[256,2432]{1,0:T(8,128)(2,1)S(1)} %convolution_convert_fusion.1), channel_id=1, source_target_pairs={{0,2},{1,3},{2,0},{3,1},{4,6},{5,7},{6,4},{7,5},{8,10},{9,11},{10,... | collective-permute-start | bytes 3735560 | tf_op jit(solution)/shard_map/ppermute | solution.py:75
  61.3 4.6 %collective-permute-start.21 = (bf16[256,2304]{1,0:T(8,128)(2,1)S(1)}, bf16[256,2304]{1,0:T(8,128)(2,1)S(1)}, u32[]{:S(2)}, u32[]{:S(2)}) collective-permute-start(bf16[256,2304]{1,0:T(8,128)(2,1)S(1)} %convolution_convert_fusion), channel_id=1, source_target_pairs={{0,2},{1,3},{2,0},{3,1},{4,6},{5,7},{6,4},{7,5},{8,10},{9,11},{10,... | collective-permute-start | bytes 3538952 | tf_op jit(solution)/shard_map/ppermute | solution.py:75
  64.2 10.3 %collective-permute-start.16 = (bf16[2,2,1,2,16,2432]{5,4,3,2,1,0:T(8,128)(2,1)S(1)}, bf16[2,2,1,2,16,2432]{5,4,3,2,1,0:T(8,128)(2,1)S(1)}, u32[]{:S(2)}, u32[]{:S(2)}) collective-permute-start(bf16[2,2,1,2,16,2432]{5,4,3,2,1,0:T(8,128)(2,1)S(1)} %slice.199), channel_id=1, source_target_pairs={{0,4},{1,5},{2,3},{3,2},{4,0},{5,1},{6,7},{7,6},{8,12},{9,13},{10,... | collective-permute-start | bytes 1867784 | tf_op jit(solution)/shard_map/ppermute | solution.py:75
  66.7 23.6 %collective-permute-start.22 = (bf16[2,1,2,2,16,2304]{5,4,3,2,1,0:T(8,128)(2,1)S(1)}, bf16[2,1,2,2,16,2304]{5,4,3,2,1,0:T(8,128)(2,1)S(1)}, u32[]{:S(2)}, u32[]{:S(2)}) collective-permute-start(bf16[2,1,2,2,16,2304]{5,4,3,2,1,0:T(8,128)(2,1)S(1)} %slice.209), channel_id=1, source_target_pairs={{0,8},{1,9},{2,18},{3,19},{4,12},{5,13},{6,22},{7,23},{8,0},{9,1},... | collective-permute-start | bytes 1769480 | tf_op jit(solution)/shard_map/ppermute | solution.py:75
  71.4 11.8 %collective-permute-start.25 = (bf16[2,2,1,2,16,2432]{5,4,3,2,1,0:T(8,128)(2,1)S(1)}, bf16[2,2,1,2,16,2432]{5,4,3,2,1,0:T(8,128)(2,1)S(1)}, u32[]{:S(2)}, u32[]{:S(2)}) collective-permute-start(bf16[2,2,1,2,16,2432]{5,4,3,2,1,0:T(8,128)(2,1)S(1)} %slice.215), channel_id=1, source_target_pairs={{0,4},{1,5},{2,3},{3,2},{4,0},{5,1},{6,7},{7,6},{8,12},{9,13},{10,... | collective-permute-start | bytes 1867784 | tf_op jit(solution)/shard_map/ppermute | solution.py:75
  74.7 15.4 %collective-permute-start.18 = (bf16[2,2,1,1,16,2432]{5,4,3,2,1,0:T(8,128)(2,1)S(1)}, bf16[2,2,1,1,16,2432]{5,4,3,2,1,0:T(8,128)(2,1)S(1)}, u32[]{:S(2)}, u32[]{:S(2)}) collective-permute-start(bf16[2,2,1,1,16,2432]{5,4,3,2,1,0:T(8,128)(2,1)S(1)} %slice.202), channel_id=1, source_target_pairs={{0,1},{1,0},{2,6},{3,7},{4,5},{5,4},{6,2},{7,3},{8,9},{9,8},{10,14... | collective-permute-start | bytes 933896 | tf_op jit(solution)/shard_map/ppermute | solution.py:75
  83.4 13.8 %collective-permute-start.26 = (bf16[2,2,1,1,16,2432]{5,4,3,2,1,0:T(8,128)(2,1)S(1)}, bf16[2,2,1,1,16,2432]{5,4,3,2,1,0:T(8,128)(2,1)S(1)}, u32[]{:S(2)}, u32[]{:S(2)}) collective-permute-start(bf16[2,2,1,1,16,2432]{5,4,3,2,1,0:T(8,128)(2,1)S(1)} %slice.217), channel_id=1, source_target_pairs={{0,1},{1,0},{2,6},{3,7},{4,5},{5,4},{6,2},{7,3},{8,9},{9,8},{10,14... | collective-permute-start | bytes 933896 | tf_op jit(solution)/shard_map/ppermute | solution.py:75
  90.2 10.5 %collective-permute-start.19 = (bf16[1,2,1,1,16,2432]{5,4,3,2,1,0:T(8,128)(2,1)S(1)}, bf16[1,2,1,1,16,2432]{5,4,3,2,1,0:T(8,128)(2,1)S(1)}, u32[]{:S(2)}, u32[]{:S(2)}) collective-permute-start(bf16[1,2,1,1,16,2432]{5,4,3,2,1,0:T(8,128)(2,1)S(1)} %slice.204), channel_id=1, source_target_pairs={{0,16},{1,17},{2,10},{3,11},{4,20},{5,21},{6,14},{7,15},{8,24},{9,... | collective-permute-start | bytes 466952 | tf_op jit(solution)/shard_map/ppermute | solution.py:75
  90.5 10.4 %collective-permute-start.23 = (bf16[2,1,1,2,16,2304]{5,4,3,2,1,0:T(8,128)(2,1)S(1)}, bf16[2,1,1,2,16,2304]{5,4,3,2,1,0:T(8,128)(2,1)S(1)}, u32[]{:S(2)}, u32[]{:S(2)}) collective-permute-start(bf16[2,1,1,2,16,2304]{5,4,3,2,1,0:T(8,128)(2,1)S(1)} %slice.211), channel_id=1, source_target_pairs={{0,4},{1,5},{2,3},{3,2},{4,0},{5,1},{6,7},{7,6},{8,12},{9,13},{10,... | collective-permute-start | bytes 884744 | tf_op jit(solution)/shard_map/ppermute | solution.py:75
  97.3 8.5 %collective-permute-start.27 = (bf16[2,1,1,1,16,2432]{5,4,3,2,1,0:T(8,128)(2,1)S(1)}, bf16[2,1,1,1,16,2432]{5,4,3,2,1,0:T(8,128)(2,1)S(1)}, u32[]{:S(2)}, u32[]{:S(2)}) collective-permute-start(bf16[2,1,1,1,16,2432]{5,4,3,2,1,0:T(8,128)(2,1)S(1)} %slice.219), channel_id=1, source_target_pairs={{0,8},{1,9},{2,18},{3,19},{4,12},{5,13},{6,22},{7,23},{8,0},{9,1},... | collective-permute-start | bytes 466952 | tf_op jit(solution)/shard_map/ppermute | solution.py:75
  100.8 4.9 %collective-permute-start.20 = (bf16[1,1,1,1,16,2432]{5,4,3,2,1,0:T(8,128)(2,1)S(1)}, bf16[1,1,1,1,16,2432]{5,4,3,2,1,0:T(8,128)(2,1)S(1)}, u32[]{:S(2)}, u32[]{:S(2)}) collective-permute-start(bf16[1,1,1,1,16,2432]{5,4,3,2,1,0:T(8,128)(2,1)S(1)} %slice.206), channel_id=1, source_target_pairs={{0,8},{1,9},{2,18},{3,19},{4,12},{5,13},{6,22},{7,23},{8,0},{9,1},... | collective-permute-start | bytes 233480 | tf_op jit(solution)/shard_map/ppermute | solution.py:75
  101.0 6.0 %collective-permute-start.24 = (bf16[2,1,1,1,16,2304]{5,4,3,2,1,0:T(8,128)(2,1)S(1)}, bf16[2,1,1,1,16,2304]{5,4,3,2,1,0:T(8,128)(2,1)S(1)}, u32[]{:S(2)}, u32[]{:S(2)}) collective-permute-start(bf16[2,1,1,1,16,2304]{5,4,3,2,1,0:T(8,128)(2,1)S(1)} %slice.213), channel_id=1, source_target_pairs={{0,1},{1,0},{2,6},{3,7},{4,5},{5,4},{6,2},{7,3},{8,9},{9,8},{10,14... | collective-permute-start | bytes 442376 | tf_op jit(solution)/shard_map/ppermute | solution.py:75
  105.8 6.0 %collective-permute-start.29 = (bf16[1,1,1,1,16,2432]{5,4,3,2,1,0:T(8,128)(2,1)S(1)}, bf16[1,1,1,1,16,2432]{5,4,3,2,1,0:T(8,128)(2,1)S(1)}, u32[]{:S(2)}, u32[]{:S(2)}) collective-permute-start(bf16[1,1,1,1,16,2432]{5,4,3,2,1,0:T(8,128)(2,1)S(1)} %slice.223), channel_id=1, source_target_pairs={{0,16},{1,17},{2,10},{3,11},{4,20},{5,21},{6,14},{7,15},{8,24},{9,... | collective-permute-start | bytes 233480 | tf_op jit(solution)/shard_map/ppermute | solution.py:75
  107.1 5.5 %collective-permute-start.28 = (bf16[1,1,1,1,16,2304]{5,4,3,2,1,0:T(8,128)(2,1)S(1)}, bf16[1,1,1,1,16,2304]{5,4,3,2,1,0:T(8,128)(2,1)S(1)}, u32[]{:S(2)}, u32[]{:S(2)}) collective-permute-start(bf16[1,1,1,1,16,2304]{5,4,3,2,1,0:T(8,128)(2,1)S(1)} %slice.221), channel_id=1, source_target_pairs={{0,16},{1,17},{2,10},{3,11},{4,20},{5,21},{6,14},{7,15},{8,24},{9,... | collective-permute-start | bytes 221192 | tf_op jit(solution)/shard_map/ppermute | solution.py:75
  (3 other events, 6.5 us)

commit v4 on v2

--- a/solution.py
+++ b/solution.py
@@ -78,13 +78,13 @@
 STEPS = ("far", "near", "late", "early")
 GATHER = (
     (22, ("near", "far", "early", "late")),
-    (16, ("near", "early", "far", "late")),
+    (16, ("near", "late", "far", "early")),
     (18, ("far", "early", "late", "near")),
 )
 SCATTER = (
     (19, ("late", "early", "far", "near")),
     (18, ("near", "late", "early", "far")),
-    (19, ("late", "early", "near", "far")),
+    (19, ("early", "late", "near", "far")),
 )
 GATHER_TURNS = (10, 1, 12, 10, 11, 2, 10, 11, 12, 10, 12, 11, 10, 10, 10, 12, 11, 11, 12, 11, 12)
 SCATTER_TURNS = (0, 11, 2, 0, 2, 0, 1, 2, 0, 1, 2, 0, 1, 2, 11)

time: 112 us -> 113 us (level)
  starting transfers between devices: 45.6 us -> 48.8 us
  waiting for transfers between devices: 40.6 us -> 37.8 us
    ppermute x30, starting transfers between devices: 45.6 us -> 48.8 us  [exchange(): return lax.ppermute(block, AXES, perm)]
    ppermute x30, waiting for transfers between devices: 40.6 us -> 37.8 us  [exchange(): return lax.ppermute(block, AXES, perm)]
  transfers between devices with their start and end apart: 30 -> 30, of which waited for: 14 -> 13; matrix products, arithmetic and copies ran while one was open for 17% -> 17% of each run, Pallas kernels for 0% -> 0%
where the time goes in v4:
time: 113 us
  starting transfers between devices  48.8 us (43%)
  waiting for transfers between devices  37.8 us (33%)
  matrix products  16.8 us (15%)
  local copies, waits for them, and re-layouts  5.91 us (5%)
  other arithmetic  2.68 us (2%)
    ppermute x30, starting transfers between devices, exchange(): return lax.ppermute(block, AXES, perm)  48.8 us
    ppermute x30, waiting for transfers between devices, exchange(): return lax.ppermute(block, AXES, perm)  37.8 us
    dot_general x6, matrix products, products(): jnp.dot(rows, w_gate[lo:hi], preferred_element_type=jnp.float32)  6.72 us
    dot_general x6, matrix products, product(): jnp.dot(hidden[j], w_down[:, lo:hi], preferred_element_type=jnp.float32)  5.23 us
    dot_general x6, matrix products, products(): jnp.dot(rows, w_up[lo:hi], preferred_element_type=jnp.float32)  4.87 us
    unnamed x12, local copies, waits for them, and re-layouts  3.02 us
  transfers between devices with their start and end apart: 30, of which 13 were waited for; matrix products, arithmetic and copies ran while one was open for 17% of the time, Pallas kernels for 0%

profile of v4, /device:TPU:0, one launch (start us, length us, event | category | flops | bytes accessed | tf_op | source)
XLA Modules:
  0.0 112.5 jit_solution(18136695731019491881)
XLA Ops:
  0.8 3.0 %collective-permute-start.1 = (bf16[1,1,1,1,16,2048]{5,4,3,2,1,0:T(8,128)(2,1)S(1)}, bf16[1,1,1,1,16,2048]{5,4,3,2,1,0:T(8,128)(2,1)S(1)}, u32[]{:S(2)}, u32[]{:S(2)}) collective-permute-start(bf16[1,1,1,1,16,2048]{5,4,3,2,1,0:T(8,128)(2,1)S(1)} %slice_bitcast_fusion.1), channel_id=1, source_target_pairs={{0,8},{1,9},{2,18},{3,19},{4,12},{5,13},{6,22},{7,23},{8,0},{9,1},... | collective-permute-start | bytes 196616 | tf_op jit(solution)/shard_map/ppermute | solution.py:75
  6.5 2.7 %collective-permute-start = (bf16[1,1,1,1,16,2432]{5,4,3,2,1,0:T(8,128)(2,1)S(1)}, bf16[1,1,1,1,16,2432]{5,4,3,2,1,0:T(8,128)(2,1)S(1)}, u32[]{:S(2)}, u32[]{:S(2)}) collective-permute-start(bf16[1,1,1,1,16,2432]{5,4,3,2,1,0:T(8,128)(2,1)S(1)} %maximum_bitcast_fusion), channel_id=1, source_target_pairs={{0,16},{1,17},{2,10},{3,11},{4,20},{5,21},{6,14},{7,15},{8,24},{9,... | collective-permute-start | bytes 233480 | tf_op jit(solution)/shard_map/ppermute | solution.py:75
  10.5 1.6 %collective-permute-start.9 = (bf16[1,2,1,1,16,2048]{5,4,3,2,1,0:T(8,128)(2,1)S(1)}, bf16[1,2,1,1,16,2048]{5,4,3,2,1,0:T(8,128)(2,1)S(1)}, u32[]{:S(2)}, u32[]{:S(2)}) collective-permute-start(bf16[1,2,1,1,16,2048]{5,4,3,2,1,0:T(8,128)(2,1)S(1)} %pad_maximum_fusion.12), channel_id=1, source_target_pairs={{0,4},{1,5},{2,3},{3,2},{4,0},{5,1},{6,7},{7,6},{8,12},{9,13},{10,... | collective-permute-start | bytes 393224 | tf_op jit(solution)/shard_map/ppermute | solution.py:75
  12.3 1.9 %collective-permute-start.2 = (bf16[2,1,1,1,16,2432]{5,4,3,2,1,0:T(8,128)(2,1)S(1)}, bf16[2,1,1,1,16,2432]{5,4,3,2,1,0:T(8,128)(2,1)S(1)}, u32[]{:S(2)}, u32[]{:S(2)}) collective-permute-start(bf16[2,1,1,1,16,2432]{5,4,3,2,1,0:T(8,128)(2,1)S(1)} %pad_maximum_fusion.11), channel_id=1, source_target_pairs={{0,1},{1,0},{2,6},{3,7},{4,5},{5,4},{6,2},{7,3},{8,9},{9,8},{10,14... | collective-permute-start | bytes 466952 | tf_op jit(solution)/shard_map/ppermute | solution.py:75
  14.2 1.2 %collective-permute-done.5 = bf16[1,1,1,1,16,2816]{5,4,3,2,1,0:T(8,128)(2,1)S(1)} collective-permute-done((bf16[1,1,1,1,16,2816]{5,4,3,2,1,0:T(8,128)(2,1)S(1)}, bf16[1,1,1,1,16,2816]{5,4,3,2,1,0:T(8,128)(2,1)S(1)}, u32[]{:S(2)}, u32[]{:S(2)}) %collective-permute-start.5) | collective-permute-done | bytes 90144 | tf_op jit(solution)/shard_map/ppermute | solution.py:75
  15.4 1.3 %collective-permute-start.6 = (bf16[1,2,1,1,16,2816]{5,4,3,2,1,0:T(8,128)(2,1)S(1)}, bf16[1,2,1,1,16,2816]{5,4,3,2,1,0:T(8,128)(2,1)S(1)}, u32[]{:S(2)}, u32[]{:S(2)}) collective-permute-start(bf16[1,2,1,1,16,2816]{5,4,3,2,1,0:T(8,128)(2,1)S(1)} %pad_maximum_fusion.10), channel_id=1, source_target_pairs={{0,16},{1,17},{2,10},{3,11},{4,20},{5,21},{6,14},{7,15},{8,24},{9,... | collective-permute-start | bytes 540680 | tf_op jit(solution)/shard_map/ppermute | solution.py:75
  16.8 1.8 %collective-permute-start.10 = (bf16[1,2,2,1,16,2048]{5,4,3,2,1,0:T(8,128)(2,1)S(1)}, bf16[1,2,2,1,16,2048]{5,4,3,2,1,0:T(8,128)(2,1)S(1)}, u32[]{:S(2)}, u32[]{:S(2)}) collective-permute-start(bf16[1,2,2,1,16,2048]{5,4,3,2,1,0:T(8,128)(2,1)S(1)} %pad_maximum_fusion.8), channel_id=1, source_target_pairs={{0,16},{1,17},{2,10},{3,11},{4,20},{5,21},{6,14},{7,15},{8,24},{9,... | collective-permute-start | bytes 786440 | tf_op jit(solution)/shard_map/ppermute | solution.py:75
  18.6 1.6 %collective-permute-start.3 = (bf16[2,1,1,2,16,2432]{5,4,3,2,1,0:T(8,128)(2,1)S(1)}, bf16[2,1,1,2,16,2432]{5,4,3,2,1,0:T(8,128)(2,1)S(1)}, u32[]{:S(2)}, u32[]{:S(2)}) collective-permute-start(bf16[2,1,1,2,16,2432]{5,4,3,2,1,0:T(8,128)(2,1)S(1)} %pad_maximum_fusion.7), channel_id=1, source_target_pairs={{0,4},{1,5},{2,3},{3,2},{4,0},{5,1},{6,7},{7,6},{8,12},{9,13},{10,... | collective-permute-start | bytes 933896 | tf_op jit(solution)/shard_map/ppermute | solution.py:75
  20.1 3.7 %collective-permute-done.6 = bf16[1,2,1,1,16,2816]{5,4,3,2,1,0:T(8,128)(2,1)S(1)} collective-permute-done((bf16[1,2,1,1,16,2816]{5,4,3,2,1,0:T(8,128)(2,1)S(1)}, bf16[1,2,1,1,16,2816]{5,4,3,2,1,0:T(8,128)(2,1)S(1)}, u32[]{:S(2)}, u32[]{:S(2)}) %collective-permute-start.6) | collective-permute-done | bytes 180256 | tf_op jit(solution)/shard_map/ppermute | solution.py:75
  23.9 1.6 %collective-permute-start.7 = (bf16[2,2,1,1,16,2816]{5,4,3,2,1,0:T(8,128)(2,1)S(1)}, bf16[2,2,1,1,16,2816]{5,4,3,2,1,0:T(8,128)(2,1)S(1)}, u32[]{:S(2)}, u32[]{:S(2)}) collective-permute-start(bf16[2,2,1,1,16,2816]{5,4,3,2,1,0:T(8,128)(2,1)S(1)} %pad_maximum_fusion.6), channel_id=1, source_target_pairs={{0,1},{1,0},{2,6},{3,7},{4,5},{5,4},{6,2},{7,3},{8,9},{9,8},{10,14... | collective-permute-start | bytes 1081352 | tf_op jit(solution)/shard_map/ppermute | solution.py:75
  25.4 11.2 %collective-permute-done.10 = bf16[1,2,2,1,16,2048]{5,4,3,2,1,0:T(8,128)(2,1)S(1)} collective-permute-done((bf16[1,2,2,1,16,2048]{5,4,3,2,1,0:T(8,128)(2,1)S(1)}, bf16[1,2,2,1,16,2048]{5,4,3,2,1,0:T(8,128)(2,1)S(1)}, u32[]{:S(2)}, u32[]{:S(2)}) %collective-permute-start.10) | collective-permute-done | bytes 262176 | tf_op jit(solution)/shard_map/ppermute | solution.py:75
  37.9 2.7 %collective-permute-start.8 = (bf16[2,2,1,2,16,2816]{5,4,3,2,1,0:T(8,128)(2,1)S(1)}, bf16[2,2,1,2,16,2816]{5,4,3,2,1,0:T(8,128)(2,1)S(1)}, u32[]{:S(2)}, u32[]{:S(2)}) collective-permute-start(bf16[2,2,1,2,16,2816]{5,4,3,2,1,0:T(8,128)(2,1)S(1)} %pad_maximum_fusion.3), channel_id=1, source_target_pairs={{0,4},{1,5},{2,3},{3,2},{4,0},{5,1},{6,7},{7,6},{8,12},{9,13},{10,... | collective-permute-start | bytes 2162696 | tf_op jit(solution)/shard_map/ppermute | solution.py:75
  40.6 5.3 %collective-permute-done.11 = bf16[2,2,2,1,16,2048]{5,4,3,2,1,0:T(8,128)(2,1)S(1)} collective-permute-done((bf16[2,2,2,1,16,2048]{5,4,3,2,1,0:T(8,128)(2,1)S(1)}, bf16[2,2,2,1,16,2048]{5,4,3,2,1,0:T(8,128)(2,1)S(1)}, u32[]{:S(2)}, u32[]{:S(2)}) %collective-permute-start.11) | collective-permute-done | bytes 524320 | tf_op jit(solution)/shard_map/ppermute | solution.py:75
  46.8 2.7 %fusion.32 = f32[256,512]{1,0:T(8,128)S(1)} fusion(bf16[256,2048]{1,0:T(8,128)(2,1)S(1)} %bitcast.97, bf16[1,7168,512]{2,1,0:T(8,128)(2,1)} %param.9), kind=kOutput, calls=%fused_computation.41 | convolution fusion | flops 536870912 | bytes 3670016 | tf_op jit(solution)/shard_map/dot_general | solution.py:115
  56.2 1.0 multiply_convert_fusion.1
  57.4 1.2 %slice-done.3 = s8[3145728]{0:T(1024)(128)(4,1)S(1)} async-done(((s8[7340032]{0:T(1024)(128)(4,1)}), s8[3145728]{0:T(1024)(128)(4,1)S(1)}, s32[]{:S(2)}) %slice-start.3) | async-done | bytes 3145752
  63.2 1.0 multiply_convert_fusion.2
  65.1 2.6 %collective-permute-start.16 = (bf16[2,2,1,2,16,2432]{5,4,3,2,1,0:T(8,128)(2,1)S(1)}, bf16[2,2,1,2,16,2432]{5,4,3,2,1,0:T(8,128)(2,1)S(1)}, u32[]{:S(2)}, u32[]{:S(2)}) collective-permute-start(bf16[2,2,1,2,16,2432]{5,4,3,2,1,0:T(8,128)(2,1)S(1)} %slice.199), channel_id=1, source_target_pairs={{0,4},{1,5},{2,3},{3,2},{4,0},{5,1},{6,7},{7,6},{8,12},{9,13},{10,... | collective-permute-start | bytes 1867784 | tf_op jit(solution)/shard_map/ppermute | solution.py:75
  68.5 1.1 collective-permute-start.23
  69.6 1.1 add_convert_fusion
  70.8 7.8 %collective-permute-done.16 = bf16[2,2,1,2,16,2432]{5,4,3,2,1,0:T(8,128)(2,1)S(1)} collective-permute-done((bf16[2,2,1,2,16,2432]{5,4,3,2,1,0:T(8,128)(2,1)S(1)}, bf16[2,2,1,2,16,2432]{5,4,3,2,1,0:T(8,128)(2,1)S(1)}, u32[]{:S(2)}, u32[]{:S(2)}) %collective-permute-start.16) | collective-permute-done | bytes 622624 | tf_op jit(solution)/shard_map/ppermute | solution.py:75
  79.3 1.9 %collective-permute-done.20 = bf16[2,2,2,1,16,2432]{5,4,3,2,1,0:T(8,128)(2,1)S(1)} collective-permute-done((bf16[2,2,2,1,16,2432]{5,4,3,2,1,0:T(8,128)(2,1)S(1)}, bf16[2,2,2,1,16,2432]{5,4,3,2,1,0:T(8,128)(2,1)S(1)}, u32[]{:S(2)}, u32[]{:S(2)}) %collective-permute-start.20) | collective-permute-done | bytes 622624 | tf_op jit(solution)/shard_map/ppermute | solution.py:75
  81.4 2.6 %collective-permute-start.22 = (bf16[2,2,1,1,16,2432]{5,4,3,2,1,0:T(8,128)(2,1)S(1)}, bf16[2,2,1,1,16,2432]{5,4,3,2,1,0:T(8,128)(2,1)S(1)}, u32[]{:S(2)}, u32[]{:S(2)}) collective-permute-start(bf16[2,2,1,1,16,2432]{5,4,3,2,1,0:T(8,128)(2,1)S(1)} %slice.209), channel_id=1, source_target_pairs={{0,4},{1,5},{2,3},{3,2},{4,0},{5,1},{6,7},{7,6},{8,12},{9,13},{10,... | collective-permute-start | bytes 933896 | tf_op jit(solution)/shard_map/ppermute | solution.py:75
  84.0 1.9 %collective-permute-done.19 = bf16[2,2,1,1,16,2432]{5,4,3,2,1,0:T(8,128)(2,1)S(1)} collective-permute-done((bf16[2,2,1,1,16,2432]{5,4,3,2,1,0:T(8,128)(2,1)S(1)}, bf16[2,2,1,1,16,2432]{5,4,3,2,1,0:T(8,128)(2,1)S(1)}, u32[]{:S(2)}, u32[]{:S(2)}) %collective-permute-start.19) | collective-permute-done | bytes 311328 | tf_op jit(solution)/shard_map/ppermute | solution.py:75
  86.1 2.9 %collective-permute-start.21 = (bf16[1,2,1,1,16,2432]{5,4,3,2,1,0:T(8,128)(2,1)S(1)}, bf16[1,2,1,1,16,2432]{5,4,3,2,1,0:T(8,128)(2,1)S(1)}, u32[]{:S(2)}, u32[]{:S(2)}) collective-permute-start(bf16[1,2,1,1,16,2432]{5,4,3,2,1,0:T(8,128)(2,1)S(1)} %slice.207), channel_id=1, source_target_pairs={{0,16},{1,17},{2,10},{3,11},{4,20},{5,21},{6,14},{7,15},{8,24},{9,... | collective-permute-start | bytes 466952 | tf_op jit(solution)/shard_map/ppermute | solution.py:75
  89.1 2.4 %collective-permute-start.26 = (bf16[2,1,1,2,16,2304]{5,4,3,2,1,0:T(8,128)(2,1)S(1)}, bf16[2,1,1,2,16,2304]{5,4,3,2,1,0:T(8,128)(2,1)S(1)}, u32[]{:S(2)}, u32[]{:S(2)}) collective-permute-start(bf16[2,1,1,2,16,2304]{5,4,3,2,1,0:T(8,128)(2,1)S(1)} %slice.217), channel_id=1, source_target_pairs={{0,4},{1,5},{2,3},{3,2},{4,0},{5,1},{6,7},{7,6},{8,12},{9,13},{10,... | collective-permute-start | bytes 884744 | tf_op jit(solution)/shard_map/ppermute | solution.py:75
  91.6 6.3 %collective-permute-start.25 = (bf16[2,1,1,1,16,2432]{5,4,3,2,1,0:T(8,128)(2,1)S(1)}, bf16[2,1,1,1,16,2432]{5,4,3,2,1,0:T(8,128)(2,1)S(1)}, u32[]{:S(2)}, u32[]{:S(2)}) collective-permute-start(bf16[2,1,1,1,16,2432]{5,4,3,2,1,0:T(8,128)(2,1)S(1)} %slice.215), channel_id=1, source_target_pairs={{0,8},{1,9},{2,18},{3,19},{4,12},{5,13},{6,22},{7,23},{8,0},{9,1},... | collective-permute-start | bytes 466952 | tf_op jit(solution)/shard_map/ppermute | solution.py:75
  98.0 2.2 %collective-permute-start.24 = (bf16[1,1,1,1,16,2432]{5,4,3,2,1,0:T(8,128)(2,1)S(1)}, bf16[1,1,1,1,16,2432]{5,4,3,2,1,0:T(8,128)(2,1)S(1)}, u32[]{:S(2)}, u32[]{:S(2)}) collective-permute-start(bf16[1,1,1,1,16,2432]{5,4,3,2,1,0:T(8,128)(2,1)S(1)} %slice.213), channel_id=1, source_target_pairs={{0,8},{1,9},{2,18},{3,19},{4,12},{5,13},{6,22},{7,23},{8,0},{9,1},... | collective-permute-start | bytes 233480 | tf_op jit(solution)/shard_map/ppermute | solution.py:75
  100.2 1.0 collective-permute-start.27
  102.7 3.7 %collective-permute-start.29 = (bf16[1,1,1,1,16,2432]{5,4,3,2,1,0:T(8,128)(2,1)S(1)}, bf16[1,1,1,1,16,2432]{5,4,3,2,1,0:T(8,128)(2,1)S(1)}, u32[]{:S(2)}, u32[]{:S(2)}) collective-permute-start(bf16[1,1,1,1,16,2432]{5,4,3,2,1,0:T(8,128)(2,1)S(1)} %slice.223), channel_id=1, source_target_pairs={{0,16},{1,17},{2,10},{3,11},{4,20},{5,21},{6,14},{7,15},{8,24},{9,... | collective-permute-start | bytes 233480 | tf_op jit(solution)/shard_map/ppermute | solution.py:75
  106.5 2.1 %collective-permute-start.28 = (bf16[1,1,1,1,16,2304]{5,4,3,2,1,0:T(8,128)(2,1)S(1)}, bf16[1,1,1,1,16,2304]{5,4,3,2,1,0:T(8,128)(2,1)S(1)}, u32[]{:S(2)}, u32[]{:S(2)}) collective-permute-start(bf16[1,1,1,1,16,2304]{5,4,3,2,1,0:T(8,128)(2,1)S(1)} %slice.221), channel_id=1, source_target_pairs={{0,16},{1,17},{2,10},{3,11},{4,20},{5,21},{6,14},{7,15},{8,24},{9,... | collective-permute-start | bytes 221192 | tf_op jit(solution)/shard_map/ppermute | solution.py:75
  108.8 3.0 %collective-permute-done.28 = bf16[1,1,1,1,16,2304]{5,4,3,2,1,0:T(8,128)(2,1)S(1)} collective-permute-done((bf16[1,1,1,1,16,2304]{5,4,3,2,1,0:T(8,128)(2,1)S(1)}, bf16[1,1,1,1,16,2304]{5,4,3,2,1,0:T(8,128)(2,1)S(1)}, u32[]{:S(2)}, u32[]{:S(2)}) %collective-permute-start.28) | collective-permute-done | bytes 73760 | tf_op jit(solution)/shard_map/ppermute | solution.py:75
  (106 shorter events, 24.3 us)
Async XLA Ops:
  0.8 9.7 %collective-permute-start.1 = (bf16[1,1,1,1,16,2048]{5,4,3,2,1,0:T(8,128)(2,1)S(1)}, bf16[1,1,1,1,16,2048]{5,4,3,2,1,0:T(8,128)(2,1)S(1)}, u32[]{:S(2)}, u32[]{:S(2)}) collective-permute-start(bf16[1,1,1,1,16,2048]{5,4,3,2,1,0:T(8,128)(2,1)S(1)} %slice_bitcast_fusion.1), channel_id=1, source_target_pairs={{0,8},{1,9},{2,18},{3,19},{4,12},{5,13},{6,22},{7,23},{8,0},{9,1},... | collective-permute-start | bytes 196616 | tf_op jit(solution)/shard_map/ppermute | solution.py:75
  6.5 5.7 %collective-permute-start = (bf16[1,1,1,1,16,2432]{5,4,3,2,1,0:T(8,128)(2,1)S(1)}, bf16[1,1,1,1,16,2432]{5,4,3,2,1,0:T(8,128)(2,1)S(1)}, u32[]{:S(2)}, u32[]{:S(2)}) collective-permute-start(bf16[1,1,1,1,16,2432]{5,4,3,2,1,0:T(8,128)(2,1)S(1)} %maximum_bitcast_fusion), channel_id=1, source_target_pairs={{0,16},{1,17},{2,10},{3,11},{4,20},{5,21},{6,14},{7,15},{8,24},{9,... | collective-permute-start | bytes 233480 | tf_op jit(solution)/shard_map/ppermute | solution.py:75
  10.0 5.4 %collective-permute-start.5 = (bf16[1,1,1,1,16,2816]{5,4,3,2,1,0:T(8,128)(2,1)S(1)}, bf16[1,1,1,1,16,2816]{5,4,3,2,1,0:T(8,128)(2,1)S(1)}, u32[]{:S(2)}, u32[]{:S(2)}) collective-permute-start(bf16[1,1,1,1,16,2816]{5,4,3,2,1,0:T(8,128)(2,1)S(1)} %slice_bitcast_fusion), channel_id=1, source_target_pairs={{0,8},{1,9},{2,18},{3,19},{4,12},{5,13},{6,22},{7,23},{8,0},{9,1},... | collective-permute-start | bytes 270344 | tf_op jit(solution)/shard_map/ppermute | solution.py:75
  10.5 6.2 %collective-permute-start.9 = (bf16[1,2,1,1,16,2048]{5,4,3,2,1,0:T(8,128)(2,1)S(1)}, bf16[1,2,1,1,16,2048]{5,4,3,2,1,0:T(8,128)(2,1)S(1)}, u32[]{:S(2)}, u32[]{:S(2)}) collective-permute-start(bf16[1,2,1,1,16,2048]{5,4,3,2,1,0:T(8,128)(2,1)S(1)} %pad_maximum_fusion.12), channel_id=1, source_target_pairs={{0,4},{1,5},{2,3},{3,2},{4,0},{5,1},{6,7},{7,6},{8,12},{9,13},{10,... | collective-permute-start | bytes 393224 | tf_op jit(solution)/shard_map/ppermute | solution.py:75
  12.3 6.3 %collective-permute-start.2 = (bf16[2,1,1,1,16,2432]{5,4,3,2,1,0:T(8,128)(2,1)S(1)}, bf16[2,1,1,1,16,2432]{5,4,3,2,1,0:T(8,128)(2,1)S(1)}, u32[]{:S(2)}, u32[]{:S(2)}) collective-permute-start(bf16[2,1,1,1,16,2432]{5,4,3,2,1,0:T(8,128)(2,1)S(1)} %pad_maximum_fusion.11), channel_id=1, source_target_pairs={{0,1},{1,0},{2,6},{3,7},{4,5},{5,4},{6,2},{7,3},{8,9},{9,8},{10,14... | collective-permute-start | bytes 466952 | tf_op jit(solution)/shard_map/ppermute | solution.py:75
  15.4 8.4 %collective-permute-start.6 = (bf16[1,2,1,1,16,2816]{5,4,3,2,1,0:T(8,128)(2,1)S(1)}, bf16[1,2,1,1,16,2816]{5,4,3,2,1,0:T(8,128)(2,1)S(1)}, u32[]{:S(2)}, u32[]{:S(2)}) collective-permute-start(bf16[1,2,1,1,16,2816]{5,4,3,2,1,0:T(8,128)(2,1)S(1)} %pad_maximum_fusion.10), channel_id=1, source_target_pairs={{0,16},{1,17},{2,10},{3,11},{4,20},{5,21},{6,14},{7,15},{8,24},{9,... | collective-permute-start | bytes 540680 | tf_op jit(solution)/shard_map/ppermute | solution.py:75
  16.7 29.4 %copy-start = (bf16[1,7168,512]{2,1,0:T(8,128)(2,1)S(1)}, bf16[1,7168,512]{2,1,0:T(8,128)(2,1)}, u32[]{:S(2)}) copy-start(bf16[1,7168,512]{2,1,0:T(8,128)(2,1)} %param.10) | copy-start | bytes 22020100
  16.8 19.8 %collective-permute-start.10 = (bf16[1,2,2,1,16,2048]{5,4,3,2,1,0:T(8,128)(2,1)S(1)}, bf16[1,2,2,1,16,2048]{5,4,3,2,1,0:T(8,128)(2,1)S(1)}, u32[]{:S(2)}, u32[]{:S(2)}) collective-permute-start(bf16[1,2,2,1,16,2048]{5,4,3,2,1,0:T(8,128)(2,1)S(1)} %pad_maximum_fusion.8), channel_id=1, source_target_pairs={{0,16},{1,17},{2,10},{3,11},{4,20},{5,21},{6,14},{7,15},{8,24},{9,... | collective-permute-start | bytes 786440 | tf_op jit(solution)/shard_map/ppermute | solution.py:75
  18.6 18.2 %collective-permute-start.3 = (bf16[2,1,1,2,16,2432]{5,4,3,2,1,0:T(8,128)(2,1)S(1)}, bf16[2,1,1,2,16,2432]{5,4,3,2,1,0:T(8,128)(2,1)S(1)}, u32[]{:S(2)}, u32[]{:S(2)}) collective-permute-start(bf16[2,1,1,2,16,2432]{5,4,3,2,1,0:T(8,128)(2,1)S(1)} %pad_maximum_fusion.7), channel_id=1, source_target_pairs={{0,4},{1,5},{2,3},{3,2},{4,0},{5,1},{6,7},{7,6},{8,12},{9,13},{10,... | collective-permute-start | bytes 933896 | tf_op jit(solution)/shard_map/ppermute | solution.py:75
  23.9 13.9 %collective-permute-start.7 = (bf16[2,2,1,1,16,2816]{5,4,3,2,1,0:T(8,128)(2,1)S(1)}, bf16[2,2,1,1,16,2816]{5,4,3,2,1,0:T(8,128)(2,1)S(1)}, u32[]{:S(2)}, u32[]{:S(2)}) collective-permute-start(bf16[2,2,1,1,16,2816]{5,4,3,2,1,0:T(8,128)(2,1)S(1)} %pad_maximum_fusion.6), channel_id=1, source_target_pairs={{0,1},{1,0},{2,6},{3,7},{4,5},{5,4},{6,2},{7,3},{8,9},{9,8},{10,14... | collective-permute-start | bytes 1081352 | tf_op jit(solution)/shard_map/ppermute | solution.py:75
  36.6 9.2 %collective-permute-start.11 = (bf16[2,2,2,1,16,2048]{5,4,3,2,1,0:T(8,128)(2,1)S(1)}, bf16[2,2,2,1,16,2048]{5,4,3,2,1,0:T(8,128)(2,1)S(1)}, u32[]{:S(2)}, u32[]{:S(2)}) collective-permute-start(bf16[2,2,2,1,16,2048]{5,4,3,2,1,0:T(8,128)(2,1)S(1)} %pad_maximum_fusion.5), channel_id=1, source_target_pairs={{0,1},{1,0},{2,6},{3,7},{4,5},{5,4},{6,2},{7,3},{8,9},{9,8},{10,14... | collective-permute-start | bytes 1572872 | tf_op jit(solution)/shard_map/ppermute | solution.py:75
  36.8 12.7 %collective-permute-start.4 = (bf16[2,1,2,2,16,2432]{5,4,3,2,1,0:T(8,128)(2,1)S(1)}, bf16[2,1,2,2,16,2432]{5,4,3,2,1,0:T(8,128)(2,1)S(1)}, u32[]{:S(2)}, u32[]{:S(2)}) collective-permute-start(bf16[2,1,2,2,16,2432]{5,4,3,2,1,0:T(8,128)(2,1)S(1)} %pad_maximum_fusion.4), channel_id=1, source_target_pairs={{0,8},{1,9},{2,18},{3,19},{4,12},{5,13},{6,22},{7,23},{8,0},{9,1},... | collective-permute-start | bytes 1867784 | tf_op jit(solution)/shard_map/ppermute | solution.py:75
  37.9 13.9 %collective-permute-start.8 = (bf16[2,2,1,2,16,2816]{5,4,3,2,1,0:T(8,128)(2,1)S(1)}, bf16[2,2,1,2,16,2816]{5,4,3,2,1,0:T(8,128)(2,1)S(1)}, u32[]{:S(2)}, u32[]{:S(2)}) collective-permute-start(bf16[2,2,1,2,16,2816]{5,4,3,2,1,0:T(8,128)(2,1)S(1)} %pad_maximum_fusion.3), channel_id=1, source_target_pairs={{0,4},{1,5},{2,3},{3,2},{4,0},{5,1},{6,7},{7,6},{8,12},{9,13},{10,... | collective-permute-start | bytes 2162696 | tf_op jit(solution)/shard_map/ppermute | solution.py:75
  46.0 6.1 %collective-permute-start.14 = (bf16[256,2048]{1,0:T(8,128)(2,1)S(1)}, bf16[256,2048]{1,0:T(8,128)(2,1)S(1)}, u32[]{:S(2)}, u32[]{:S(2)}) collective-permute-start(bf16[256,2048]{1,0:T(8,128)(2,1)S(1)} %bitcast.95), channel_id=1, source_target_pairs={{0,2},{1,3},{2,0},{3,1},{4,6},{5,7},{6,4},{7,5},{8,10},{9,11},{10,... | collective-permute-start | bytes 3145736 | tf_op jit(solution)/shard_map/ppermute | solution.py:75
  46.1 4.9 %slice-start = ((s8[7340032]{0:T(1024)(128)(4,1)}), s8[4194304]{0:T(1024)(128)(4,1)S(1)}, s32[]{:S(2)}) async-start(s8[7340032]{0:T(1024)(128)(4,1)} %bitcast.99), calls=%async_computation | async-start | bytes 8388608
  49.7 3.8 %collective-permute-start.12 = (bf16[256,2432]{1,0:T(8,128)(2,1)S(1)}, bf16[256,2432]{1,0:T(8,128)(2,1)S(1)}, u32[]{:S(2)}, u32[]{:S(2)}) collective-permute-start(bf16[256,2432]{1,0:T(8,128)(2,1)S(1)} %bitcast.85), channel_id=1, source_target_pairs={{0,2},{1,3},{2,0},{3,1},{4,6},{5,7},{6,4},{7,5},{8,10},{9,11},{10,... | collective-permute-start | bytes 3735560 | tf_op jit(solution)/shard_map/ppermute | solution.py:75
  52.0 3.3 %collective-permute-start.13 = (bf16[256,2816]{1,0:T(8,128)(2,1)S(1)}, bf16[256,2816]{1,0:T(8,128)(2,1)S(1)}, u32[]{:S(2)}, u32[]{:S(2)}) collective-permute-start(bf16[256,2816]{1,0:T(8,128)(2,1)S(1)} %bitcast.82), channel_id=1, source_target_pairs={{0,2},{1,3},{2,0},{3,1},{4,6},{5,7},{6,4},{7,5},{8,10},{9,11},{10,... | collective-permute-start | bytes 4325384 | tf_op jit(solution)/shard_map/ppermute | solution.py:75
  59.5 4.6 %collective-permute-start.15 = (bf16[256,2432]{1,0:T(8,128)(2,1)S(1)}, bf16[256,2432]{1,0:T(8,128)(2,1)S(1)}, u32[]{:S(2)}, u32[]{:S(2)}) collective-permute-start(bf16[256,2432]{1,0:T(8,128)(2,1)S(1)} %fusion), channel_id=1, source_target_pairs={{0,2},{1,3},{2,0},{3,1},{4,6},{5,7},{6,4},{7,5},{8,10},{9,11},{10,... | collective-permute-start | bytes 3735560 | tf_op jit(solution)/shard_map/ppermute | solution.py:75
  60.8 6.9 %collective-permute-start.18 = (bf16[256,2304]{1,0:T(8,128)(2,1)S(1)}, bf16[256,2304]{1,0:T(8,128)(2,1)S(1)}, u32[]{:S(2)}, u32[]{:S(2)}) collective-permute-start(bf16[256,2304]{1,0:T(8,128)(2,1)S(1)} %multiply_convert_fusion), channel_id=1, source_target_pairs={{0,2},{1,3},{2,0},{3,1},{4,6},{5,7},{6,4},{7,5},{8,10},{9,11},{10,... | collective-permute-start | bytes 3538952 | tf_op jit(solution)/shard_map/ppermute | solution.py:75
  61.8 7.8 %collective-permute-start.17 = (bf16[256,2432]{1,0:T(8,128)(2,1)S(1)}, bf16[256,2432]{1,0:T(8,128)(2,1)S(1)}, u32[]{:S(2)}, u32[]{:S(2)}) collective-permute-start(bf16[256,2432]{1,0:T(8,128)(2,1)S(1)} %fusion.1), channel_id=1, source_target_pairs={{0,2},{1,3},{2,0},{3,1},{4,6},{5,7},{6,4},{7,5},{8,10},{9,11},{10,... | collective-permute-start | bytes 3735560 | tf_op jit(solution)/shard_map/ppermute | solution.py:75
  65.1 13.5 %collective-permute-start.16 = (bf16[2,2,1,2,16,2432]{5,4,3,2,1,0:T(8,128)(2,1)S(1)}, bf16[2,2,1,2,16,2432]{5,4,3,2,1,0:T(8,128)(2,1)S(1)}, u32[]{:S(2)}, u32[]{:S(2)}) collective-permute-start(bf16[2,2,1,2,16,2432]{5,4,3,2,1,0:T(8,128)(2,1)S(1)} %slice.199), channel_id=1, source_target_pairs={{0,4},{1,5},{2,3},{3,2},{4,0},{5,1},{6,7},{7,6},{8,12},{9,13},{10,... | collective-permute-start | bytes 1867784 | tf_op jit(solution)/shard_map/ppermute | solution.py:75
  68.5 17.4 %collective-permute-start.23 = (bf16[2,1,2,2,16,2304]{5,4,3,2,1,0:T(8,128)(2,1)S(1)}, bf16[2,1,2,2,16,2304]{5,4,3,2,1,0:T(8,128)(2,1)S(1)}, u32[]{:S(2)}, u32[]{:S(2)}) collective-permute-start(bf16[2,1,2,2,16,2304]{5,4,3,2,1,0:T(8,128)(2,1)S(1)} %slice.211), channel_id=1, source_target_pairs={{0,8},{1,9},{2,18},{3,19},{4,12},{5,13},{6,22},{7,23},{8,0},{9,1},... | collective-permute-start | bytes 1769480 | tf_op jit(solution)/shard_map/ppermute | solution.py:75
  70.7 10.5 %collective-permute-start.20 = (bf16[2,2,2,1,16,2432]{5,4,3,2,1,0:T(8,128)(2,1)S(1)}, bf16[2,2,2,1,16,2432]{5,4,3,2,1,0:T(8,128)(2,1)S(1)}, u32[]{:S(2)}, u32[]{:S(2)}) collective-permute-start(bf16[2,2,2,1,16,2432]{5,4,3,2,1,0:T(8,128)(2,1)S(1)} %slice.205), channel_id=1, source_target_pairs={{0,1},{1,0},{2,6},{3,7},{4,5},{5,4},{6,2},{7,3},{8,9},{9,8},{10,14... | collective-permute-start | bytes 1867784 | tf_op jit(solution)/shard_map/ppermute | solution.py:75
  78.8 7.1 %collective-permute-start.19 = (bf16[2,2,1,1,16,2432]{5,4,3,2,1,0:T(8,128)(2,1)S(1)}, bf16[2,2,1,1,16,2432]{5,4,3,2,1,0:T(8,128)(2,1)S(1)}, u32[]{:S(2)}, u32[]{:S(2)}) collective-permute-start(bf16[2,2,1,1,16,2432]{5,4,3,2,1,0:T(8,128)(2,1)S(1)} %slice.203), channel_id=1, source_target_pairs={{0,1},{1,0},{2,6},{3,7},{4,5},{5,4},{6,2},{7,3},{8,9},{9,8},{10,14... | collective-permute-start | bytes 933896 | tf_op jit(solution)/shard_map/ppermute | solution.py:75
  81.4 10.1 %collective-permute-start.22 = (bf16[2,2,1,1,16,2432]{5,4,3,2,1,0:T(8,128)(2,1)S(1)}, bf16[2,2,1,1,16,2432]{5,4,3,2,1,0:T(8,128)(2,1)S(1)}, u32[]{:S(2)}, u32[]{:S(2)}) collective-permute-start(bf16[2,2,1,1,16,2432]{5,4,3,2,1,0:T(8,128)(2,1)S(1)} %slice.209), channel_id=1, source_target_pairs={{0,4},{1,5},{2,3},{3,2},{4,0},{5,1},{6,7},{7,6},{8,12},{9,13},{10,... | collective-permute-start | bytes 933896 | tf_op jit(solution)/shard_map/ppermute | solution.py:75
  86.1 11.8 %collective-permute-start.21 = (bf16[1,2,1,1,16,2432]{5,4,3,2,1,0:T(8,128)(2,1)S(1)}, bf16[1,2,1,1,16,2432]{5,4,3,2,1,0:T(8,128)(2,1)S(1)}, u32[]{:S(2)}, u32[]{:S(2)}) collective-permute-start(bf16[1,2,1,1,16,2432]{5,4,3,2,1,0:T(8,128)(2,1)S(1)} %slice.207), channel_id=1, source_target_pairs={{0,16},{1,17},{2,10},{3,11},{4,20},{5,21},{6,14},{7,15},{8,24},{9,... | collective-permute-start | bytes 466952 | tf_op jit(solution)/shard_map/ppermute | solution.py:75
  89.1 11.0 %collective-permute-start.26 = (bf16[2,1,1,2,16,2304]{5,4,3,2,1,0:T(8,128)(2,1)S(1)}, bf16[2,1,1,2,16,2304]{5,4,3,2,1,0:T(8,128)(2,1)S(1)}, u32[]{:S(2)}, u32[]{:S(2)}) collective-permute-start(bf16[2,1,1,2,16,2304]{5,4,3,2,1,0:T(8,128)(2,1)S(1)} %slice.217), channel_id=1, source_target_pairs={{0,4},{1,5},{2,3},{3,2},{4,0},{5,1},{6,7},{7,6},{8,12},{9,13},{10,... | collective-permute-start | bytes 884744 | tf_op jit(solution)/shard_map/ppermute | solution.py:75
  91.6 10.3 %collective-permute-start.25 = (bf16[2,1,1,1,16,2432]{5,4,3,2,1,0:T(8,128)(2,1)S(1)}, bf16[2,1,1,1,16,2432]{5,4,3,2,1,0:T(8,128)(2,1)S(1)}, u32[]{:S(2)}, u32[]{:S(2)}) collective-permute-start(bf16[2,1,1,1,16,2432]{5,4,3,2,1,0:T(8,128)(2,1)S(1)} %slice.215), channel_id=1, source_target_pairs={{0,8},{1,9},{2,18},{3,19},{4,12},{5,13},{6,22},{7,23},{8,0},{9,1},... | collective-permute-start | bytes 466952 | tf_op jit(solution)/shard_map/ppermute | solution.py:75
  98.0 4.7 %collective-permute-start.24 = (bf16[1,1,1,1,16,2432]{5,4,3,2,1,0:T(8,128)(2,1)S(1)}, bf16[1,1,1,1,16,2432]{5,4,3,2,1,0:T(8,128)(2,1)S(1)}, u32[]{:S(2)}, u32[]{:S(2)}) collective-permute-start(bf16[1,1,1,1,16,2432]{5,4,3,2,1,0:T(8,128)(2,1)S(1)} %slice.213), channel_id=1, source_target_pairs={{0,8},{1,9},{2,18},{3,19},{4,12},{5,13},{6,22},{7,23},{8,0},{9,1},... | collective-permute-start | bytes 233480 | tf_op jit(solution)/shard_map/ppermute | solution.py:75
  100.2 6.2 %collective-permute-start.27 = (bf16[2,1,1,1,16,2304]{5,4,3,2,1,0:T(8,128)(2,1)S(1)}, bf16[2,1,1,1,16,2304]{5,4,3,2,1,0:T(8,128)(2,1)S(1)}, u32[]{:S(2)}, u32[]{:S(2)}) collective-permute-start(bf16[2,1,1,1,16,2304]{5,4,3,2,1,0:T(8,128)(2,1)S(1)} %slice.219), channel_id=1, source_target_pairs={{0,1},{1,0},{2,6},{3,7},{4,5},{5,4},{6,2},{7,3},{8,9},{9,8},{10,14... | collective-permute-start | bytes 442376 | tf_op jit(solution)/shard_map/ppermute | solution.py:75
  102.7 6.1 %collective-permute-start.29 = (bf16[1,1,1,1,16,2432]{5,4,3,2,1,0:T(8,128)(2,1)S(1)}, bf16[1,1,1,1,16,2432]{5,4,3,2,1,0:T(8,128)(2,1)S(1)}, u32[]{:S(2)}, u32[]{:S(2)}) collective-permute-start(bf16[1,1,1,1,16,2432]{5,4,3,2,1,0:T(8,128)(2,1)S(1)} %slice.223), channel_id=1, source_target_pairs={{0,16},{1,17},{2,10},{3,11},{4,20},{5,21},{6,14},{7,15},{8,24},{9,... | collective-permute-start | bytes 233480 | tf_op jit(solution)/shard_map/ppermute | solution.py:75
  106.5 5.3 %collective-permute-start.28 = (bf16[1,1,1,1,16,2304]{5,4,3,2,1,0:T(8,128)(2,1)S(1)}, bf16[1,1,1,1,16,2304]{5,4,3,2,1,0:T(8,128)(2,1)S(1)}, u32[]{:S(2)}, u32[]{:S(2)}) collective-permute-start(bf16[1,1,1,1,16,2304]{5,4,3,2,1,0:T(8,128)(2,1)S(1)} %slice.221), channel_id=1, source_target_pairs={{0,16},{1,17},{2,10},{3,11},{4,20},{5,21},{6,14},{7,15},{8,24},{9,... | collective-permute-start | bytes 221192 | tf_op jit(solution)/shard_map/ppermute | solution.py:75
  (3 other events, 8.9 us)

commit v5 on v2

--- a/solution.py
+++ b/solution.py
@@ -88,7 +88,7 @@
 )
 GATHER_TURNS = (10, 1, 12, 10, 11, 2, 10, 11, 12, 10, 12, 11, 10, 10, 10, 12, 11, 11, 12, 11, 12)
 SCATTER_TURNS = (0, 11, 2, 0, 2, 0, 1, 2, 0, 1, 2, 0, 1, 2, 11)
-PACKED = 2
+PACKED = 0
 
 
 def chunks_of(width, plan):

time: 112 us -> 114 us (1.018)
  waiting for transfers between devices: 40.6 us -> 48.7 us
  starting transfers between devices: 45.6 us -> 39.6 us
    ppermute x30, waiting for transfers between devices: 40.6 us -> 48.7 us  [exchange(): return lax.ppermute(block, AXES, perm)]
    ppermute x30, starting transfers between devices: 45.6 us -> 39.6 us  [exchange(): return lax.ppermute(block, AXES, perm)]
where the time goes in v5:
time: 114 us
  waiting for transfers between devices  48.7 us (43%)
  starting transfers between devices  39.6 us (35%)
  matrix products  16.6 us (15%)
  local copies, waits for them, and re-layouts  5.92 us (5%)
  other arithmetic  2.68 us (2%)
    ppermute x30, waiting for transfers between devices, exchange(): return lax.ppermute(block, AXES, perm)  48.7 us
    ppermute x30, starting transfers between devices, exchange(): return lax.ppermute(block, AXES, perm)  39.6 us
    dot_general x6, matrix products, products(): jnp.dot(rows, w_gate[lo:hi], preferred_element_type=jnp.float32)  6.53 us
    dot_general x6, matrix products, product(): jnp.dot(hidden[j], w_down[:, lo:hi], preferred_element_type=jnp.float32)  5.24 us
    dot_general x6, matrix products, products(): jnp.dot(rows, w_up[lo:hi], preferred_element_type=jnp.float32)  4.85 us
    unnamed x12, local copies, waits for them, and re-layouts  3.03 us
  transfers between devices with their start and end apart: 30, of which 14 were waited for; matrix products, arithmetic and copies ran while one was open for 17% of the time, Pallas kernels for 0%

profile of v5, /device:TPU:0, one launch (start us, length us, event | category | flops | bytes accessed | tf_op | source)
XLA Modules:
  0.0 114.1 jit_solution(3234439286420518395)
XLA Ops:
  0.8 3.0 %collective-permute-start.4 = (bf16[1,1,1,1,16,2048]{5,4,3,2,1,0:T(8,128)(2,1)S(1)}, bf16[1,1,1,1,16,2048]{5,4,3,2,1,0:T(8,128)(2,1)S(1)}, u32[]{:S(2)}, u32[]{:S(2)}) collective-permute-start(bf16[1,1,1,1,16,2048]{5,4,3,2,1,0:T(8,128)(2,1)S(1)} %slice_bitcast_fusion.1), channel_id=1, source_target_pairs={{0,8},{1,9},{2,18},{3,19},{4,12},{5,13},{6,22},{7,23},{8,0},{9,1},... | collective-permute-start | bytes 196616 | tf_op jit(solution)/shard_map/ppermute | solution.py:75
  4.8 2.6 %collective-permute-start.8 = (bf16[1,1,1,1,16,2304]{5,4,3,2,1,0:T(8,128)(2,1)S(1)}, bf16[1,1,1,1,16,2304]{5,4,3,2,1,0:T(8,128)(2,1)S(1)}, u32[]{:S(2)}, u32[]{:S(2)}) collective-permute-start(bf16[1,1,1,1,16,2304]{5,4,3,2,1,0:T(8,128)(2,1)S(1)} %slice_bitcast_fusion), channel_id=1, source_target_pairs={{0,16},{1,17},{2,10},{3,11},{4,20},{5,21},{6,14},{7,15},{8,24},{9,... | collective-permute-start | bytes 221192 | tf_op jit(solution)/shard_map/ppermute | solution.py:75
  10.5 1.6 %collective-permute-start.5 = (bf16[1,2,1,1,16,2048]{5,4,3,2,1,0:T(8,128)(2,1)S(1)}, bf16[1,2,1,1,16,2048]{5,4,3,2,1,0:T(8,128)(2,1)S(1)}, u32[]{:S(2)}, u32[]{:S(2)}) collective-permute-start(bf16[1,2,1,1,16,2048]{5,4,3,2,1,0:T(8,128)(2,1)S(1)} %pad_maximum_fusion.12), channel_id=1, source_target_pairs={{0,1},{1,0},{2,6},{3,7},{4,5},{5,4},{6,2},{7,3},{8,9},{9,8},{10,14... | collective-permute-start | bytes 393224 | tf_op jit(solution)/shard_map/ppermute | solution.py:75
  12.7 2.8 %collective-permute-done = bf16[1,1,1,1,16,2944]{5,4,3,2,1,0:T(8,128)(2,1)S(1)} collective-permute-done((bf16[1,1,1,1,16,2944]{5,4,3,2,1,0:T(8,128)(2,1)S(1)}, bf16[1,1,1,1,16,2944]{5,4,3,2,1,0:T(8,128)(2,1)S(1)}, u32[]{:S(2)}, u32[]{:S(2)}) %collective-permute-start) | collective-permute-done | bytes 94240 | tf_op jit(solution)/shard_map/ppermute | solution.py:75
  15.7 3.0 %collective-permute-start.6 = (bf16[1,2,1,2,16,2048]{5,4,3,2,1,0:T(8,128)(2,1)S(1)}, bf16[1,2,1,2,16,2048]{5,4,3,2,1,0:T(8,128)(2,1)S(1)}, u32[]{:S(2)}, u32[]{:S(2)}) collective-permute-start(bf16[1,2,1,2,16,2048]{5,4,3,2,1,0:T(8,128)(2,1)S(1)} %pad_maximum_fusion.8), channel_id=1, source_target_pairs={{0,16},{1,17},{2,10},{3,11},{4,20},{5,21},{6,14},{7,15},{8,24},{9,... | collective-permute-start | bytes 786440 | tf_op jit(solution)/shard_map/ppermute | solution.py:75
  18.6 1.6 %collective-permute-start.10 = (bf16[2,1,1,2,16,2304]{5,4,3,2,1,0:T(8,128)(2,1)S(1)}, bf16[2,1,1,2,16,2304]{5,4,3,2,1,0:T(8,128)(2,1)S(1)}, u32[]{:S(2)}, u32[]{:S(2)}) collective-permute-start(bf16[2,1,1,2,16,2304]{5,4,3,2,1,0:T(8,128)(2,1)S(1)} %pad_maximum_fusion.7), channel_id=1, source_target_pairs={{0,4},{1,5},{2,3},{3,2},{4,0},{5,1},{6,7},{7,6},{8,12},{9,13},{10,... | collective-permute-start | bytes 884744 | tf_op jit(solution)/shard_map/ppermute | solution.py:75
  20.2 6.2 %collective-permute-done.1 = bf16[1,2,1,1,16,2944]{5,4,3,2,1,0:T(8,128)(2,1)S(1)} collective-permute-done((bf16[1,2,1,1,16,2944]{5,4,3,2,1,0:T(8,128)(2,1)S(1)}, bf16[1,2,1,1,16,2944]{5,4,3,2,1,0:T(8,128)(2,1)S(1)}, u32[]{:S(2)}, u32[]{:S(2)}) %collective-permute-start.1) | collective-permute-done | bytes 188448 | tf_op jit(solution)/shard_map/ppermute | solution.py:75
  26.5 1.6 %collective-permute-start.2 = (bf16[2,2,1,1,16,2944]{5,4,3,2,1,0:T(8,128)(2,1)S(1)}, bf16[2,2,1,1,16,2944]{5,4,3,2,1,0:T(8,128)(2,1)S(1)}, u32[]{:S(2)}, u32[]{:S(2)}) collective-permute-start(bf16[2,2,1,1,16,2944]{5,4,3,2,1,0:T(8,128)(2,1)S(1)} %pad_maximum_fusion.6), channel_id=1, source_target_pairs={{0,1},{1,0},{2,6},{3,7},{4,5},{5,4},{6,2},{7,3},{8,9},{9,8},{10,14... | collective-permute-start | bytes 1130504 | tf_op jit(solution)/shard_map/ppermute | solution.py:75
  28.0 1.3 %collective-permute-done.6 = bf16[1,2,1,2,16,2048]{5,4,3,2,1,0:T(8,128)(2,1)S(1)} collective-permute-done((bf16[1,2,1,2,16,2048]{5,4,3,2,1,0:T(8,128)(2,1)S(1)}, bf16[1,2,1,2,16,2048]{5,4,3,2,1,0:T(8,128)(2,1)S(1)}, u32[]{:S(2)}, u32[]{:S(2)}) %collective-permute-start.6) | collective-permute-done | bytes 262176 | tf_op jit(solution)/shard_map/ppermute | solution.py:75
  29.4 1.6 %collective-permute-start.7 = (bf16[2,2,1,2,16,2048]{5,4,3,2,1,0:T(8,128)(2,1)S(1)}, bf16[2,2,1,2,16,2048]{5,4,3,2,1,0:T(8,128)(2,1)S(1)}, u32[]{:S(2)}, u32[]{:S(2)}) collective-permute-start(bf16[2,2,1,2,16,2048]{5,4,3,2,1,0:T(8,128)(2,1)S(1)} %pad_maximum_fusion.5), channel_id=1, source_target_pairs={{0,4},{1,5},{2,3},{3,2},{4,0},{5,1},{6,7},{7,6},{8,12},{9,13},{10,... | collective-permute-start | bytes 1572872 | tf_op jit(solution)/shard_map/ppermute | solution.py:75
  31.1 7.1 %collective-permute-done.2 = bf16[2,2,1,1,16,2944]{5,4,3,2,1,0:T(8,128)(2,1)S(1)} collective-permute-done((bf16[2,2,1,1,16,2944]{5,4,3,2,1,0:T(8,128)(2,1)S(1)}, bf16[2,2,1,1,16,2944]{5,4,3,2,1,0:T(8,128)(2,1)S(1)}, u32[]{:S(2)}, u32[]{:S(2)}) %collective-permute-start.2) | collective-permute-done | bytes 376864 | tf_op jit(solution)/shard_map/ppermute | solution.py:75
  38.3 1.6 %collective-permute-start.3 = (bf16[2,2,1,2,16,2944]{5,4,3,2,1,0:T(8,128)(2,1)S(1)}, bf16[2,2,1,2,16,2944]{5,4,3,2,1,0:T(8,128)(2,1)S(1)}, u32[]{:S(2)}, u32[]{:S(2)}) collective-permute-start(bf16[2,2,1,2,16,2944]{5,4,3,2,1,0:T(8,128)(2,1)S(1)} %pad_maximum_fusion.3), channel_id=1, source_target_pairs={{0,4},{1,5},{2,3},{3,2},{4,0},{5,1},{6,7},{7,6},{8,12},{9,13},{10,... | collective-permute-start | bytes 2261000 | tf_op jit(solution)/shard_map/ppermute | solution.py:75
  40.9 2.5 %fusion.32 = f32[256,512]{1,0:T(8,128)S(1)} fusion(bf16[256,2048]{1,0:T(8,128)(2,1)S(1)} %bitcast.97, bf16[1,7168,512]{2,1,0:T(8,128)(2,1)} %param.9), kind=kOutput, calls=%fused_computation.41 | convolution fusion | flops 536870912 | bytes 3670016 | tf_op jit(solution)/shard_map/dot_general | solution.py:115
  43.3 2.5 %collective-permute-done.11 = bf16[2,1,2,2,16,2304]{5,4,3,2,1,0:T(8,128)(2,1)S(1)} collective-permute-done((bf16[2,1,2,2,16,2304]{5,4,3,2,1,0:T(8,128)(2,1)S(1)}, bf16[2,1,2,2,16,2304]{5,4,3,2,1,0:T(8,128)(2,1)S(1)}, u32[]{:S(2)}, u32[]{:S(2)}) %collective-permute-start.11) | collective-permute-done | bytes 589856 | tf_op jit(solution)/shard_map/ppermute | solution.py:75
  46.8 3.2 %collective-permute-done.3 = bf16[2,2,1,2,16,2944]{5,4,3,2,1,0:T(8,128)(2,1)S(1)} collective-permute-done((bf16[2,2,1,2,16,2944]{5,4,3,2,1,0:T(8,128)(2,1)S(1)}, bf16[2,2,1,2,16,2944]{5,4,3,2,1,0:T(8,128)(2,1)S(1)}, u32[]{:S(2)}, u32[]{:S(2)}) %collective-permute-start.3) | collective-permute-done | bytes 753696 | tf_op jit(solution)/shard_map/ppermute | solution.py:75
  55.2 1.0 multiply_convert_fusion.1
  56.4 1.2 %slice-done.3 = s8[3145728]{0:T(1024)(128)(4,1)S(1)} async-done(((s8[7340032]{0:T(1024)(128)(4,1)}), s8[3145728]{0:T(1024)(128)(4,1)S(1)}, s32[]{:S(2)}) %slice-start.3) | async-done | bytes 3145752
  62.2 1.0 multiply_convert_fusion.2
  64.2 1.6 %collective-permute-start.16 = (bf16[2,2,1,2,16,2432]{5,4,3,2,1,0:T(8,128)(2,1)S(1)}, bf16[2,2,1,2,16,2432]{5,4,3,2,1,0:T(8,128)(2,1)S(1)}, u32[]{:S(2)}, u32[]{:S(2)}) collective-permute-start(bf16[2,2,1,2,16,2432]{5,4,3,2,1,0:T(8,128)(2,1)S(1)} %slice.199), channel_id=1, source_target_pairs={{0,4},{1,5},{2,3},{3,2},{4,0},{5,1},{6,7},{7,6},{8,12},{9,13},{10,... | collective-permute-start | bytes 1867784 | tf_op jit(solution)/shard_map/ppermute | solution.py:75
  66.7 1.1 add_convert_fusion
  68.4 6.1 %collective-permute-done.16 = bf16[2,2,1,2,16,2432]{5,4,3,2,1,0:T(8,128)(2,1)S(1)} collective-permute-done((bf16[2,2,1,2,16,2432]{5,4,3,2,1,0:T(8,128)(2,1)S(1)}, bf16[2,2,1,2,16,2432]{5,4,3,2,1,0:T(8,128)(2,1)S(1)}, u32[]{:S(2)}, u32[]{:S(2)}) %collective-permute-start.16) | collective-permute-done | bytes 622624 | tf_op jit(solution)/shard_map/ppermute | solution.py:75
  74.6 5.5 %collective-permute-start.19 = (bf16[2,2,1,1,16,2432]{5,4,3,2,1,0:T(8,128)(2,1)S(1)}, bf16[2,2,1,1,16,2432]{5,4,3,2,1,0:T(8,128)(2,1)S(1)}, u32[]{:S(2)}, u32[]{:S(2)}) collective-permute-start(bf16[2,2,1,1,16,2432]{5,4,3,2,1,0:T(8,128)(2,1)S(1)} %slice.203), channel_id=1, source_target_pairs={{0,1},{1,0},{2,6},{3,7},{4,5},{5,4},{6,2},{7,3},{8,9},{9,8},{10,14... | collective-permute-start | bytes 933896 | tf_op jit(solution)/shard_map/ppermute | solution.py:75
  80.1 1.9 %collective-permute-done.20 = bf16[2,2,1,2,16,2432]{5,4,3,2,1,0:T(8,128)(2,1)S(1)} collective-permute-done((bf16[2,2,1,2,16,2432]{5,4,3,2,1,0:T(8,128)(2,1)S(1)}, bf16[2,2,1,2,16,2432]{5,4,3,2,1,0:T(8,128)(2,1)S(1)}, u32[]{:S(2)}, u32[]{:S(2)}) %collective-permute-start.20) | collective-permute-done | bytes 622624 | tf_op jit(solution)/shard_map/ppermute | solution.py:75
  82.2 7.9 %collective-permute-start.22 = (bf16[2,2,1,1,16,2432]{5,4,3,2,1,0:T(8,128)(2,1)S(1)}, bf16[2,2,1,1,16,2432]{5,4,3,2,1,0:T(8,128)(2,1)S(1)}, u32[]{:S(2)}, u32[]{:S(2)}) collective-permute-start(bf16[2,2,1,1,16,2432]{5,4,3,2,1,0:T(8,128)(2,1)S(1)} %slice.209), channel_id=1, source_target_pairs={{0,1},{1,0},{2,6},{3,7},{4,5},{5,4},{6,2},{7,3},{8,9},{9,8},{10,14... | collective-permute-start | bytes 933896 | tf_op jit(solution)/shard_map/ppermute | solution.py:75
  90.5 1.6 %collective-permute-start.26 = (bf16[2,1,1,2,16,2304]{5,4,3,2,1,0:T(8,128)(2,1)S(1)}, bf16[2,1,1,2,16,2304]{5,4,3,2,1,0:T(8,128)(2,1)S(1)}, u32[]{:S(2)}, u32[]{:S(2)}) collective-permute-start(bf16[2,1,1,2,16,2304]{5,4,3,2,1,0:T(8,128)(2,1)S(1)} %slice.217), channel_id=1, source_target_pairs={{0,4},{1,5},{2,3},{3,2},{4,0},{5,1},{6,7},{7,6},{8,12},{9,13},{10,... | collective-permute-start | bytes 884744 | tf_op jit(solution)/shard_map/ppermute | solution.py:75
  92.1 5.1 %collective-permute-done.22 = bf16[2,2,1,1,16,2432]{5,4,3,2,1,0:T(8,128)(2,1)S(1)} collective-permute-done((bf16[2,2,1,1,16,2432]{5,4,3,2,1,0:T(8,128)(2,1)S(1)}, bf16[2,2,1,1,16,2432]{5,4,3,2,1,0:T(8,128)(2,1)S(1)}, u32[]{:S(2)}, u32[]{:S(2)}) %collective-permute-start.22) | collective-permute-done | bytes 311328 | tf_op jit(solution)/shard_map/ppermute | solution.py:75
  97.3 3.6 %collective-permute-done.21 = bf16[1,2,1,1,16,2432]{5,4,3,2,1,0:T(8,128)(2,1)S(1)} collective-permute-done((bf16[1,2,1,1,16,2432]{5,4,3,2,1,0:T(8,128)(2,1)S(1)}, bf16[1,2,1,1,16,2432]{5,4,3,2,1,0:T(8,128)(2,1)S(1)}, u32[]{:S(2)}, u32[]{:S(2)}) %collective-permute-start.21) | collective-permute-done | bytes 155680 | tf_op jit(solution)/shard_map/ppermute | solution.py:75
  101.3 2.3 %collective-permute-done.25 = bf16[2,1,1,1,16,2432]{5,4,3,2,1,0:T(8,128)(2,1)S(1)} collective-permute-done((bf16[2,1,1,1,16,2432]{5,4,3,2,1,0:T(8,128)(2,1)S(1)}, bf16[2,1,1,1,16,2432]{5,4,3,2,1,0:T(8,128)(2,1)S(1)}, u32[]{:S(2)}, u32[]{:S(2)}) %collective-permute-start.25) | collective-permute-done | bytes 155680 | tf_op jit(solution)/shard_map/ppermute | solution.py:75
  103.6 2.7 %collective-permute-done.24 = bf16[1,1,1,1,16,2432]{5,4,3,2,1,0:T(8,128)(2,1)S(1)} collective-permute-done((bf16[1,1,1,1,16,2432]{5,4,3,2,1,0:T(8,128)(2,1)S(1)}, bf16[1,1,1,1,16,2432]{5,4,3,2,1,0:T(8,128)(2,1)S(1)}, u32[]{:S(2)}, u32[]{:S(2)}) %collective-permute-start.24) | collective-permute-done | bytes 77856 | tf_op jit(solution)/shard_map/ppermute | solution.py:75
  106.5 3.0 %collective-permute-start.28 = (bf16[1,1,1,1,16,2304]{5,4,3,2,1,0:T(8,128)(2,1)S(1)}, bf16[1,1,1,1,16,2304]{5,4,3,2,1,0:T(8,128)(2,1)S(1)}, u32[]{:S(2)}, u32[]{:S(2)}) collective-permute-start(bf16[1,1,1,1,16,2304]{5,4,3,2,1,0:T(8,128)(2,1)S(1)} %slice.221), channel_id=1, source_target_pairs={{0,16},{1,17},{2,10},{3,11},{4,20},{5,21},{6,14},{7,15},{8,24},{9,... | collective-permute-start | bytes 221192 | tf_op jit(solution)/shard_map/ppermute | solution.py:75
  109.4 2.4 %collective-permute-done.29 = bf16[1,1,1,1,16,2432]{5,4,3,2,1,0:T(8,128)(2,1)S(1)} collective-permute-done((bf16[1,1,1,1,16,2432]{5,4,3,2,1,0:T(8,128)(2,1)S(1)}, bf16[1,1,1,1,16,2432]{5,4,3,2,1,0:T(8,128)(2,1)S(1)}, u32[]{:S(2)}, u32[]{:S(2)}) %collective-permute-start.29) | collective-permute-done | bytes 77856 | tf_op jit(solution)/shard_map/ppermute | solution.py:75
  111.8 1.6 %collective-permute-done.28 = bf16[1,1,1,1,16,2304]{5,4,3,2,1,0:T(8,128)(2,1)S(1)} collective-permute-done((bf16[1,1,1,1,16,2304]{5,4,3,2,1,0:T(8,128)(2,1)S(1)}, bf16[1,1,1,1,16,2304]{5,4,3,2,1,0:T(8,128)(2,1)S(1)}, u32[]{:S(2)}, u32[]{:S(2)}) %collective-permute-start.28) | collective-permute-done | bytes 73760 | tf_op jit(solution)/shard_map/ppermute | solution.py:75
  (106 shorter events, 22.2 us)
Async XLA Ops:
  0.8 9.7 %collective-permute-start.4 = (bf16[1,1,1,1,16,2048]{5,4,3,2,1,0:T(8,128)(2,1)S(1)}, bf16[1,1,1,1,16,2048]{5,4,3,2,1,0:T(8,128)(2,1)S(1)}, u32[]{:S(2)}, u32[]{:S(2)}) collective-permute-start(bf16[1,1,1,1,16,2048]{5,4,3,2,1,0:T(8,128)(2,1)S(1)} %slice_bitcast_fusion.1), channel_id=1, source_target_pairs={{0,8},{1,9},{2,18},{3,19},{4,12},{5,13},{6,22},{7,23},{8,0},{9,1},... | collective-permute-start | bytes 196616 | tf_op jit(solution)/shard_map/ppermute | solution.py:75
  4.8 7.3 %collective-permute-start.8 = (bf16[1,1,1,1,16,2304]{5,4,3,2,1,0:T(8,128)(2,1)S(1)}, bf16[1,1,1,1,16,2304]{5,4,3,2,1,0:T(8,128)(2,1)S(1)}, u32[]{:S(2)}, u32[]{:S(2)}) collective-permute-start(bf16[1,1,1,1,16,2304]{5,4,3,2,1,0:T(8,128)(2,1)S(1)} %slice_bitcast_fusion), channel_id=1, source_target_pairs={{0,16},{1,17},{2,10},{3,11},{4,20},{5,21},{6,14},{7,15},{8,24},{9,... | collective-permute-start | bytes 221192 | tf_op jit(solution)/shard_map/ppermute | solution.py:75
  10.0 5.5 %collective-permute-start = (bf16[1,1,1,1,16,2944]{5,4,3,2,1,0:T(8,128)(2,1)S(1)}, bf16[1,1,1,1,16,2944]{5,4,3,2,1,0:T(8,128)(2,1)S(1)}, u32[]{:S(2)}, u32[]{:S(2)}) collective-permute-start(bf16[1,1,1,1,16,2944]{5,4,3,2,1,0:T(8,128)(2,1)S(1)} %maximum_bitcast_fusion), channel_id=1, source_target_pairs={{0,8},{1,9},{2,18},{3,19},{4,12},{5,13},{6,22},{7,23},{8,0},{9,1},... | collective-permute-start | bytes 282632 | tf_op jit(solution)/shard_map/ppermute | solution.py:75
  10.5 5.1 %collective-permute-start.5 = (bf16[1,2,1,1,16,2048]{5,4,3,2,1,0:T(8,128)(2,1)S(1)}, bf16[1,2,1,1,16,2048]{5,4,3,2,1,0:T(8,128)(2,1)S(1)}, u32[]{:S(2)}, u32[]{:S(2)}) collective-permute-start(bf16[1,2,1,1,16,2048]{5,4,3,2,1,0:T(8,128)(2,1)S(1)} %pad_maximum_fusion.12), channel_id=1, source_target_pairs={{0,1},{1,0},{2,6},{3,7},{4,5},{5,4},{6,2},{7,3},{8,9},{9,8},{10,14... | collective-permute-start | bytes 393224 | tf_op jit(solution)/shard_map/ppermute | solution.py:75
  12.1 6.5 %collective-permute-start.9 = (bf16[2,1,1,1,16,2304]{5,4,3,2,1,0:T(8,128)(2,1)S(1)}, bf16[2,1,1,1,16,2304]{5,4,3,2,1,0:T(8,128)(2,1)S(1)}, u32[]{:S(2)}, u32[]{:S(2)}) collective-permute-start(bf16[2,1,1,1,16,2304]{5,4,3,2,1,0:T(8,128)(2,1)S(1)} %pad_maximum_fusion.11), channel_id=1, source_target_pairs={{0,1},{1,0},{2,6},{3,7},{4,5},{5,4},{6,2},{7,3},{8,9},{9,8},{10,14... | collective-permute-start | bytes 442376 | tf_op jit(solution)/shard_map/ppermute | solution.py:75
  15.5 10.9 %collective-permute-start.1 = (bf16[1,2,1,1,16,2944]{5,4,3,2,1,0:T(8,128)(2,1)S(1)}, bf16[1,2,1,1,16,2944]{5,4,3,2,1,0:T(8,128)(2,1)S(1)}, u32[]{:S(2)}, u32[]{:S(2)}) collective-permute-start(bf16[1,2,1,1,16,2944]{5,4,3,2,1,0:T(8,128)(2,1)S(1)} %pad_maximum_fusion.10), channel_id=1, source_target_pairs={{0,16},{1,17},{2,10},{3,11},{4,20},{5,21},{6,14},{7,15},{8,24},{9,... | collective-permute-start | bytes 565256 | tf_op jit(solution)/shard_map/ppermute | solution.py:75
  15.6 24.5 %copy-start = (bf16[1,7168,512]{2,1,0:T(8,128)(2,1)S(1)}, bf16[1,7168,512]{2,1,0:T(8,128)(2,1)}, u32[]{:S(2)}) copy-start(bf16[1,7168,512]{2,1,0:T(8,128)(2,1)} %param.10) | copy-start | bytes 22020100
  15.7 13.7 %collective-permute-start.6 = (bf16[1,2,1,2,16,2048]{5,4,3,2,1,0:T(8,128)(2,1)S(1)}, bf16[1,2,1,2,16,2048]{5,4,3,2,1,0:T(8,128)(2,1)S(1)}, u32[]{:S(2)}, u32[]{:S(2)}) collective-permute-start(bf16[1,2,1,2,16,2048]{5,4,3,2,1,0:T(8,128)(2,1)S(1)} %pad_maximum_fusion.8), channel_id=1, source_target_pairs={{0,16},{1,17},{2,10},{3,11},{4,20},{5,21},{6,14},{7,15},{8,24},{9,... | collective-permute-start | bytes 786440 | tf_op jit(solution)/shard_map/ppermute | solution.py:75
  18.6 12.3 %collective-permute-start.10 = (bf16[2,1,1,2,16,2304]{5,4,3,2,1,0:T(8,128)(2,1)S(1)}, bf16[2,1,1,2,16,2304]{5,4,3,2,1,0:T(8,128)(2,1)S(1)}, u32[]{:S(2)}, u32[]{:S(2)}) collective-permute-start(bf16[2,1,1,2,16,2304]{5,4,3,2,1,0:T(8,128)(2,1)S(1)} %pad_maximum_fusion.7), channel_id=1, source_target_pairs={{0,4},{1,5},{2,3},{3,2},{4,0},{5,1},{6,7},{7,6},{8,12},{9,13},{10,... | collective-permute-start | bytes 884744 | tf_op jit(solution)/shard_map/ppermute | solution.py:75
  26.5 11.8 %collective-permute-start.2 = (bf16[2,2,1,1,16,2944]{5,4,3,2,1,0:T(8,128)(2,1)S(1)}, bf16[2,2,1,1,16,2944]{5,4,3,2,1,0:T(8,128)(2,1)S(1)}, u32[]{:S(2)}, u32[]{:S(2)}) collective-permute-start(bf16[2,2,1,1,16,2944]{5,4,3,2,1,0:T(8,128)(2,1)S(1)} %pad_maximum_fusion.6), channel_id=1, source_target_pairs={{0,1},{1,0},{2,6},{3,7},{4,5},{5,4},{6,2},{7,3},{8,9},{9,8},{10,14... | collective-permute-start | bytes 1130504 | tf_op jit(solution)/shard_map/ppermute | solution.py:75
  29.4 10.5 %collective-permute-start.7 = (bf16[2,2,1,2,16,2048]{5,4,3,2,1,0:T(8,128)(2,1)S(1)}, bf16[2,2,1,2,16,2048]{5,4,3,2,1,0:T(8,128)(2,1)S(1)}, u32[]{:S(2)}, u32[]{:S(2)}) collective-permute-start(bf16[2,2,1,2,16,2048]{5,4,3,2,1,0:T(8,128)(2,1)S(1)} %pad_maximum_fusion.5), channel_id=1, source_target_pairs={{0,4},{1,5},{2,3},{3,2},{4,0},{5,1},{6,7},{7,6},{8,12},{9,13},{10,... | collective-permute-start | bytes 1572872 | tf_op jit(solution)/shard_map/ppermute | solution.py:75
  31.0 14.8 %collective-permute-start.11 = (bf16[2,1,2,2,16,2304]{5,4,3,2,1,0:T(8,128)(2,1)S(1)}, bf16[2,1,2,2,16,2304]{5,4,3,2,1,0:T(8,128)(2,1)S(1)}, u32[]{:S(2)}, u32[]{:S(2)}) collective-permute-start(bf16[2,1,2,2,16,2304]{5,4,3,2,1,0:T(8,128)(2,1)S(1)} %pad_maximum_fusion.4), channel_id=1, source_target_pairs={{0,8},{1,9},{2,18},{3,19},{4,12},{5,13},{6,22},{7,23},{8,0},{9,1},... | collective-permute-start | bytes 1769480 | tf_op jit(solution)/shard_map/ppermute | solution.py:75
  38.3 11.7 %collective-permute-start.3 = (bf16[2,2,1,2,16,2944]{5,4,3,2,1,0:T(8,128)(2,1)S(1)}, bf16[2,2,1,2,16,2944]{5,4,3,2,1,0:T(8,128)(2,1)S(1)}, u32[]{:S(2)}, u32[]{:S(2)}) collective-permute-start(bf16[2,2,1,2,16,2944]{5,4,3,2,1,0:T(8,128)(2,1)S(1)} %pad_maximum_fusion.3), channel_id=1, source_target_pairs={{0,4},{1,5},{2,3},{3,2},{4,0},{5,1},{6,7},{7,6},{8,12},{9,13},{10,... | collective-permute-start | bytes 2261000 | tf_op jit(solution)/shard_map/ppermute | solution.py:75
  40.0 11.1 %collective-permute-start.13 = (bf16[256,2048]{1,0:T(8,128)(2,1)S(1)}, bf16[256,2048]{1,0:T(8,128)(2,1)S(1)}, u32[]{:S(2)}, u32[]{:S(2)}) collective-permute-start(bf16[256,2048]{1,0:T(8,128)(2,1)S(1)} %bitcast.95), channel_id=1, source_target_pairs={{0,2},{1,3},{2,0},{3,1},{4,6},{5,7},{6,4},{7,5},{8,10},{9,11},{10,... | collective-permute-start | bytes 3145736 | tf_op jit(solution)/shard_map/ppermute | solution.py:75
  40.8 9.5 %slice-start = ((s8[7340032]{0:T(1024)(128)(4,1)}), s8[4194304]{0:T(1024)(128)(4,1)S(1)}, s32[]{:S(2)}) async-start(s8[7340032]{0:T(1024)(128)(4,1)} %bitcast.99), calls=%async_computation | async-start | bytes 8388608
  46.0 6.6 %collective-permute-start.14 = (bf16[256,2304]{1,0:T(8,128)(2,1)S(1)}, bf16[256,2304]{1,0:T(8,128)(2,1)S(1)}, u32[]{:S(2)}, u32[]{:S(2)}) collective-permute-start(bf16[256,2304]{1,0:T(8,128)(2,1)S(1)} %bitcast.92), channel_id=1, source_target_pairs={{0,2},{1,3},{2,0},{3,1},{4,6},{5,7},{6,4},{7,5},{8,10},{9,11},{10,... | collective-permute-start | bytes 3538952 | tf_op jit(solution)/shard_map/ppermute | solution.py:75
  50.2 3.9 %collective-permute-start.12 = (bf16[256,2944]{1,0:T(8,128)(2,1)S(1)}, bf16[256,2944]{1,0:T(8,128)(2,1)S(1)}, u32[]{:S(2)}, u32[]{:S(2)}) collective-permute-start(bf16[256,2944]{1,0:T(8,128)(2,1)S(1)} %bitcast.82), channel_id=1, source_target_pairs={{0,2},{1,3},{2,0},{3,1},{4,6},{5,7},{6,4},{7,5},{8,10},{9,11},{10,... | collective-permute-start | bytes 4521992 | tf_op jit(solution)/shard_map/ppermute | solution.py:75
  58.5 4.7 %collective-permute-start.15 = (bf16[256,2432]{1,0:T(8,128)(2,1)S(1)}, bf16[256,2432]{1,0:T(8,128)(2,1)S(1)}, u32[]{:S(2)}, u32[]{:S(2)}) collective-permute-start(bf16[256,2432]{1,0:T(8,128)(2,1)S(1)} %fusion), channel_id=1, source_target_pairs={{0,2},{1,3},{2,0},{3,1},{4,6},{5,7},{6,4},{7,5},{8,10},{9,11},{10,... | collective-permute-start | bytes 3735560 | tf_op jit(solution)/shard_map/ppermute | solution.py:75
  60.7 5.0 %collective-permute-start.18 = (bf16[256,2304]{1,0:T(8,128)(2,1)S(1)}, bf16[256,2304]{1,0:T(8,128)(2,1)S(1)}, u32[]{:S(2)}, u32[]{:S(2)}) collective-permute-start(bf16[256,2304]{1,0:T(8,128)(2,1)S(1)} %multiply_convert_fusion), channel_id=1, source_target_pairs={{0,2},{1,3},{2,0},{3,1},{4,6},{5,7},{6,4},{7,5},{8,10},{9,11},{10,... | collective-permute-start | bytes 3538952 | tf_op jit(solution)/shard_map/ppermute | solution.py:75
  61.7 5.0 %collective-permute-start.17 = (bf16[256,2432]{1,0:T(8,128)(2,1)S(1)}, bf16[256,2432]{1,0:T(8,128)(2,1)S(1)}, u32[]{:S(2)}, u32[]{:S(2)}) collective-permute-start(bf16[256,2432]{1,0:T(8,128)(2,1)S(1)} %fusion.1), channel_id=1, source_target_pairs={{0,2},{1,3},{2,0},{3,1},{4,6},{5,7},{6,4},{7,5},{8,10},{9,11},{10,... | collective-permute-start | bytes 3735560 | tf_op jit(solution)/shard_map/ppermute | solution.py:75
  64.2 10.3 %collective-permute-start.16 = (bf16[2,2,1,2,16,2432]{5,4,3,2,1,0:T(8,128)(2,1)S(1)}, bf16[2,2,1,2,16,2432]{5,4,3,2,1,0:T(8,128)(2,1)S(1)}, u32[]{:S(2)}, u32[]{:S(2)}) collective-permute-start(bf16[2,2,1,2,16,2432]{5,4,3,2,1,0:T(8,128)(2,1)S(1)} %slice.199), channel_id=1, source_target_pairs={{0,4},{1,5},{2,3},{3,2},{4,0},{5,1},{6,7},{7,6},{8,12},{9,13},{10,... | collective-permute-start | bytes 1867784 | tf_op jit(solution)/shard_map/ppermute | solution.py:75
  66.6 23.6 %collective-permute-start.23 = (bf16[2,1,2,2,16,2304]{5,4,3,2,1,0:T(8,128)(2,1)S(1)}, bf16[2,1,2,2,16,2304]{5,4,3,2,1,0:T(8,128)(2,1)S(1)}, u32[]{:S(2)}, u32[]{:S(2)}) collective-permute-start(bf16[2,1,2,2,16,2304]{5,4,3,2,1,0:T(8,128)(2,1)S(1)} %slice.211), channel_id=1, source_target_pairs={{0,8},{1,9},{2,18},{3,19},{4,12},{5,13},{6,22},{7,23},{8,0},{9,1},... | collective-permute-start | bytes 1769480 | tf_op jit(solution)/shard_map/ppermute | solution.py:75
  67.8 14.2 %collective-permute-start.20 = (bf16[2,2,1,2,16,2432]{5,4,3,2,1,0:T(8,128)(2,1)S(1)}, bf16[2,2,1,2,16,2432]{5,4,3,2,1,0:T(8,128)(2,1)S(1)}, u32[]{:S(2)}, u32[]{:S(2)}) collective-permute-start(bf16[2,2,1,2,16,2432]{5,4,3,2,1,0:T(8,128)(2,1)S(1)} %slice.205), channel_id=1, source_target_pairs={{0,4},{1,5},{2,3},{3,2},{4,0},{5,1},{6,7},{7,6},{8,12},{9,13},{10,... | collective-permute-start | bytes 1867784 | tf_op jit(solution)/shard_map/ppermute | solution.py:75
  74.6 15.5 %collective-permute-start.19 = (bf16[2,2,1,1,16,2432]{5,4,3,2,1,0:T(8,128)(2,1)S(1)}, bf16[2,2,1,1,16,2432]{5,4,3,2,1,0:T(8,128)(2,1)S(1)}, u32[]{:S(2)}, u32[]{:S(2)}) collective-permute-start(bf16[2,2,1,1,16,2432]{5,4,3,2,1,0:T(8,128)(2,1)S(1)} %slice.203), channel_id=1, source_target_pairs={{0,1},{1,0},{2,6},{3,7},{4,5},{5,4},{6,2},{7,3},{8,9},{9,8},{10,14... | collective-permute-start | bytes 933896 | tf_op jit(solution)/shard_map/ppermute | solution.py:75
  82.2 14.9 %collective-permute-start.22 = (bf16[2,2,1,1,16,2432]{5,4,3,2,1,0:T(8,128)(2,1)S(1)}, bf16[2,2,1,1,16,2432]{5,4,3,2,1,0:T(8,128)(2,1)S(1)}, u32[]{:S(2)}, u32[]{:S(2)}) collective-permute-start(bf16[2,2,1,1,16,2432]{5,4,3,2,1,0:T(8,128)(2,1)S(1)} %slice.209), channel_id=1, source_target_pairs={{0,1},{1,0},{2,6},{3,7},{4,5},{5,4},{6,2},{7,3},{8,9},{9,8},{10,14... | collective-permute-start | bytes 933896 | tf_op jit(solution)/shard_map/ppermute | solution.py:75
  90.4 10.5 %collective-permute-start.21 = (bf16[1,2,1,1,16,2432]{5,4,3,2,1,0:T(8,128)(2,1)S(1)}, bf16[1,2,1,1,16,2432]{5,4,3,2,1,0:T(8,128)(2,1)S(1)}, u32[]{:S(2)}, u32[]{:S(2)}) collective-permute-start(bf16[1,2,1,1,16,2432]{5,4,3,2,1,0:T(8,128)(2,1)S(1)} %slice.207), channel_id=1, source_target_pairs={{0,16},{1,17},{2,10},{3,11},{4,20},{5,21},{6,14},{7,15},{8,24},{9,... | collective-permute-start | bytes 466952 | tf_op jit(solution)/shard_map/ppermute | solution.py:75
  90.5 10.6 %collective-permute-start.26 = (bf16[2,1,1,2,16,2304]{5,4,3,2,1,0:T(8,128)(2,1)S(1)}, bf16[2,1,1,2,16,2304]{5,4,3,2,1,0:T(8,128)(2,1)S(1)}, u32[]{:S(2)}, u32[]{:S(2)}) collective-permute-start(bf16[2,1,1,2,16,2304]{5,4,3,2,1,0:T(8,128)(2,1)S(1)} %slice.217), channel_id=1, source_target_pairs={{0,4},{1,5},{2,3},{3,2},{4,0},{5,1},{6,7},{7,6},{8,12},{9,13},{10,... | collective-permute-start | bytes 884744 | tf_op jit(solution)/shard_map/ppermute | solution.py:75
  97.2 6.3 %collective-permute-start.25 = (bf16[2,1,1,1,16,2432]{5,4,3,2,1,0:T(8,128)(2,1)S(1)}, bf16[2,1,1,1,16,2432]{5,4,3,2,1,0:T(8,128)(2,1)S(1)}, u32[]{:S(2)}, u32[]{:S(2)}) collective-permute-start(bf16[2,1,1,1,16,2432]{5,4,3,2,1,0:T(8,128)(2,1)S(1)} %slice.215), channel_id=1, source_target_pairs={{0,8},{1,9},{2,18},{3,19},{4,12},{5,13},{6,22},{7,23},{8,0},{9,1},... | collective-permute-start | bytes 466952 | tf_op jit(solution)/shard_map/ppermute | solution.py:75
  101.0 5.3 %collective-permute-start.24 = (bf16[1,1,1,1,16,2432]{5,4,3,2,1,0:T(8,128)(2,1)S(1)}, bf16[1,1,1,1,16,2432]{5,4,3,2,1,0:T(8,128)(2,1)S(1)}, u32[]{:S(2)}, u32[]{:S(2)}) collective-permute-start(bf16[1,1,1,1,16,2432]{5,4,3,2,1,0:T(8,128)(2,1)S(1)} %slice.213), channel_id=1, source_target_pairs={{0,8},{1,9},{2,18},{3,19},{4,12},{5,13},{6,22},{7,23},{8,0},{9,1},... | collective-permute-start | bytes 233480 | tf_op jit(solution)/shard_map/ppermute | solution.py:75
  101.2 5.2 %collective-permute-start.27 = (bf16[2,1,1,1,16,2304]{5,4,3,2,1,0:T(8,128)(2,1)S(1)}, bf16[2,1,1,1,16,2304]{5,4,3,2,1,0:T(8,128)(2,1)S(1)}, u32[]{:S(2)}, u32[]{:S(2)}) collective-permute-start(bf16[2,1,1,1,16,2304]{5,4,3,2,1,0:T(8,128)(2,1)S(1)} %slice.219), channel_id=1, source_target_pairs={{0,1},{1,0},{2,6},{3,7},{4,5},{5,4},{6,2},{7,3},{8,9},{9,8},{10,14... | collective-permute-start | bytes 442376 | tf_op jit(solution)/shard_map/ppermute | solution.py:75
  106.3 5.5 %collective-permute-start.29 = (bf16[1,1,1,1,16,2432]{5,4,3,2,1,0:T(8,128)(2,1)S(1)}, bf16[1,1,1,1,16,2432]{5,4,3,2,1,0:T(8,128)(2,1)S(1)}, u32[]{:S(2)}, u32[]{:S(2)}) collective-permute-start(bf16[1,1,1,1,16,2432]{5,4,3,2,1,0:T(8,128)(2,1)S(1)} %slice.223), channel_id=1, source_target_pairs={{0,16},{1,17},{2,10},{3,11},{4,20},{5,21},{6,14},{7,15},{8,24},{9,... | collective-permute-start | bytes 233480 | tf_op jit(solution)/shard_map/ppermute | solution.py:75
  106.5 6.9 %collective-permute-start.28 = (bf16[1,1,1,1,16,2304]{5,4,3,2,1,0:T(8,128)(2,1)S(1)}, bf16[1,1,1,1,16,2304]{5,4,3,2,1,0:T(8,128)(2,1)S(1)}, u32[]{:S(2)}, u32[]{:S(2)}) collective-permute-start(bf16[1,1,1,1,16,2304]{5,4,3,2,1,0:T(8,128)(2,1)S(1)} %slice.221), channel_id=1, source_target_pairs={{0,16},{1,17},{2,10},{3,11},{4,20},{5,21},{6,14},{7,15},{8,24},{9,... | collective-permute-start | bytes 221192 | tf_op jit(solution)/shard_map/ppermute | solution.py:75
  (3 other events, 9.0 us)

commit v6 on v4

--- a/solution.py
+++ b/solution.py
@@ -88,7 +88,7 @@
 )
 GATHER_TURNS = (10, 1, 12, 10, 11, 2, 10, 11, 12, 10, 12, 11, 10, 10, 10, 12, 11, 11, 12, 11, 12)
 SCATTER_TURNS = (0, 11, 2, 0, 2, 0, 1, 2, 0, 1, 2, 0, 1, 2, 11)
-PACKED = 2
+PACKED = 1
 
 
 def chunks_of(width, plan):

time: 113 us -> 116 us (1.027)
  waiting for transfers between devices: 37.8 us -> 45.7 us
  starting transfers between devices: 48.8 us -> 41.7 us
  matrix products: 16.8 us -> 18.5 us
    ppermute x30, waiting for transfers between devices: 37.8 us -> 45.7 us  [exchange(): return lax.ppermute(block, AXES, perm)]
    ppermute x30, starting transfers between devices: 48.8 us -> 41.7 us  [exchange(): return lax.ppermute(block, AXES, perm)]
    dot_general x6, matrix products: 4.87 us -> 8.28 us  [products(): jnp.dot(rows, w_up[lo:hi], preferred_element_type=jnp.float32)]
    dot_general x6, matrix products: 6.72 us -> 4.78 us  [products(): jnp.dot(rows, w_gate[lo:hi], preferred_element_type=jnp.float32)]
where the time goes in v6:
time: 116 us
  waiting for transfers between devices  45.7 us (39%)
  starting transfers between devices  41.7 us (36%)
  matrix products  18.5 us (16%)
  local copies, waits for them, and re-layouts  6.69 us (6%)
  other arithmetic  2.67 us (2%)
    ppermute x30, waiting for transfers between devices, exchange(): return lax.ppermute(block, AXES, perm)  45.7 us
    ppermute x30, starting transfers between devices, exchange(): return lax.ppermute(block, AXES, perm)  41.7 us
    dot_general x6, matrix products, products(): jnp.dot(rows, w_up[lo:hi], preferred_element_type=jnp.float32)  8.28 us
    dot_general x6, matrix products, product(): jnp.dot(hidden[j], w_down[:, lo:hi], preferred_element_type=jnp.float32)  5.45 us
    dot_general x6, matrix products, products(): jnp.dot(rows, w_gate[lo:hi], preferred_element_type=jnp.float32)  4.78 us
    unnamed x12, local copies, waits for them, and re-layouts  3.8 us
  transfers between devices with their start and end apart: 30, of which 13 were waited for; matrix products, arithmetic and copies ran while one was open for 17% of the time, Pallas kernels for 0%

profile of v6, /device:TPU:0, one launch (start us, length us, event | category | flops | bytes accessed | tf_op | source)
XLA Modules:
  0.0 115.8 jit_solution(9301416651661363713)
XLA Ops:
  2.6 3.1 %collective-permute-start = (bf16[1,1,1,1,16,2176]{5,4,3,2,1,0:T(8,128)(2,1)S(1)}, bf16[1,1,1,1,16,2176]{5,4,3,2,1,0:T(8,128)(2,1)S(1)}, u32[]{:S(2)}, u32[]{:S(2)}) collective-permute-start(bf16[1,1,1,1,16,2176]{5,4,3,2,1,0:T(8,128)(2,1)S(1)} %maximum_bitcast_fusion), channel_id=1, source_target_pairs={{0,8},{1,9},{2,18},{3,19},{4,12},{5,13},{6,22},{7,23},{8,0},{9,1},... | collective-permute-start | bytes 208904 | tf_op jit(solution)/shard_map/ppermute | solution.py:75
  6.5 2.6 %collective-permute-start.8 = (bf16[1,1,1,1,16,2304]{5,4,3,2,1,0:T(8,128)(2,1)S(1)}, bf16[1,1,1,1,16,2304]{5,4,3,2,1,0:T(8,128)(2,1)S(1)}, u32[]{:S(2)}, u32[]{:S(2)}) collective-permute-start(bf16[1,1,1,1,16,2304]{5,4,3,2,1,0:T(8,128)(2,1)S(1)} %slice_bitcast_fusion.1), channel_id=1, source_target_pairs={{0,16},{1,17},{2,10},{3,11},{4,20},{5,21},{6,14},{7,15},{8,24},{9,... | collective-permute-start | bytes 221192 | tf_op jit(solution)/shard_map/ppermute | solution.py:75
  10.5 1.6 %collective-permute-start.1 = (bf16[1,2,1,1,16,2176]{5,4,3,2,1,0:T(8,128)(2,1)S(1)}, bf16[1,2,1,1,16,2176]{5,4,3,2,1,0:T(8,128)(2,1)S(1)}, u32[]{:S(2)}, u32[]{:S(2)}) collective-permute-start(bf16[1,2,1,1,16,2176]{5,4,3,2,1,0:T(8,128)(2,1)S(1)} %pad_maximum_fusion.12), channel_id=1, source_target_pairs={{0,4},{1,5},{2,3},{3,2},{4,0},{5,1},{6,7},{7,6},{8,12},{9,13},{10,... | collective-permute-start | bytes 417800 | tf_op jit(solution)/shard_map/ppermute | solution.py:75
  12.6 1.6 %collective-permute-start.9 = (bf16[2,1,1,1,16,2304]{5,4,3,2,1,0:T(8,128)(2,1)S(1)}, bf16[2,1,1,1,16,2304]{5,4,3,2,1,0:T(8,128)(2,1)S(1)}, u32[]{:S(2)}, u32[]{:S(2)}) collective-permute-start(bf16[2,1,1,1,16,2304]{5,4,3,2,1,0:T(8,128)(2,1)S(1)} %pad_maximum_fusion.11), channel_id=1, source_target_pairs={{0,1},{1,0},{2,6},{3,7},{4,5},{5,4},{6,2},{7,3},{8,9},{9,8},{10,14... | collective-permute-start | bytes 442376 | tf_op jit(solution)/shard_map/ppermute | solution.py:75
  14.2 1.2 %collective-permute-done.4 = bf16[1,1,1,1,16,2816]{5,4,3,2,1,0:T(8,128)(2,1)S(1)} collective-permute-done((bf16[1,1,1,1,16,2816]{5,4,3,2,1,0:T(8,128)(2,1)S(1)}, bf16[1,1,1,1,16,2816]{5,4,3,2,1,0:T(8,128)(2,1)S(1)}, u32[]{:S(2)}, u32[]{:S(2)}) %collective-permute-start.4) | collective-permute-done | bytes 90144 | tf_op jit(solution)/shard_map/ppermute | solution.py:75
  15.4 1.2 %collective-permute-start.5 = (bf16[1,2,1,1,16,2816]{5,4,3,2,1,0:T(8,128)(2,1)S(1)}, bf16[1,2,1,1,16,2816]{5,4,3,2,1,0:T(8,128)(2,1)S(1)}, u32[]{:S(2)}, u32[]{:S(2)}) collective-permute-start(bf16[1,2,1,1,16,2816]{5,4,3,2,1,0:T(8,128)(2,1)S(1)} %pad_maximum_fusion.10), channel_id=1, source_target_pairs={{0,16},{1,17},{2,10},{3,11},{4,20},{5,21},{6,14},{7,15},{8,24},{9,... | collective-permute-start | bytes 540680 | tf_op jit(solution)/shard_map/ppermute | solution.py:75
  16.7 2.4 %collective-permute-start.2 = (bf16[1,2,2,1,16,2176]{5,4,3,2,1,0:T(8,128)(2,1)S(1)}, bf16[1,2,2,1,16,2176]{5,4,3,2,1,0:T(8,128)(2,1)S(1)}, u32[]{:S(2)}, u32[]{:S(2)}) collective-permute-start(bf16[1,2,2,1,16,2176]{5,4,3,2,1,0:T(8,128)(2,1)S(1)} %pad_maximum_fusion.8), channel_id=1, source_target_pairs={{0,16},{1,17},{2,10},{3,11},{4,20},{5,21},{6,14},{7,15},{8,24},{9,... | collective-permute-start | bytes 835592 | tf_op jit(solution)/shard_map/ppermute | solution.py:75
  19.2 1.6 %collective-permute-start.10 = (bf16[2,1,1,2,16,2304]{5,4,3,2,1,0:T(8,128)(2,1)S(1)}, bf16[2,1,1,2,16,2304]{5,4,3,2,1,0:T(8,128)(2,1)S(1)}, u32[]{:S(2)}, u32[]{:S(2)}) collective-permute-start(bf16[2,1,1,2,16,2304]{5,4,3,2,1,0:T(8,128)(2,1)S(1)} %pad_maximum_fusion.7), channel_id=1, source_target_pairs={{0,4},{1,5},{2,3},{3,2},{4,0},{5,1},{6,7},{7,6},{8,12},{9,13},{10,... | collective-permute-start | bytes 884744 | tf_op jit(solution)/shard_map/ppermute | solution.py:75
  20.8 3.0 %collective-permute-done.5 = bf16[1,2,1,1,16,2816]{5,4,3,2,1,0:T(8,128)(2,1)S(1)} collective-permute-done((bf16[1,2,1,1,16,2816]{5,4,3,2,1,0:T(8,128)(2,1)S(1)}, bf16[1,2,1,1,16,2816]{5,4,3,2,1,0:T(8,128)(2,1)S(1)}, u32[]{:S(2)}, u32[]{:S(2)}) %collective-permute-start.5) | collective-permute-done | bytes 180256 | tf_op jit(solution)/shard_map/ppermute | solution.py:75
  23.8 1.6 %collective-permute-start.6 = (bf16[2,2,1,1,16,2816]{5,4,3,2,1,0:T(8,128)(2,1)S(1)}, bf16[2,2,1,1,16,2816]{5,4,3,2,1,0:T(8,128)(2,1)S(1)}, u32[]{:S(2)}, u32[]{:S(2)}) collective-permute-start(bf16[2,2,1,1,16,2816]{5,4,3,2,1,0:T(8,128)(2,1)S(1)} %pad_maximum_fusion.6), channel_id=1, source_target_pairs={{0,1},{1,0},{2,6},{3,7},{4,5},{5,4},{6,2},{7,3},{8,9},{9,8},{10,14... | collective-permute-start | bytes 1081352 | tf_op jit(solution)/shard_map/ppermute | solution.py:75
  25.4 11.1 %collective-permute-done.2 = bf16[1,2,2,1,16,2176]{5,4,3,2,1,0:T(8,128)(2,1)S(1)} collective-permute-done((bf16[1,2,2,1,16,2176]{5,4,3,2,1,0:T(8,128)(2,1)S(1)}, bf16[1,2,2,1,16,2176]{5,4,3,2,1,0:T(8,128)(2,1)S(1)}, u32[]{:S(2)}, u32[]{:S(2)}) %collective-permute-start.2) | collective-permute-done | bytes 278560 | tf_op jit(solution)/shard_map/ppermute | solution.py:75
  37.7 2.8 %collective-permute-start.7 = (bf16[2,2,1,2,16,2816]{5,4,3,2,1,0:T(8,128)(2,1)S(1)}, bf16[2,2,1,2,16,2816]{5,4,3,2,1,0:T(8,128)(2,1)S(1)}, u32[]{:S(2)}, u32[]{:S(2)}) collective-permute-start(bf16[2,2,1,2,16,2816]{5,4,3,2,1,0:T(8,128)(2,1)S(1)} %pad_maximum_fusion.3), channel_id=1, source_target_pairs={{0,4},{1,5},{2,3},{3,2},{4,0},{5,1},{6,7},{7,6},{8,12},{9,13},{10,... | collective-permute-start | bytes 2162696 | tf_op jit(solution)/shard_map/ppermute | solution.py:75
  40.5 5.7 %collective-permute-done.3 = bf16[2,2,2,1,16,2176]{5,4,3,2,1,0:T(8,128)(2,1)S(1)} collective-permute-done((bf16[2,2,2,1,16,2176]{5,4,3,2,1,0:T(8,128)(2,1)S(1)}, bf16[2,2,2,1,16,2176]{5,4,3,2,1,0:T(8,128)(2,1)S(1)}, u32[]{:S(2)}, u32[]{:S(2)}) %collective-permute-start.3) | collective-permute-done | bytes 557088 | tf_op jit(solution)/shard_map/ppermute | solution.py:75
  46.4 2.3 %fusion.28 = f32[256,512]{1,0:T(8,128)S(1)} fusion(bf16[1,7168,512]{2,1,0:T(8,128)(2,1)} %param.10, bf16[256,2176]{1,0:T(8,128)(2,1)S(1)} %bitcast.86), kind=kOutput, calls=%fused_computation.37 | convolution fusion | flops 536870912 | bytes 3670016 | tf_op jit(solution)/shard_map/dot_general | solution.py:116
  50.1 2.6 %fusion.16 = f32[256,512]{1,0:T(8,128)S(1)} fusion(bf16[256,2304]{1,0:T(8,128)(2,1)S(1)} %bitcast.96, bf16[1,7168,512]{2,1,0:T(8,128)(2,1)} %param.10), kind=kOutput, calls=%fused_computation.23 | convolution fusion | flops 603979776 | bytes 4063232 | tf_op jit(solution)/shard_map/dot_general | solution.py:116
  58.6 1.0 multiply_convert_fusion.1
  59.9 1.2 %slice-done.3 = s8[3145728]{0:T(1024)(128)(4,1)S(1)} async-done(((s8[7340032]{0:T(1024)(128)(4,1)}), s8[3145728]{0:T(1024)(128)(4,1)S(1)}, s32[]{:S(2)}) %slice-start.3) | async-done | bytes 3145752
  67.3 2.6 %collective-permute-start.16 = (bf16[2,2,1,2,16,2432]{5,4,3,2,1,0:T(8,128)(2,1)S(1)}, bf16[2,2,1,2,16,2432]{5,4,3,2,1,0:T(8,128)(2,1)S(1)}, u32[]{:S(2)}, u32[]{:S(2)}) collective-permute-start(bf16[2,2,1,2,16,2432]{5,4,3,2,1,0:T(8,128)(2,1)S(1)} %slice.199), channel_id=1, source_target_pairs={{0,4},{1,5},{2,3},{3,2},{4,0},{5,1},{6,7},{7,6},{8,12},{9,13},{10,... | collective-permute-start | bytes 1867784 | tf_op jit(solution)/shard_map/ppermute | solution.py:75
  70.8 1.1 collective-permute-start.23
  71.9 1.1 add_convert_fusion
  73.1 9.0 %collective-permute-done.16 = bf16[2,2,1,2,16,2432]{5,4,3,2,1,0:T(8,128)(2,1)S(1)} collective-permute-done((bf16[2,2,1,2,16,2432]{5,4,3,2,1,0:T(8,128)(2,1)S(1)}, bf16[2,2,1,2,16,2432]{5,4,3,2,1,0:T(8,128)(2,1)S(1)}, u32[]{:S(2)}, u32[]{:S(2)}) %collective-permute-start.16) | collective-permute-done | bytes 622624 | tf_op jit(solution)/shard_map/ppermute | solution.py:75
  82.4 1.4 %collective-permute-done.20 = bf16[2,2,2,1,16,2432]{5,4,3,2,1,0:T(8,128)(2,1)S(1)} collective-permute-done((bf16[2,2,2,1,16,2432]{5,4,3,2,1,0:T(8,128)(2,1)S(1)}, bf16[2,2,2,1,16,2432]{5,4,3,2,1,0:T(8,128)(2,1)S(1)}, u32[]{:S(2)}, u32[]{:S(2)}) %collective-permute-start.20) | collective-permute-done | bytes 622624 | tf_op jit(solution)/shard_map/ppermute | solution.py:75
  84.0 2.6 %collective-permute-start.22 = (bf16[2,2,1,1,16,2432]{5,4,3,2,1,0:T(8,128)(2,1)S(1)}, bf16[2,2,1,1,16,2432]{5,4,3,2,1,0:T(8,128)(2,1)S(1)}, u32[]{:S(2)}, u32[]{:S(2)}) collective-permute-start(bf16[2,2,1,1,16,2432]{5,4,3,2,1,0:T(8,128)(2,1)S(1)} %slice.209), channel_id=1, source_target_pairs={{0,4},{1,5},{2,3},{3,2},{4,0},{5,1},{6,7},{7,6},{8,12},{9,13},{10,... | collective-permute-start | bytes 933896 | tf_op jit(solution)/shard_map/ppermute | solution.py:75
  86.6 4.1 %collective-permute-done.19 = bf16[2,2,1,1,16,2432]{5,4,3,2,1,0:T(8,128)(2,1)S(1)} collective-permute-done((bf16[2,2,1,1,16,2432]{5,4,3,2,1,0:T(8,128)(2,1)S(1)}, bf16[2,2,1,1,16,2432]{5,4,3,2,1,0:T(8,128)(2,1)S(1)}, u32[]{:S(2)}, u32[]{:S(2)}) %collective-permute-start.19) | collective-permute-done | bytes 311328 | tf_op jit(solution)/shard_map/ppermute | solution.py:75
  91.0 1.8 %collective-permute-start.21 = (bf16[1,2,1,1,16,2432]{5,4,3,2,1,0:T(8,128)(2,1)S(1)}, bf16[1,2,1,1,16,2432]{5,4,3,2,1,0:T(8,128)(2,1)S(1)}, u32[]{:S(2)}, u32[]{:S(2)}) collective-permute-start(bf16[1,2,1,1,16,2432]{5,4,3,2,1,0:T(8,128)(2,1)S(1)} %slice.207), channel_id=1, source_target_pairs={{0,16},{1,17},{2,10},{3,11},{4,20},{5,21},{6,14},{7,15},{8,24},{9,... | collective-permute-start | bytes 466952 | tf_op jit(solution)/shard_map/ppermute | solution.py:75
  93.8 5.6 %collective-permute-start.25 = (bf16[2,1,1,1,16,2432]{5,4,3,2,1,0:T(8,128)(2,1)S(1)}, bf16[2,1,1,1,16,2432]{5,4,3,2,1,0:T(8,128)(2,1)S(1)}, u32[]{:S(2)}, u32[]{:S(2)}) collective-permute-start(bf16[2,1,1,1,16,2432]{5,4,3,2,1,0:T(8,128)(2,1)S(1)} %slice.215), channel_id=1, source_target_pairs={{0,8},{1,9},{2,18},{3,19},{4,12},{5,13},{6,22},{7,23},{8,0},{9,1},... | collective-permute-start | bytes 466952 | tf_op jit(solution)/shard_map/ppermute | solution.py:75
  99.4 2.7 %collective-permute-done.21 = bf16[1,2,1,1,16,2432]{5,4,3,2,1,0:T(8,128)(2,1)S(1)} collective-permute-done((bf16[1,2,1,1,16,2432]{5,4,3,2,1,0:T(8,128)(2,1)S(1)}, bf16[1,2,1,1,16,2432]{5,4,3,2,1,0:T(8,128)(2,1)S(1)}, u32[]{:S(2)}, u32[]{:S(2)}) %collective-permute-start.21) | collective-permute-done | bytes 155680 | tf_op jit(solution)/shard_map/ppermute | solution.py:75
  103.1 1.4 %collective-permute-done.25 = bf16[2,1,1,1,16,2432]{5,4,3,2,1,0:T(8,128)(2,1)S(1)} collective-permute-done((bf16[2,1,1,1,16,2432]{5,4,3,2,1,0:T(8,128)(2,1)S(1)}, bf16[2,1,1,1,16,2432]{5,4,3,2,1,0:T(8,128)(2,1)S(1)}, u32[]{:S(2)}, u32[]{:S(2)}) %collective-permute-start.25) | collective-permute-done | bytes 155680 | tf_op jit(solution)/shard_map/ppermute | solution.py:75
  104.6 2.2 %collective-permute-done.24 = bf16[1,1,1,1,16,2432]{5,4,3,2,1,0:T(8,128)(2,1)S(1)} collective-permute-done((bf16[1,1,1,1,16,2432]{5,4,3,2,1,0:T(8,128)(2,1)S(1)}, bf16[1,1,1,1,16,2432]{5,4,3,2,1,0:T(8,128)(2,1)S(1)}, u32[]{:S(2)}, u32[]{:S(2)}) %collective-permute-start.24) | collective-permute-done | bytes 77856 | tf_op jit(solution)/shard_map/ppermute | solution.py:75
  106.9 2.8 %collective-permute-start.29 = (bf16[1,1,1,1,16,2432]{5,4,3,2,1,0:T(8,128)(2,1)S(1)}, bf16[1,1,1,1,16,2432]{5,4,3,2,1,0:T(8,128)(2,1)S(1)}, u32[]{:S(2)}, u32[]{:S(2)}) collective-permute-start(bf16[1,1,1,1,16,2432]{5,4,3,2,1,0:T(8,128)(2,1)S(1)} %slice.223), channel_id=1, source_target_pairs={{0,16},{1,17},{2,10},{3,11},{4,20},{5,21},{6,14},{7,15},{8,24},{9,... | collective-permute-start | bytes 233480 | tf_op jit(solution)/shard_map/ppermute | solution.py:75
  109.7 2.1 %collective-permute-start.28 = (bf16[1,1,1,1,16,2304]{5,4,3,2,1,0:T(8,128)(2,1)S(1)}, bf16[1,1,1,1,16,2304]{5,4,3,2,1,0:T(8,128)(2,1)S(1)}, u32[]{:S(2)}, u32[]{:S(2)}) collective-permute-start(bf16[1,1,1,1,16,2304]{5,4,3,2,1,0:T(8,128)(2,1)S(1)} %slice.221), channel_id=1, source_target_pairs={{0,16},{1,17},{2,10},{3,11},{4,20},{5,21},{6,14},{7,15},{8,24},{9,... | collective-permute-start | bytes 221192 | tf_op jit(solution)/shard_map/ppermute | solution.py:75
  112.3 2.8 %collective-permute-done.28 = bf16[1,1,1,1,16,2304]{5,4,3,2,1,0:T(8,128)(2,1)S(1)} collective-permute-done((bf16[1,1,1,1,16,2304]{5,4,3,2,1,0:T(8,128)(2,1)S(1)}, bf16[1,1,1,1,16,2304]{5,4,3,2,1,0:T(8,128)(2,1)S(1)}, u32[]{:S(2)}, u32[]{:S(2)}) %collective-permute-start.28) | collective-permute-done | bytes 73760 | tf_op jit(solution)/shard_map/ppermute | solution.py:75
  (106 shorter events, 25.4 us)
Async XLA Ops:
  2.6 7.9 %collective-permute-start = (bf16[1,1,1,1,16,2176]{5,4,3,2,1,0:T(8,128)(2,1)S(1)}, bf16[1,1,1,1,16,2176]{5,4,3,2,1,0:T(8,128)(2,1)S(1)}, u32[]{:S(2)}, u32[]{:S(2)}) collective-permute-start(bf16[1,1,1,1,16,2176]{5,4,3,2,1,0:T(8,128)(2,1)S(1)} %maximum_bitcast_fusion), channel_id=1, source_target_pairs={{0,8},{1,9},{2,18},{3,19},{4,12},{5,13},{6,22},{7,23},{8,0},{9,1},... | collective-permute-start | bytes 208904 | tf_op jit(solution)/shard_map/ppermute | solution.py:75
  6.5 6.0 %collective-permute-start.8 = (bf16[1,1,1,1,16,2304]{5,4,3,2,1,0:T(8,128)(2,1)S(1)}, bf16[1,1,1,1,16,2304]{5,4,3,2,1,0:T(8,128)(2,1)S(1)}, u32[]{:S(2)}, u32[]{:S(2)}) collective-permute-start(bf16[1,1,1,1,16,2304]{5,4,3,2,1,0:T(8,128)(2,1)S(1)} %slice_bitcast_fusion.1), channel_id=1, source_target_pairs={{0,16},{1,17},{2,10},{3,11},{4,20},{5,21},{6,14},{7,15},{8,24},{9,... | collective-permute-start | bytes 221192 | tf_op jit(solution)/shard_map/ppermute | solution.py:75
  10.0 5.4 %collective-permute-start.4 = (bf16[1,1,1,1,16,2816]{5,4,3,2,1,0:T(8,128)(2,1)S(1)}, bf16[1,1,1,1,16,2816]{5,4,3,2,1,0:T(8,128)(2,1)S(1)}, u32[]{:S(2)}, u32[]{:S(2)}) collective-permute-start(bf16[1,1,1,1,16,2816]{5,4,3,2,1,0:T(8,128)(2,1)S(1)} %slice_bitcast_fusion), channel_id=1, source_target_pairs={{0,8},{1,9},{2,18},{3,19},{4,12},{5,13},{6,22},{7,23},{8,0},{9,1},... | collective-permute-start | bytes 270344 | tf_op jit(solution)/shard_map/ppermute | solution.py:75
  10.5 6.1 %collective-permute-start.1 = (bf16[1,2,1,1,16,2176]{5,4,3,2,1,0:T(8,128)(2,1)S(1)}, bf16[1,2,1,1,16,2176]{5,4,3,2,1,0:T(8,128)(2,1)S(1)}, u32[]{:S(2)}, u32[]{:S(2)}) collective-permute-start(bf16[1,2,1,1,16,2176]{5,4,3,2,1,0:T(8,128)(2,1)S(1)} %pad_maximum_fusion.12), channel_id=1, source_target_pairs={{0,4},{1,5},{2,3},{3,2},{4,0},{5,1},{6,7},{7,6},{8,12},{9,13},{10,... | collective-permute-start | bytes 417800 | tf_op jit(solution)/shard_map/ppermute | solution.py:75
  12.6 6.6 %collective-permute-start.9 = (bf16[2,1,1,1,16,2304]{5,4,3,2,1,0:T(8,128)(2,1)S(1)}, bf16[2,1,1,1,16,2304]{5,4,3,2,1,0:T(8,128)(2,1)S(1)}, u32[]{:S(2)}, u32[]{:S(2)}) collective-permute-start(bf16[2,1,1,1,16,2304]{5,4,3,2,1,0:T(8,128)(2,1)S(1)} %pad_maximum_fusion.11), channel_id=1, source_target_pairs={{0,1},{1,0},{2,6},{3,7},{4,5},{5,4},{6,2},{7,3},{8,9},{9,8},{10,14... | collective-permute-start | bytes 442376 | tf_op jit(solution)/shard_map/ppermute | solution.py:75
  15.4 8.4 %collective-permute-start.5 = (bf16[1,2,1,1,16,2816]{5,4,3,2,1,0:T(8,128)(2,1)S(1)}, bf16[1,2,1,1,16,2816]{5,4,3,2,1,0:T(8,128)(2,1)S(1)}, u32[]{:S(2)}, u32[]{:S(2)}) collective-permute-start(bf16[1,2,1,1,16,2816]{5,4,3,2,1,0:T(8,128)(2,1)S(1)} %pad_maximum_fusion.10), channel_id=1, source_target_pairs={{0,16},{1,17},{2,10},{3,11},{4,20},{5,21},{6,14},{7,15},{8,24},{9,... | collective-permute-start | bytes 540680 | tf_op jit(solution)/shard_map/ppermute | solution.py:75
  16.7 19.8 %collective-permute-start.2 = (bf16[1,2,2,1,16,2176]{5,4,3,2,1,0:T(8,128)(2,1)S(1)}, bf16[1,2,2,1,16,2176]{5,4,3,2,1,0:T(8,128)(2,1)S(1)}, u32[]{:S(2)}, u32[]{:S(2)}) collective-permute-start(bf16[1,2,2,1,16,2176]{5,4,3,2,1,0:T(8,128)(2,1)S(1)} %pad_maximum_fusion.8), channel_id=1, source_target_pairs={{0,16},{1,17},{2,10},{3,11},{4,20},{5,21},{6,14},{7,15},{8,24},{9,... | collective-permute-start | bytes 835592 | tf_op jit(solution)/shard_map/ppermute | solution.py:75
  19.2 17.5 %collective-permute-start.10 = (bf16[2,1,1,2,16,2304]{5,4,3,2,1,0:T(8,128)(2,1)S(1)}, bf16[2,1,1,2,16,2304]{5,4,3,2,1,0:T(8,128)(2,1)S(1)}, u32[]{:S(2)}, u32[]{:S(2)}) collective-permute-start(bf16[2,1,1,2,16,2304]{5,4,3,2,1,0:T(8,128)(2,1)S(1)} %pad_maximum_fusion.7), channel_id=1, source_target_pairs={{0,4},{1,5},{2,3},{3,2},{4,0},{5,1},{6,7},{7,6},{8,12},{9,13},{10,... | collective-permute-start | bytes 884744 | tf_op jit(solution)/shard_map/ppermute | solution.py:75
  23.8 13.8 %collective-permute-start.6 = (bf16[2,2,1,1,16,2816]{5,4,3,2,1,0:T(8,128)(2,1)S(1)}, bf16[2,2,1,1,16,2816]{5,4,3,2,1,0:T(8,128)(2,1)S(1)}, u32[]{:S(2)}, u32[]{:S(2)}) collective-permute-start(bf16[2,2,1,1,16,2816]{5,4,3,2,1,0:T(8,128)(2,1)S(1)} %pad_maximum_fusion.6), channel_id=1, source_target_pairs={{0,1},{1,0},{2,6},{3,7},{4,5},{5,4},{6,2},{7,3},{8,9},{9,8},{10,14... | collective-permute-start | bytes 1081352 | tf_op jit(solution)/shard_map/ppermute | solution.py:75
  36.6 9.6 %collective-permute-start.3 = (bf16[2,2,2,1,16,2176]{5,4,3,2,1,0:T(8,128)(2,1)S(1)}, bf16[2,2,2,1,16,2176]{5,4,3,2,1,0:T(8,128)(2,1)S(1)}, u32[]{:S(2)}, u32[]{:S(2)}) collective-permute-start(bf16[2,2,2,1,16,2176]{5,4,3,2,1,0:T(8,128)(2,1)S(1)} %pad_maximum_fusion.5), channel_id=1, source_target_pairs={{0,1},{1,0},{2,6},{3,7},{4,5},{5,4},{6,2},{7,3},{8,9},{9,8},{10,14... | collective-permute-start | bytes 1671176 | tf_op jit(solution)/shard_map/ppermute | solution.py:75
  36.7 12.7 %collective-permute-start.11 = (bf16[2,1,2,2,16,2304]{5,4,3,2,1,0:T(8,128)(2,1)S(1)}, bf16[2,1,2,2,16,2304]{5,4,3,2,1,0:T(8,128)(2,1)S(1)}, u32[]{:S(2)}, u32[]{:S(2)}) collective-permute-start(bf16[2,1,2,2,16,2304]{5,4,3,2,1,0:T(8,128)(2,1)S(1)} %pad_maximum_fusion.4), channel_id=1, source_target_pairs={{0,8},{1,9},{2,18},{3,19},{4,12},{5,13},{6,22},{7,23},{8,0},{9,1},... | collective-permute-start | bytes 1769480 | tf_op jit(solution)/shard_map/ppermute | solution.py:75
  37.6 11.0 %copy-start = (bf16[1,7168,512]{2,1,0:T(8,128)(2,1)S(1)}, bf16[1,7168,512]{2,1,0:T(8,128)(2,1)}, u32[]{:S(2)}) copy-start(bf16[1,7168,512]{2,1,0:T(8,128)(2,1)} %param.9) | copy-start | bytes 22020100
  37.7 15.0 %collective-permute-start.7 = (bf16[2,2,1,2,16,2816]{5,4,3,2,1,0:T(8,128)(2,1)S(1)}, bf16[2,2,1,2,16,2816]{5,4,3,2,1,0:T(8,128)(2,1)S(1)}, u32[]{:S(2)}, u32[]{:S(2)}) collective-permute-start(bf16[2,2,1,2,16,2816]{5,4,3,2,1,0:T(8,128)(2,1)S(1)} %pad_maximum_fusion.3), channel_id=1, source_target_pairs={{0,4},{1,5},{2,3},{3,2},{4,0},{5,1},{6,7},{7,6},{8,12},{9,13},{10,... | collective-permute-start | bytes 2162696 | tf_op jit(solution)/shard_map/ppermute | solution.py:75
  46.3 7.4 %collective-permute-start.12 = (bf16[256,2176]{1,0:T(8,128)(2,1)S(1)}, bf16[256,2176]{1,0:T(8,128)(2,1)S(1)}, u32[]{:S(2)}, u32[]{:S(2)}) collective-permute-start(bf16[256,2176]{1,0:T(8,128)(2,1)S(1)} %bitcast.85), channel_id=1, source_target_pairs={{0,2},{1,3},{2,0},{3,1},{4,6},{5,7},{6,4},{7,5},{8,10},{9,11},{10,... | collective-permute-start | bytes 3342344 | tf_op jit(solution)/shard_map/ppermute | solution.py:75
  49.6 6.6 %collective-permute-start.14 = (bf16[256,2304]{1,0:T(8,128)(2,1)S(1)}, bf16[256,2304]{1,0:T(8,128)(2,1)S(1)}, u32[]{:S(2)}, u32[]{:S(2)}) collective-permute-start(bf16[256,2304]{1,0:T(8,128)(2,1)S(1)} %bitcast.95), channel_id=1, source_target_pairs={{0,2},{1,3},{2,0},{3,1},{4,6},{5,7},{6,4},{7,5},{8,10},{9,11},{10,... | collective-permute-start | bytes 3538952 | tf_op jit(solution)/shard_map/ppermute | solution.py:75
  50.1 3.8 %slice-start = ((s8[7340032]{0:T(1024)(128)(4,1)}), s8[4194304]{0:T(1024)(128)(4,1)S(1)}, s32[]{:S(2)}) async-start(s8[7340032]{0:T(1024)(128)(4,1)} %bitcast.99), calls=%async_computation | async-start | bytes 8388608
  52.9 4.8 %collective-permute-start.13 = (bf16[256,2816]{1,0:T(8,128)(2,1)S(1)}, bf16[256,2816]{1,0:T(8,128)(2,1)S(1)}, u32[]{:S(2)}, u32[]{:S(2)}) collective-permute-start(bf16[256,2816]{1,0:T(8,128)(2,1)S(1)} %bitcast.82), channel_id=1, source_target_pairs={{0,2},{1,3},{2,0},{3,1},{4,6},{5,7},{6,4},{7,5},{8,10},{9,11},{10,... | collective-permute-start | bytes 4325384 | tf_op jit(solution)/shard_map/ppermute | solution.py:75
  62.0 4.3 %collective-permute-start.15 = (bf16[256,2432]{1,0:T(8,128)(2,1)S(1)}, bf16[256,2432]{1,0:T(8,128)(2,1)S(1)}, u32[]{:S(2)}, u32[]{:S(2)}) collective-permute-start(bf16[256,2432]{1,0:T(8,128)(2,1)S(1)} %fusion), channel_id=1, source_target_pairs={{0,2},{1,3},{2,0},{3,1},{4,6},{5,7},{6,4},{7,5},{8,10},{9,11},{10,... | collective-permute-start | bytes 3735560 | tf_op jit(solution)/shard_map/ppermute | solution.py:75
  62.9 7.0 %collective-permute-start.18 = (bf16[256,2304]{1,0:T(8,128)(2,1)S(1)}, bf16[256,2304]{1,0:T(8,128)(2,1)S(1)}, u32[]{:S(2)}, u32[]{:S(2)}) collective-permute-start(bf16[256,2304]{1,0:T(8,128)(2,1)S(1)} %multiply_convert_fusion), channel_id=1, source_target_pairs={{0,2},{1,3},{2,0},{3,1},{4,6},{5,7},{6,4},{7,5},{8,10},{9,11},{10,... | collective-permute-start | bytes 3538952 | tf_op jit(solution)/shard_map/ppermute | solution.py:75
  64.3 7.5 %collective-permute-start.17 = (bf16[256,2432]{1,0:T(8,128)(2,1)S(1)}, bf16[256,2432]{1,0:T(8,128)(2,1)S(1)}, u32[]{:S(2)}, u32[]{:S(2)}) collective-permute-start(bf16[256,2432]{1,0:T(8,128)(2,1)S(1)} %fusion.1), channel_id=1, source_target_pairs={{0,2},{1,3},{2,0},{3,1},{4,6},{5,7},{6,4},{7,5},{8,10},{9,11},{10,... | collective-permute-start | bytes 3735560 | tf_op jit(solution)/shard_map/ppermute | solution.py:75
  67.3 14.8 %collective-permute-start.16 = (bf16[2,2,1,2,16,2432]{5,4,3,2,1,0:T(8,128)(2,1)S(1)}, bf16[2,2,1,2,16,2432]{5,4,3,2,1,0:T(8,128)(2,1)S(1)}, u32[]{:S(2)}, u32[]{:S(2)}) collective-permute-start(bf16[2,2,1,2,16,2432]{5,4,3,2,1,0:T(8,128)(2,1)S(1)} %slice.199), channel_id=1, source_target_pairs={{0,4},{1,5},{2,3},{3,2},{4,0},{5,1},{6,7},{7,6},{8,12},{9,13},{10,... | collective-permute-start | bytes 1867784 | tf_op jit(solution)/shard_map/ppermute | solution.py:75
  70.8 20.0 %collective-permute-start.23 = (bf16[2,1,2,2,16,2304]{5,4,3,2,1,0:T(8,128)(2,1)S(1)}, bf16[2,1,2,2,16,2304]{5,4,3,2,1,0:T(8,128)(2,1)S(1)}, u32[]{:S(2)}, u32[]{:S(2)}) collective-permute-start(bf16[2,1,2,2,16,2304]{5,4,3,2,1,0:T(8,128)(2,1)S(1)} %slice.211), channel_id=1, source_target_pairs={{0,8},{1,9},{2,18},{3,19},{4,12},{5,13},{6,22},{7,23},{8,0},{9,1},... | collective-permute-start | bytes 1769480 | tf_op jit(solution)/shard_map/ppermute | solution.py:75
  73.0 10.7 %collective-permute-start.20 = (bf16[2,2,2,1,16,2432]{5,4,3,2,1,0:T(8,128)(2,1)S(1)}, bf16[2,2,2,1,16,2432]{5,4,3,2,1,0:T(8,128)(2,1)S(1)}, u32[]{:S(2)}, u32[]{:S(2)}) collective-permute-start(bf16[2,2,2,1,16,2432]{5,4,3,2,1,0:T(8,128)(2,1)S(1)} %slice.205), channel_id=1, source_target_pairs={{0,1},{1,0},{2,6},{3,7},{4,5},{5,4},{6,2},{7,3},{8,9},{9,8},{10,14... | collective-permute-start | bytes 1867784 | tf_op jit(solution)/shard_map/ppermute | solution.py:75
  82.3 8.4 %collective-permute-start.19 = (bf16[2,2,1,1,16,2432]{5,4,3,2,1,0:T(8,128)(2,1)S(1)}, bf16[2,2,1,1,16,2432]{5,4,3,2,1,0:T(8,128)(2,1)S(1)}, u32[]{:S(2)}, u32[]{:S(2)}) collective-permute-start(bf16[2,2,1,1,16,2432]{5,4,3,2,1,0:T(8,128)(2,1)S(1)} %slice.203), channel_id=1, source_target_pairs={{0,1},{1,0},{2,6},{3,7},{4,5},{5,4},{6,2},{7,3},{8,9},{9,8},{10,14... | collective-permute-start | bytes 933896 | tf_op jit(solution)/shard_map/ppermute | solution.py:75
  84.0 9.8 %collective-permute-start.22 = (bf16[2,2,1,1,16,2432]{5,4,3,2,1,0:T(8,128)(2,1)S(1)}, bf16[2,2,1,1,16,2432]{5,4,3,2,1,0:T(8,128)(2,1)S(1)}, u32[]{:S(2)}, u32[]{:S(2)}) collective-permute-start(bf16[2,2,1,1,16,2432]{5,4,3,2,1,0:T(8,128)(2,1)S(1)} %slice.209), channel_id=1, source_target_pairs={{0,4},{1,5},{2,3},{3,2},{4,0},{5,1},{6,7},{7,6},{8,12},{9,13},{10,... | collective-permute-start | bytes 933896 | tf_op jit(solution)/shard_map/ppermute | solution.py:75
  91.0 11.1 %collective-permute-start.21 = (bf16[1,2,1,1,16,2432]{5,4,3,2,1,0:T(8,128)(2,1)S(1)}, bf16[1,2,1,1,16,2432]{5,4,3,2,1,0:T(8,128)(2,1)S(1)}, u32[]{:S(2)}, u32[]{:S(2)}) collective-permute-start(bf16[1,2,1,1,16,2432]{5,4,3,2,1,0:T(8,128)(2,1)S(1)} %slice.207), channel_id=1, source_target_pairs={{0,16},{1,17},{2,10},{3,11},{4,20},{5,21},{6,14},{7,15},{8,24},{9,... | collective-permute-start | bytes 466952 | tf_op jit(solution)/shard_map/ppermute | solution.py:75
  92.8 10.1 %collective-permute-start.26 = (bf16[2,1,1,2,16,2304]{5,4,3,2,1,0:T(8,128)(2,1)S(1)}, bf16[2,1,1,2,16,2304]{5,4,3,2,1,0:T(8,128)(2,1)S(1)}, u32[]{:S(2)}, u32[]{:S(2)}) collective-permute-start(bf16[2,1,1,2,16,2304]{5,4,3,2,1,0:T(8,128)(2,1)S(1)} %slice.217), channel_id=1, source_target_pairs={{0,4},{1,5},{2,3},{3,2},{4,0},{5,1},{6,7},{7,6},{8,12},{9,13},{10,... | collective-permute-start | bytes 884744 | tf_op jit(solution)/shard_map/ppermute | solution.py:75
  93.8 10.7 %collective-permute-start.25 = (bf16[2,1,1,1,16,2432]{5,4,3,2,1,0:T(8,128)(2,1)S(1)}, bf16[2,1,1,1,16,2432]{5,4,3,2,1,0:T(8,128)(2,1)S(1)}, u32[]{:S(2)}, u32[]{:S(2)}) collective-permute-start(bf16[2,1,1,1,16,2432]{5,4,3,2,1,0:T(8,128)(2,1)S(1)} %slice.215), channel_id=1, source_target_pairs={{0,8},{1,9},{2,18},{3,19},{4,12},{5,13},{6,22},{7,23},{8,0},{9,1},... | collective-permute-start | bytes 466952 | tf_op jit(solution)/shard_map/ppermute | solution.py:75
  102.2 4.7 %collective-permute-start.24 = (bf16[1,1,1,1,16,2432]{5,4,3,2,1,0:T(8,128)(2,1)S(1)}, bf16[1,1,1,1,16,2432]{5,4,3,2,1,0:T(8,128)(2,1)S(1)}, u32[]{:S(2)}, u32[]{:S(2)}) collective-permute-start(bf16[1,1,1,1,16,2432]{5,4,3,2,1,0:T(8,128)(2,1)S(1)} %slice.213), channel_id=1, source_target_pairs={{0,8},{1,9},{2,18},{3,19},{4,12},{5,13},{6,22},{7,23},{8,0},{9,1},... | collective-permute-start | bytes 233480 | tf_op jit(solution)/shard_map/ppermute | solution.py:75
  103.0 6.6 %collective-permute-start.27 = (bf16[2,1,1,1,16,2304]{5,4,3,2,1,0:T(8,128)(2,1)S(1)}, bf16[2,1,1,1,16,2304]{5,4,3,2,1,0:T(8,128)(2,1)S(1)}, u32[]{:S(2)}, u32[]{:S(2)}) collective-permute-start(bf16[2,1,1,1,16,2304]{5,4,3,2,1,0:T(8,128)(2,1)S(1)} %slice.219), channel_id=1, source_target_pairs={{0,1},{1,0},{2,6},{3,7},{4,5},{5,4},{6,2},{7,3},{8,9},{9,8},{10,14... | collective-permute-start | bytes 442376 | tf_op jit(solution)/shard_map/ppermute | solution.py:75
  106.9 5.4 %collective-permute-start.29 = (bf16[1,1,1,1,16,2432]{5,4,3,2,1,0:T(8,128)(2,1)S(1)}, bf16[1,1,1,1,16,2432]{5,4,3,2,1,0:T(8,128)(2,1)S(1)}, u32[]{:S(2)}, u32[]{:S(2)}) collective-permute-start(bf16[1,1,1,1,16,2432]{5,4,3,2,1,0:T(8,128)(2,1)S(1)} %slice.223), channel_id=1, source_target_pairs={{0,16},{1,17},{2,10},{3,11},{4,20},{5,21},{6,14},{7,15},{8,24},{9,... | collective-permute-start | bytes 233480 | tf_op jit(solution)/shard_map/ppermute | solution.py:75
  109.7 5.3 %collective-permute-start.28 = (bf16[1,1,1,1,16,2304]{5,4,3,2,1,0:T(8,128)(2,1)S(1)}, bf16[1,1,1,1,16,2304]{5,4,3,2,1,0:T(8,128)(2,1)S(1)}, u32[]{:S(2)}, u32[]{:S(2)}) collective-permute-start(bf16[1,1,1,1,16,2304]{5,4,3,2,1,0:T(8,128)(2,1)S(1)} %slice.221), channel_id=1, source_target_pairs={{0,16},{1,17},{2,10},{3,11},{4,20},{5,21},{6,14},{7,15},{8,24},{9,... | collective-permute-start | bytes 221192 | tf_op jit(solution)/shard_map/ppermute | solution.py:75
  (3 other events, 6.6 us)
